TPU v7x, 32 devices: a whole 2x2x4 slice. The times are simulated.
32 devices in a mesh: row: 8 (over y, x, core), col: 4 (over z).
Axes of the slice: x: 2, y: 2, z: 4, core: 2. Of those that a mesh axis runs over, the one named last changes fastest.
Arguments:
- op_tiles: float32 [256, 4, 64, 64], P('row', 'col'), may hold values from -18 to 18
- op_rows: int32 [256, 4], P('row', 'col'), may hold values from 0 to 7
- op_cols: int32 [256, 4], P('row', 'col'), may hold values from 0 to 15
- op_count: int32 [8, 4], P('row', 'col'), may hold values from 1 to 32, as said below
- pro_tiles: float32 [64, 4, 64, 64], P('row', 'col'), may hold values from -0.1875 to 0.1875
- pro_cols: int32 [64, 4], P('row', 'col'), may hold values from 0 to 3
- pro_live: int32 [64, 4], P('row', 'col'), may hold values 0 or 1
Outputs:
- product: float32 [64, 16, 64, 64], P('row', 'col')
- coarse: float32 [16, 16, 64, 64], P('row', 'col')
Inputs may be any that keep to these rules, and one draw needn't show every extreme that they name: `op_count`: live slots of each device's list; some device's list is full in every draw.
All inputs are finite; a program needn't handle non-finite values. No bound on the sum of `pro_live` on one device may be relied on, other than what follows from the above.
Results may differ from a plain program's by a relative error of at most 0.0003.
Values sent between devices are 32-bit elements; how exact they have to be, the bound alone decides.
No kernel may reach another device: no remote copies, remote signals or barrier semaphores. Data moves between devices by JAX's collectives and lax.ppermute only.
A program may use at most 128 MiB of HBM per device.

v0:
```python
import jax
import jax.numpy as jnp
from jax import lax
from jax.sharding import PartitionSpec as P

COARSEN = 4


precise = lax.Precision.HIGHEST


def column_panel(masked_pro, pro_cols):
    return (
        lax.all_gather(masked_pro, "row", axis=0, tiled=True),
        lax.all_gather(pro_cols, "row", axis=0, tiled=True),
    )


def shards(op_tiles, op_rows, op_cols, op_count, pro_tiles, pro_cols, pro_live):
    list_len = op_tiles.shape[0]
    tile_size = op_tiles.shape[2]
    fine_rows = pro_tiles.shape[0]
    row_count = lax.axis_size("row")
    col_count = lax.axis_size("col")
    fine_total = fine_rows * row_count
    fine_cols = fine_total // col_count
    coarse_total = fine_total // COARSEN
    coarse_cols = coarse_total // col_count
    col_index = lax.axis_index("col")
    live_op = (jnp.arange(list_len, dtype=jnp.int32) < op_count[0, 0]).astype(jnp.float32)
    masked_op = op_tiles[:, 0] * live_op[:, None, None]
    masked_pro = pro_tiles * pro_live.astype(jnp.float32)[:, :, None, None]
    op_where = jnp.stack([op_rows[:, 0], op_cols[:, 0] + col_index * fine_cols], axis=1)
    panel_tiles, panel_ids = column_panel(masked_pro, pro_cols)
    empty_product = jnp.zeros((fine_rows, coarse_cols, tile_size, tile_size), jnp.float32)
    piece_tiles = lax.all_gather(masked_op, "col", axis=0, tiled=True)
    piece_where = lax.all_gather(op_where, "col", axis=0, tiled=True)
    fine_ids = piece_where[:, 1]
    right_tiles = panel_tiles[fine_ids, 0]
    targets = panel_ids[fine_ids, 0]
    tile_prods = jnp.einsum("nab,nbc->nac", piece_tiles, right_tiles, precision=precise)
    product = empty_product.at[piece_where[:, 0], targets].add(tile_prods)
    coarse_ids = pro_cols + col_index * coarse_cols
    empty_term = jnp.zeros((coarse_total, coarse_cols, tile_size, tile_size), jnp.float32)
    piece_tiles = lax.all_gather(masked_pro, "col", axis=1, tiled=True)
    piece_ids = lax.all_gather(coarse_ids, "col", axis=1, tiled=True)
    tile_prods = jnp.einsum("ksba,kjbc->ksjac", piece_tiles, product, precision=precise)
    partial_sum = empty_term.at[piece_ids.reshape(-1)].add(
        tile_prods.reshape((-1,) + tile_prods.shape[2:])
    )
    coarse = lax.psum_scatter(partial_sum, "row", scatter_dimension=0, tiled=True)
    return (product, coarse)


def solution(mesh):
    return jax.shard_map(
        shards,
        mesh=mesh,
        in_specs=(
            P("row", "col", None, None),
            P("row", "col"),
            P("row", "col"),
            P("row", "col"),
            P("row", "col", None, None),
            P("row", "col"),
            P("row", "col"),
        ),
        out_specs=(P("row", "col", None, None), P("row", "col", None, None)),
        check_vma=False,
    )
```

profile of v0, /device:TPU:0, one launch (start us, length us, event | category | flops | bytes accessed | tf_op | source)
XLA Modules:
  0.0 223.5 jit_solution(290114570325958954)
XLA Ops:
  7.2 0.7 convert_bitcast_fusion
  7.9 1.7 broadcast_multiply_fusion
  10.4 2.3 %bitcast_multiply_fusion = f32[32,64,64]{2,1,0:T(8,128)} fusion(f32[32,1,64,64]{3,2,1,0:T(8,128)} %param.7, f32[32]{0:T(128)S(1)} %compare_convert_fusion), kind=kLoop, calls=%fused_computation.7 | loop fusion | flops 131072 | bytes 1048704 | tf_op jit(solution)/shard_map/mul | solution.py:31
  12.8 0.7 add_bitcast_fusion.1
  13.4 12.5 %all-gather.1 = s32[4,1,8]{2,1,0:T(1,128)S(1)} all-gather(s32[1,1,8]{2,1,0:T(1,128)S(1)} %add_bitcast_fusion.1), channel_id=1, replica_groups=mesh['row'=8,'col'=4] {'col'}, dimensions={0}, use_global_device_ids=true | all-gather | bytes 160 | tf_op jit(solution)/shard_map/all_gather | solution.py:46
  26.0 0.7 broadcast_add_fusion
  26.6 0.7 add_bitcast_fusion
  27.3 7.6 %all-gather = s32[4,32,2]{1,2,0:T(2,128)S(1)} all-gather(s32[1,32,2]{1,2,0:T(2,128)S(1)} %add_bitcast_fusion), channel_id=1, replica_groups=mesh['row'=8,'col'=4] {'col'}, dimensions={0}, use_global_device_ids=true | all-gather | bytes 1280 | tf_op jit(solution)/shard_map/all_gather | solution.py:37
  35.1 1.3 dynamic-slice
  37.0 0.8 bitcast_dynamic-update-slice_fusion
  37.8 8.0 %all-reduce.1 = s32[64]{0:T(128)S(1)} all-reduce(s32[64]{0:T(128)S(1)} %bitcast_dynamic-update-slice_fusion), channel_id=1, replica_groups=mesh['row'=8,'col'=4] {'row'}, use_global_device_ids=true, to_apply=%add.1 | all-reduce | flops 64 | bytes 512
  45.8 1.2 gather_fusion
  47.1 33.5 %all_gather.23 = f32[8,4,64,64]{3,2,1,0:T(8,128)S(1)} all-gather(f32[8,1,64,64]{3,2,1,0:T(8,128)S(1)} %copy-done.2), channel_id=1, replica_groups=mesh['row'=8,'col'=4] {'col'}, dimensions={1}, use_global_device_ids=true | all-gather | bytes 655360 | tf_op jit(solution)/shard_map/all_gather | solution.py:45
  80.6 4.4 %gather_fusion.1 = f32[128,64,64]{2,1,0:T(8,128)} fusion(f32[64,1,64,64]{3,2,1,0:T(8,128)} %all-gather.7.cloned.1.call-done, s32[128]{0:T(128)S(1)} %fusion.5), kind=kCustom, calls=%fused_computation.1 | custom fusion | bytes 4195328 | tf_op jit(solution)/shard_map/gather | solution.py:39
  85.0 50.1 %all-gather.5.cloned.1.call-done = f32[128,64,64]{2,1,0:T(8,128)} async-done(((f32[32,64,64]{2,1,0:T(8,128)}), f32[128,64,64]{2,1,0:T(8,128)}) %all-gather.5.cloned.1.call-update) | async-done | bytes 2097168 | tf_op jit(solution)/shard_map/all_gather | solution.py:36
  135.0 9.8 %fusion.8 = f32[128,64,64]{2,1,0:T(8,128)} fusion(f32[128,64,64]{2,1,0:T(8,128)} %all-gather.5.cloned.1.call-done, f32[128,64,64]{2,1,0:T(8,128)} %gather_fusion.1), kind=kOutput, calls=%fused_computation.28 | convolution fusion | flops 402653184 | bytes 6291456 | tf_op jit(solution)/shard_map/nab,nbc->nac/dot_general | solution.py:41
  144.8 0.1 broadcast_in_dim.4
  145.0 14.6 %scatter_fusion = f32[8,4,64,64]{3,2,1,0:T(8,128)S(1)} fusion(f32[8,4,64,64]{3,2,1,0:T(8,128)S(1)} %broadcast_in_dim.4, s32[128]{0:T(128)S(1)} %fusion.7, f32[128,64,64]{2,1,0:T(8,128)} %fusion.8), kind=kCustom, calls=%fused_computation.2 | custom fusion | flops 524288 | bytes 6292480 | tf_op jit(solution)/shard_map/scatter-add | solution.py:42
  159.6 5.0 %convolution_bitcast_fusion = f32[8,4,4,64,64]{3,4,1,2,0:T(8,128)} fusion(f32[8,4,64,64]{3,2,1,0:T(8,128)S(1)} %scatter_fusion, f32[8,4,64,64]{3,2,1,0:T(8,128)S(1)} %all_gather.23), kind=kOutput, calls=%fused_computation.4 | convolution fusion | flops 402653184 | bytes 3145728 | tf_op jit(solution)/shard_map/ksba,kjbc->ksjac/dot_general | solution.py:47
  164.6 5.4 %copy.18 = f32[8,4,4,64,64]{4,3,2,1,0:T(8,128)} copy(f32[8,4,4,64,64]{3,4,1,2,0:T(8,128)} %convolution_bitcast_fusion) | data formatting | bytes 4194304 | tf_op jit(solution)/shard_map/ksba,kjbc->ksjac/transpose | solution.py:47
  170.0 0.2 broadcast_in_dim.5
  170.2 6.5 %scatter_fusion.1 = f32[16,4,64,64]{3,2,1,0:T(8,128)S(1)} fusion(f32[16,4,64,64]{3,2,1,0:T(8,128)S(1)} %broadcast_in_dim.5, s32[32]{0:T(128)S(1)} %fusion.6, f32[32,4,64,64]{3,2,1,0:T(8,128)} %bitcast.45), kind=kCustom, calls=%fused_computation.3 | custom fusion | flops 524288 | bytes 6291584 | tf_op jit(solution)/shard_map/scatter-add | solution.py:48
  176.7 1.3 copy-done.1
  178.1 39.0 %reduce-scatter.2.cloned.1.call-done = f32[2,4,64,64]{3,2,1,0:T(8,128)} async-done(((f32[16,4,64,64]{3,2,1,0:T(8,128)}), f32[2,4,64,64]{3,2,1,0:T(8,128)}) %reduce-scatter.2.cloned.1.call-update) | async-done | bytes 131088 | tf_op jit(solution)/shard_map/reduce_scatter | solution.py:51
  (21 shorter events, 0.5 us)
Async XLA Ops:
  7.2 73.4 %all-gather.7.cloned.1.call-start = ((), (), s32[]{:S(2)}) async-start(), calls=%async_computation.2 | async-start | bytes 2359296 | tf_op jit(solution)/shard_map/all_gather | solution.py:14
  9.6 37.4 %copy-start.2 = (f32[8,1,64,64]{3,2,1,0:T(8,128)S(1)}, f32[8,1,64,64]{3,2,1,0:T(8,128)}, u32[]{:S(2)}) copy-start(f32[8,1,64,64]{3,2,1,0:T(8,128)} %broadcast_multiply_fusion) | copy-start | bytes 393220
  9.6 125.4 %all-gather.5.cloned.1.call-start = ((), (), s32[]{:S(2)}) async-start(), calls=%async_computation.1 | async-start | bytes 5242880 | tf_op jit(solution)/shard_map/all_gather | solution.py:36
  12.7 204.3 %reduce-scatter.2.cloned.1.call-start = ((), (), s32[]{:S(2)}) async-start(), calls=%async_computation.3 | async-start | bytes 2359296 | tf_op jit(solution)/shard_map/reduce_scatter | solution.py:51
  159.6 10.4 %copy-start = (f32[8,4,64,64]{3,2,1,0:T(8,128)}, f32[8,4,64,64]{3,2,1,0:T(8,128)S(1)}, u32[]{:S(2)}) copy-start(f32[8,4,64,64]{3,2,1,0:T(8,128)S(1)} %scatter_fusion) | copy-start | bytes 1572868
  176.7 1.3 copy-start.1
Sparse Core Ops, SparseCore 0:
  10.5 30.5 all-gather.6
  43.2 91.7 all-gather.4
  178.2 38.7 reduce-scatter.1
where the time goes:
time: 224 us
  waiting for transfers between devices  89.1 us (40%)
  blocking collectives  61.6 us (28%)
  other arithmetic  27.8 us (12%)
  between operations  15.1 us (7%)
  local copies, waits for them, and re-layouts  15 us (7%)
  matrix products  14.8 us (7%)
    all_gather x1, waiting for transfers between devices, shards(): piece_tiles = lax.all_gather(masked_op, 'col', axis=0, tiled=True)  50.1 us
    reduce_scatter x1, waiting for transfers between devices, shards(): lax.psum_scatter(partial_sum, 'row', scatter_dimension=0, tiled=True)  39 us
    all_gather x1, blocking collectives, shards(): piece_tiles = lax.all_gather(masked_pro, 'col', axis=1, tiled=True)  33.5 us
    scatter-add x1, other arithmetic, shards(): product = empty_product.at[piece_where[:, 0], targets].add(tile_prods)  14.6 us
    all_gather x1, blocking collectives, shards(): piece_ids = lax.all_gather(coarse_ids, 'col', axis=1, tiled=True)  12.5 us
    dot_general x1, matrix products, shards(): jnp.einsum('nab,nbc->nac', piece_tiles, right_tiles, precision=precise)  9.83 us
    unnamed x1, blocking collectives  8.02 us
    all_gather x1, blocking collectives, shards(): piece_where = lax.all_gather(op_where, 'col', axis=0, tiled=True)  7.56 us
  transfers between devices with their start and end apart: 3, of which 2 were waited for; matrix products, arithmetic and copies ran while one was open for 5% of the time, Pallas kernels for 0%

commit v1 on v0

v1 whole, which is shorter than its diff:
```python
import functools

import jax
import jax.numpy as jnp
from jax import lax
from jax.experimental import pallas as pl
from jax.experimental.pallas import tpu as pltpu
from jax.sharding import PartitionSpec as P

COARSEN = 4
GROUP = 16
META = 8
VMEM_BYTES = 48 * 2**20

f32, bf16, i32 = jnp.float32, jnp.bfloat16, jnp.int32
VMEM = pl.BlockSpec(memory_space=pltpu.VMEM)
SMEM = pl.BlockSpec(memory_space=pltpu.SMEM)


def call(kernel, out_shape, n_in, scratch=(), flops=0, nbytes=0):
    return pl.pallas_call(
        kernel,
        out_shape=out_shape,
        in_specs=[VMEM] * n_in,
        out_specs=jax.tree.map(lambda _: VMEM, out_shape),
        scratch_shapes=list(scratch),
        compiler_params=pltpu.CompilerParams(vmem_limit_bytes=VMEM_BYTES),
        cost_estimate=pl.CostEstimate(flops=flops, bytes_accessed=nbytes, transcendentals=0),
    )


def shape(*dims, dtype=f32):
    return jax.ShapeDtypeStruct(dims, dtype)


def pack(fine_cols, coarse_cols, op, pro, rows, cols, count, pro_cols, pro_live, z_pay, r_pay):
    list_len, tile = op.shape[0], op.shape[2]
    fine_rows = pro.shape[0]
    half, quarter = GROUP // 2, fine_rows // 2
    col_index = lax.axis_index("col")
    for block in range(list_len // 2):
        low = block // half * GROUP + block % half
        z_pay[block * tile : (block + 1) * tile, :] = jnp.concatenate([op[low, 0], op[low + half, 0]], axis=1)
    base = list_len // 2 * tile
    for k in range(quarter):
        pair = jnp.concatenate([pro[k, 0], pro[k + quarter, 0]], axis=1)
        r_pay[k * tile : (k + 1) * tile, :] = pair
        turned = pair.T
        z_pay[base + k * tile : base + (k + 1) * tile, :] = jnp.concatenate([turned[:tile], turned[tile:]], axis=1)
    meta = base + quarter * tile
    z_pay[meta : meta + META, :] = jnp.zeros((META, 2 * tile), f32)
    r_pay[quarter * tile : quarter * tile + META, :] = jnp.zeros((META, 2 * tile), f32)
    z_pay[meta : meta + 1, 0:list_len] = rows[...].astype(f32)
    z_pay[meta + 1 : meta + 2, 0:list_len] = (cols[...] + col_index * fine_cols).astype(f32)
    z_pay[meta + 2 : meta + 3, 0:1] = count[...].astype(f32)
    z_pay[meta + 2 : meta + 3, 1:2] = jnp.full((1, 1), col_index, i32).astype(f32)
    live = pro_live[...] > 0
    z_pay[meta + 3 : meta + 4, 0:fine_rows] = jnp.where(live, pro_cols[...] + col_index * coarse_cols, -1).astype(f32)
    r_pay[quarter * tile : quarter * tile + 1, 0:fine_rows] = jnp.where(live, pro_cols[...], -1).astype(f32)


def split(x):
    high = x.astype(bf16)
    return high, (x - high.astype(f32)).astype(bf16)


def halves(pair):
    tile = pair.shape[0]
    high = pair.astype(bf16).astype(f32)
    low = pair - high
    left = lax.broadcasted_iota(i32, pair.shape, 1) < tile
    first = jnp.where(left, high, pltpu.roll(low, tile, 1))
    second = jnp.where(left, pltpu.roll(high, tile, 1), low)
    return first.astype(bf16), second.astype(bf16)


def to_smem(refs, at, dst, sems):
    copies = [
        pltpu.make_async_copy(ref.at[pl.ds(row, META)], dst.at[i], sems.at[i])
        for i, (ref, row) in enumerate(zip(refs, at))
    ]
    for copy in copies:
        copy.start()
    for copy in copies:
        copy.wait()


def add_products(z_pay, meta, panel, target_of, fine_total, coarse_cols, acc, tile, list_len):
    count = meta[2, 0].astype(i32)
    half = GROUP // 2
    for group in range(list_len // GROUP):

        @pl.when(count > group * GROUP)
        def _():
            for p in range(half):
                block = group * half + p
                high, low = split(z_pay[block * tile : (block + 1) * tile, :])
                left = jnp.concatenate([high, low], axis=0)
                rights, places = [], []
                for slot in (group * GROUP + p, group * GROUP + p + half):
                    fine = meta[1, slot].astype(i32)
                    target = target_of(fine)
                    live = jnp.logical_and(slot < count, target >= 0)
                    rights.append(panel[jnp.where(live, fine, fine_total)])
                    places.append(jnp.where(live, meta[0, slot].astype(i32) * coarse_cols + target, 0))
                empty = jnp.zeros_like(rights[0])
                right = jnp.concatenate(
                    [jnp.concatenate([rights[0], empty], axis=0), jnp.concatenate([empty, rights[1]], axis=0)], axis=1
                )
                prods = jnp.dot(left, right, preferred_element_type=f32)
                for side, place in enumerate(places):
                    part = prods[:, side * 2 * tile : (side + 1) * 2 * tile]
                    acc[place] += part[:tile] + part[tile:]


def target_reader(panel_meta, fine_rows, row_count):
    row_index = lax.axis_index("row")

    def target_of(fine):
        return panel_meta[(fine // fine_rows) ^ row_index, 0, fine % fine_rows].astype(i32)

    return target_of


def first_products(n_panel, n_pays, sizes, *refs):
    tile, list_len, fine_rows, coarse_cols = sizes
    r_pays, refs = refs[:n_panel], refs[n_panel:]
    z_pays, refs = refs[:n_pays], refs[n_pays:]
    acc, panel, panel_meta, z_meta, sems = refs
    quarter = fine_rows // 2
    fine_total = fine_rows * n_panel
    row_index = lax.axis_index("row")
    z_at = z_pays[0].shape[0] - META
    to_smem(r_pays, [quarter * tile] * n_panel, panel_meta, sems)
    to_smem(z_pays, [z_at] * n_pays, z_meta, sems)
    acc[...] = jnp.zeros_like(acc)
    panel[fine_total] = jnp.zeros((tile, 2 * tile), bf16)
    for m, r_pay in enumerate(r_pays):
        base = (row_index ^ m) * fine_rows
        for k in range(quarter):
            panel[base + k], panel[base + k + quarter] = halves(r_pay[k * tile : (k + 1) * tile, :])
    target_of = target_reader(panel_meta, fine_rows, n_panel)
    for i, z_pay in enumerate(z_pays):
        add_products(z_pay, z_meta.at[i], panel, target_of, fine_total, coarse_cols, acc, tile, list_len)


def last_products(n_panel, n_pays, n_more, sizes, *refs):
    tile, list_len, fine_rows, coarse_cols = sizes
    acc_in, panel, refs = refs[0], refs[1], refs[2:]
    r_metas, refs = refs[:n_panel], refs[n_panel:]
    z_pays, refs = refs[:n_pays], refs[n_pays:]
    product, keep, send = refs[:3]
    acc, weights, strips, panel_meta, z_meta, sems = refs[3:]
    quarter = fine_rows // 2
    fine_total = fine_rows * n_panel
    row_index = lax.axis_index("row")
    z_at = z_pays[0].shape[0] - META
    to_smem(r_metas, [quarter * tile] * n_panel, panel_meta, sems)
    to_smem(z_pays, [z_at] * n_pays, z_meta, sems)
    acc[...] = acc_in[...]
    target_of = target_reader(panel_meta, fine_rows, n_panel)
    base = list_len // 2 * tile
    n_cols = weights.shape[1] // tile
    for i, z_pay in enumerate(z_pays):
        if i >= n_pays - n_more:
            add_products(z_pay, z_meta.at[i], panel, target_of, fine_total, coarse_cols, acc, tile, list_len)

        @pl.when(z_meta[i, 2, 0] > 0)
        def _(i=i, z_pay=z_pay):
            at = pl.multiple_of(z_meta[i, 2, 1].astype(i32) * tile, tile)
            for k in range(quarter):
                pair = halves(z_pay[base + k * tile : base + (k + 1) * tile, :])
                for kk, wide in zip((k, k + quarter), pair):
                    weights[kk, pl.ds(at, tile), :] = wide

    keep[...] = jnp.zeros_like(keep)
    send[...] = jnp.zeros_like(send)
    for k in range(fine_rows):
        sums = []
        for m in range(coarse_cols):
            part = acc[k * coarse_cols + m]
            total = part + pltpu.roll(part, tile, 1)
            product[k, m] = total[:, :tile]
            sums.append(total)
        left = lax.broadcasted_iota(i32, sums[0].shape, 1) < tile
        strip = jnp.concatenate(
            [jnp.where(left, sums[m], sums[m + 1]) for m in range(0, coarse_cols, 2)], axis=1
        )
        high, low = split(strip)
        right = jnp.concatenate([high, high, low, low], axis=0)
        wide = weights[k]
        strips[k] = jnp.dot(jnp.concatenate([wide, wide], axis=1), right, preferred_element_type=f32)
    owned = keep.shape[1]
    n_chips = keep.shape[0]
    for i, z_pay in enumerate(z_pays):

        @pl.when(z_meta[i, 2, 0] > 0)
        def _(i=i):
            at = pl.multiple_of(z_meta[i, 2, 1].astype(i32) * tile, tile)
            for k in range(fine_rows):
                goal = z_meta[i, 3, k].astype(i32)
                owner = (goal // owned) ^ row_index
                where = (owner // 2, goal % owned)
                live = goal >= 0

                @pl.when(jnp.logical_and(live, owner % 2 == 0))
                def _():
                    keep[where] += strips[k, pl.ds(at, tile), :]

                @pl.when(jnp.logical_and(live, owner % 2 == 1))
                def _():
                    send[where] += strips[k, pl.ds(at, tile), :]


def add_pair(keep, received, *outs):
    for m, out in enumerate(outs):
        out[...] = keep[m] + received[m]


def add_all(*refs):
    *parts, out = refs
    total = parts[0][...]
    for part in parts[1:]:
        total = total + part[...]
    tile = out.shape[2]
    for j in range(out.shape[0]):
        for m in range(out.shape[1]):
            out[j, m] = total[j, :, m * tile : (m + 1) * tile]


def swap(x, axis, mask):
    n = lax.axis_size(axis)
    return lax.ppermute(x, axis, [(i, i ^ mask) for i in range(n)])


def line_gather(own):
    n = lax.axis_size("col")

    def hop(x, first, step):
        pairs = []
        for i in range(first, n - 1, 2):
            if i - (step - 1) >= 0:
                pairs.append((i, i + 1))
            if i + step <= n - 1:
                pairs.append((i + 1, i))
        return lax.ppermute(x, "col", pairs) if pairs else None

    steps, even, odd = [], own, own
    for step in range(1, n):
        even, odd = (
            None if odd is None and step > 1 else hop(own if step == 1 else odd, 0, step),
            None if even is None and step > 1 else hop(own if step == 1 else even, 1, step),
        )
        steps.append([x for x in (even, odd) if x is not None])
    return steps


def shards(op_tiles, op_rows, op_cols, op_count, pro_tiles, pro_cols, pro_live):
    list_len, tile = op_tiles.shape[0], op_tiles.shape[2]
    fine_rows = pro_tiles.shape[0]
    row_count, col_count = lax.axis_size("row"), lax.axis_size("col")
    fine_total = fine_rows * row_count
    fine_cols = fine_total // col_count
    coarse_total = fine_total // COARSEN
    coarse_cols = coarse_total // col_count
    owned = coarse_total // row_count
    n_chips = row_count // 2
    sizes = (tile, list_len, fine_rows, coarse_cols)
    z_rows = (list_len // 2 + fine_rows // 2) * tile + META
    r_rows = fine_rows // 2 * tile + META

    z_pay, r_pay = call(
        functools.partial(pack, fine_cols, coarse_cols),
        (shape(z_rows, 2 * tile), shape(r_rows, 2 * tile)),
        7,
        nbytes=4 * 2**20,
    )(
        op_tiles,
        pro_tiles,
        op_rows.reshape(1, -1),
        op_cols.reshape(1, -1),
        op_count,
        pro_cols.reshape(1, -1),
        pro_live.reshape(1, -1),
    )

    steps = line_gather(z_pay)
    chips = [r_pay] + [swap(r_pay, "row", m) for m in range(2, row_count, 2)]
    cores = [swap(x, "row", 1) for x in chips]
    panel_pays = [x for pair in zip(chips, cores) for x in pair]

    first = [z_pay] + steps[0]
    more = [x for step in steps[1:] for x in step]
    n_first, n_more = len(first), len(more)
    acc, panel = call(
        functools.partial(first_products, row_count, n_first, sizes),
        (shape(fine_rows * coarse_cols, tile, 2 * tile), shape(fine_total + 1, tile, 2 * tile, dtype=bf16)),
        row_count + n_first,
        (
            pltpu.SMEM((row_count, META, 2 * tile), f32),
            pltpu.SMEM((n_first, META, 2 * tile), f32),
            pltpu.SemaphoreType.DMA((max(row_count, n_first),)),
        ),
        flops=2**28,
        nbytes=4 * 2**20,
    )(*panel_pays, *first)

    n_pays = n_first + n_more
    product, keep, send = call(
        functools.partial(last_products, row_count, n_pays, n_more, sizes),
        (
            shape(fine_rows, coarse_cols, tile, tile),
            shape(n_chips, owned, tile, coarse_cols * tile),
            shape(n_chips, owned, tile, coarse_cols * tile),
        ),
        2 + row_count + n_pays,
        (
            pltpu.VMEM((fine_rows * coarse_cols, tile, 2 * tile), f32),
            pltpu.VMEM((fine_rows, col_count * tile, 2 * tile), bf16),
            pltpu.VMEM((fine_rows, col_count * tile, coarse_cols * tile), f32),
            pltpu.SMEM((row_count, META, 2 * tile), f32),
            pltpu.SMEM((n_pays, META, 2 * tile), f32),
            pltpu.SemaphoreType.DMA((max(row_count, n_pays),)),
        ),
        flops=2**28,
        nbytes=4 * 2**20,
    )(acc, panel, *panel_pays, *first, *more)

    received = swap(send, "row", 1)
    part = shape(owned, tile, coarse_cols * tile)
    parts = call(add_pair, (part,) * n_chips, 2, nbytes=2**20)(keep, received)
    others = [swap(parts[m], "row", 2 * m) for m in range(1, n_chips)]
    coarse = call(add_all, shape(owned, coarse_cols, tile, tile), n_chips, nbytes=2**20)(parts[0], *others)
    return (product, coarse)


def solution(mesh):
    return jax.shard_map(
        shards,
        mesh=mesh,
        in_specs=(
            P("row", "col", None, None),
            P("row", "col"),
            P("row", "col"),
            P("row", "col"),
            P("row", "col", None, None),
            P("row", "col"),
            P("row", "col"),
        ),
        out_specs=(P("row", "col", None, None), P("row", "col", None, None)),
        check_vma=False,
    )
```

time: 224 us -> 79.7 us (0.36)
  blocking collectives: 61.6 us -> 0 us
  waiting for transfers between devices: 89.1 us -> 44 us
  other arithmetic: 27.8 us -> 0 us
  matrix products: 14.8 us -> 0 us
  starting transfers between devices: 0.12 us -> 14.8 us
  between operations: 15.1 us -> 1.39 us
  Pallas kernels: 0 us -> 12.7 us
  local copies, waits for them, and re-layouts: 15 us -> 6.75 us
    all_gather x3 -> x0, blocking collectives: 53.6 us -> none  [the longest x1 33.5 us: shards(): piece_tiles = lax.all_gather(masked_pro, 'col', axis=1, tiled=True)]
    all_gather x2 -> x0, waiting for transfers between devices: 50.1 us -> none  [the longest x1 50.1 us: shards(): piece_tiles = lax.all_gather(masked_op, 'col', axis=0, tiled=True)]
    ppermute x0 -> x16, waiting for transfers between devices: none -> 44 us  [the longest x5 29.4 us: hop(): return lax.ppermute(x, 'col', pairs) if pairs else None]
    reduce_scatter x1 -> x0, waiting for transfers between devices: 39 us -> none  [shards(): lax.psum_scatter(partial_sum, 'row', scatter_dimension=0, tiled=True)]
    scatter-add x2 -> x0, other arithmetic: 21.1 us -> none  [the longest x1 14.6 us: shards(): product = empty_product.at[piece_where[:, 0], targets].add(tile_prods)]
    dot_general x2 -> x0, matrix products: 14.8 us -> none  [the longest x1 9.83 us: shards(): jnp.einsum('nab,nbc->nac', piece_tiles, right_tiles, precision=precise)]
    ppermute x0 -> x16, starting transfers between devices: none -> 14.8 us  [the longest x11 7.76 us: swap(): return lax.ppermute(x, axis, [(i, i ^ mask) for i in range(n)])]
    pallas_call x0 -> x5, Pallas kernels: none -> 12.7 us  [the longest x1 8.08 us: shards(): call(functools.partial(last_products, row_count, n_pays, n_more, sizes),...]
  transfers between devices with their start and end apart: 3 -> 16, of which waited for: 2 -> 12; matrix products, arithmetic and copies ran while one was open for 5% -> 0% of each run, Pallas kernels for 0% -> 4%
where the time goes in v1:
time: 79.7 us; the launch traced here: 79.6 us
  waiting for transfers between devices  44 us (55%)
  starting transfers between devices  14.8 us (19%)
  Pallas kernels  12.7 us (16%)
  local copies, waits for them, and re-layouts  6.75 us (8%)
  between operations  1.39 us (2%)
    ppermute x5, waiting for transfers between devices, hop(): return lax.ppermute(x, 'col', pairs) if pairs else None  29.4 us
    ppermute x11, waiting for transfers between devices, swap(): return lax.ppermute(x, axis, [(i, i ^ mask) for i in range(n)])  14.5 us
    pallas_call x1, Pallas kernels, shards(): call(functools.partial(last_products, row_count, n_pays, n_more, sizes),...  8.08 us
    ppermute x11, starting transfers between devices, swap(): return lax.ppermute(x, axis, [(i, i ^ mask) for i in range(n)])  7.76 us
    ppermute x5, starting transfers between devices, hop(): return lax.ppermute(x, 'col', pairs) if pairs else None  7.06 us
    unnamed x16, local copies, waits for them, and re-layouts  6.75 us
    pallas_call x1, Pallas kernels, shards(): call(functools.partial(first_products, row_count, n_first, sizes), (shape...  3.19 us
  transfers between devices with their start and end apart: 16, of which 12 were waited for; matrix products, arithmetic and copies ran while one was open for 0% of the time, Pallas kernels for 4%

profile of v1, /device:TPU:0, one launch (start us, length us, event | category | flops | bytes accessed | tf_op | source)
XLA Modules:
  0.0 79.6 jit_solution(7083208266714363131)
XLA Ops:
  1.3 1.2 %copy-done.1 = f32[32,1,64,64]{3,2,1,0:T(8,128)S(1)} copy-done((f32[32,1,64,64]{3,2,1,0:T(8,128)S(1)}, f32[32,1,64,64]{3,2,1,0:T(8,128)}, u32[]{:S(2)}) %copy-start.1) | copy-done | bytes 524312
  2.5 0.9 %copy-done.3 = f32[8,1,64,64]{3,2,1,0:T(8,128)S(1)} copy-done((f32[8,1,64,64]{3,2,1,0:T(8,128)S(1)}, f32[8,1,64,64]{3,2,1,0:T(8,128)}, u32[]{:S(2)}) %copy-start.3) | copy-done | bytes 131096
  6.7 3.1 %collective-permute-start.7 = (f32[1288,128]{1,0:T(8,128)S(1)}, f32[1288,128]{1,0:T(8,128)S(1)}, u32[]{:S(2)}, u32[]{:S(2)}) collective-permute-start(f32[1288,128]{1,0:T(8,128)S(1)} %get-tuple-element.14.refs_8_.refs_10_), channel_id=1, source_target_pairs={{0,1},{1,0},{2,3},{3,2},{4,5},{5,4},{6,7},{7,6},{8,9},{9,8},{10,11... | collective-permute-start | bytes 1978376 | tf_op jit(solution)/shard_map/ppermute | solution.py:246
  10.4 14.1 %collective-permute-done.7.refs_9_.refs_11_ = f32[1288,128]{1,0:T(8,128)S(1)} collective-permute-done((f32[1288,128]{1,0:T(8,128)S(1)}, f32[1288,128]{1,0:T(8,128)S(1)}, u32[]{:S(2)}, u32[]{:S(2)}) %collective-permute-start.7) | collective-permute-done | bytes 659488 | tf_op jit(solution)/shard_map/ppermute | solution.py:246
  24.6 0.7 collective-permute-start.10
  25.3 1.3 %collective-permute-start.9 = (f32[1288,128]{1,0:T(8,128)S(1)}, f32[1288,128]{1,0:T(8,128)S(1)}, u32[]{:S(2)}, u32[]{:S(2)}) collective-permute-start(f32[1288,128]{1,0:T(8,128)S(1)} %collective-permute-done.8.refs_10_.refs_12_), channel_id=1, source_target_pairs={{1,0},{2,3},{5,4},{6,7},{9,8},{10,11},{13,12},{14,15},{17,16},{18,... | collective-permute-start | bytes 1978376 | tf_op jit(solution)/shard_map/ppermute | solution.py:246
  26.6 1.3 %collective-permute-start.11 = (f32[1288,128]{1,0:T(8,128)S(1)}, f32[1288,128]{1,0:T(8,128)S(1)}, u32[]{:S(2)}, u32[]{:S(2)}) collective-permute-start(f32[1288,128]{1,0:T(8,128)S(1)} %collective-permute-done.10.refs_14_), channel_id=1, source_target_pairs={{1,0},{2,3},{5,4},{6,7},{9,8},{10,11},{13,12},{14,15},{17,16},{18,... | collective-permute-start | bytes 1978376 | tf_op jit(solution)/shard_map/ppermute | solution.py:246
  27.9 2.7 %collective-permute-start.5 = (f32[264,128]{1,0:T(8,128)S(1)}, f32[264,128]{1,0:T(8,128)S(1)}, u32[]{:S(2)}, u32[]{:S(2)}) collective-permute-start(f32[264,128]{1,0:T(8,128)S(1)} %get-tuple-element.13.refs_0_.refs_2_), channel_id=1, source_target_pairs={{0,24},{4,28},{8,16},{12,20},{16,8},{20,12},{24,0},{28,4},{1,25},{... | collective-permute-start | bytes 405512 | tf_op jit(solution)/shard_map/ppermute | solution.py:233
  31.4 3.3 %collective-permute-done.5.refs_6_.refs_8_ = f32[264,128]{1,0:T(8,128)S(1)} collective-permute-done((f32[264,128]{1,0:T(8,128)S(1)}, f32[264,128]{1,0:T(8,128)S(1)}, u32[]{:S(2)}, u32[]{:S(2)}) %collective-permute-start.5) | collective-permute-done | bytes 135200 | tf_op jit(solution)/shard_map/ppermute | solution.py:233
  34.8 1.8 %collective-permute-done.3.refs_4_.refs_6_ = f32[264,128]{1,0:T(8,128)S(1)} collective-permute-done((f32[264,128]{1,0:T(8,128)S(1)}, f32[264,128]{1,0:T(8,128)S(1)}, u32[]{:S(2)}, u32[]{:S(2)}) %collective-permute-start.3) | collective-permute-done | bytes 135200 | tf_op jit(solution)/shard_map/ppermute | solution.py:233
  37.1 0.8 collective-permute-done.6.refs_7_.refs_9_
  38.4 3.2 %shard_map.87 = (f32[32,64,128]{2,1,0:T(8,128)S(1)}, bf16[65,64,128]{2,1,0:T(8,128)(2,1)S(1)}) custom-call(f32[264,128]{1,0:T(8,128)S(1)} %get-tuple-element.13.refs_0_.refs_2_, f32[264,128]{1,0:T(8,128)S(1)} %collective-permute-done.refs_1_.refs_3_, f32[264,128]{1,0:T(8,128)S(1)} %collective-permute-done.1.refs_2_.refs_4_, ...), custom_call_target="tpu_custom_call" | custom-call | flops 268435456 | bytes 4194304 | tf_op jit(solution)/shard_map/pallas_call | solution.py:295
  41.6 1.0 %copy-done = bf16[65,64,128]{2,1,0:T(8,128)(2,1)} copy-done((bf16[65,64,128]{2,1,0:T(8,128)(2,1)}, bf16[65,64,128]{2,1,0:T(8,128)(2,1)S(1)}, u32[]{:S(2)}) %copy-start) | copy-done | bytes 1064984
  42.6 1.0 %copy-done.2 = f32[32,64,128]{2,1,0:T(8,128)} copy-done((f32[32,64,128]{2,1,0:T(8,128)}, f32[32,64,128]{2,1,0:T(8,128)S(1)}, u32[]{:S(2)}) %copy-start.2) | copy-done | bytes 1048600
  43.6 1.8 %collective-permute-done.9.refs_13_ = f32[1288,128]{1,0:T(8,128)S(1)} collective-permute-done((f32[1288,128]{1,0:T(8,128)S(1)}, f32[1288,128]{1,0:T(8,128)S(1)}, u32[]{:S(2)}, u32[]{:S(2)}) %collective-permute-start.9) | collective-permute-done | bytes 659488 | tf_op jit(solution)/shard_map/ppermute | solution.py:246
  45.4 13.5 %collective-permute-done.11.refs_15_ = f32[1288,128]{1,0:T(8,128)S(1)} collective-permute-done((f32[1288,128]{1,0:T(8,128)S(1)}, f32[1288,128]{1,0:T(8,128)S(1)}, u32[]{:S(2)}, u32[]{:S(2)}) %collective-permute-start.11) | collective-permute-done | bytes 659488 | tf_op jit(solution)/shard_map/ppermute | solution.py:246
  58.9 8.1 %shard_map.88 = (f32[8,4,64,64]{3,2,1,0:T(8,128)}, f32[4,2,64,256]{3,2,1,0:T(8,128)S(1)}, f32[4,2,64,256]{3,2,1,0:T(8,128)S(1)}) custom-call(f32[32,64,128]{2,1,0:T(8,128)} %copy-done.2, bf16[65,64,128]{2,1,0:T(8,128)(2,1)} %copy-done, f32[264,128]{1,0:T(8,128)S(1)} %get-tuple-element.13.refs_0_.refs_2_, ...), custom_call_target="tpu_custom_call" | custom-call | flops 268435456 | bytes 4194304 | tf_op jit(solution)/shard_map/pallas_call | solution.py:309
  67.0 1.9 %collective-permute-done.12.received = f32[4,2,64,256]{3,2,1,0:T(8,128)S(1)} collective-permute-done((f32[4,2,64,256]{3,2,1,0:T(8,128)S(1)}, f32[4,2,64,256]{3,2,1,0:T(8,128)S(1)}, u32[]{:S(2)}, u32[]{:S(2)}) %collective-permute-start.12) | collective-permute-done | bytes 524320 | tf_op jit(solution)/shard_map/ppermute | solution.py:233
  69.0 1.1 %collective-permute-start.13 = (f32[2,64,256]{2,1,0:T(8,128)S(1)}, f32[2,64,256]{2,1,0:T(8,128)S(1)}, u32[]{:S(2)}, u32[]{:S(2)}) collective-permute-start(f32[2,64,256]{2,1,0:T(8,128)S(1)} %get-tuple-element.21), channel_id=1, source_target_pairs={{0,8},{4,12},{8,0},{12,4},{16,24},{20,28},{24,16},{28,20},{1,9},{5... | collective-permute-start | bytes 393224 | tf_op jit(solution)/shard_map/ppermute | solution.py:233
  70.1 2.4 %collective-permute-start.14 = (f32[2,64,256]{2,1,0:T(8,128)S(1)}, f32[2,64,256]{2,1,0:T(8,128)S(1)}, u32[]{:S(2)}, u32[]{:S(2)}) collective-permute-start(f32[2,64,256]{2,1,0:T(8,128)S(1)} %get-tuple-element.22), channel_id=1, source_target_pairs={{0,16},{4,20},{8,24},{12,28},{16,0},{20,4},{24,8},{28,12},{1,17},{... | collective-permute-start | bytes 393224 | tf_op jit(solution)/shard_map/ppermute | solution.py:233
  72.6 2.2 %collective-permute-done.13.refs_1_ = f32[2,64,256]{2,1,0:T(8,128)S(1)} collective-permute-done((f32[2,64,256]{2,1,0:T(8,128)S(1)}, f32[2,64,256]{2,1,0:T(8,128)S(1)}, u32[]{:S(2)}, u32[]{:S(2)}) %collective-permute-start.13) | collective-permute-done | bytes 131104 | tf_op jit(solution)/shard_map/ppermute | solution.py:233
  74.7 3.4 %collective-permute-done.14.refs_2_ = f32[2,64,256]{2,1,0:T(8,128)S(1)} collective-permute-done((f32[2,64,256]{2,1,0:T(8,128)S(1)}, f32[2,64,256]{2,1,0:T(8,128)S(1)}, u32[]{:S(2)}, u32[]{:S(2)}) %collective-permute-start.14) | collective-permute-done | bytes 131104 | tf_op jit(solution)/shard_map/ppermute | solution.py:233
  78.1 0.7 collective-permute-done.15.refs_3_
  78.8 0.8 %shard_map.90 = f32[2,4,64,64]{3,2,1,0:T(8,128)} custom-call(f32[2,64,256]{2,1,0:T(8,128)S(1)} %get-tuple-element.20.refs_0_, f32[2,64,256]{2,1,0:T(8,128)S(1)} %collective-permute-done.13.refs_1_, f32[2,64,256]{2,1,0:T(8,128)S(1)} %collective-permute-done.14.refs_2_, f32[2,64,256]{2,1,0:T(8,128)S(1)} %collective-permute-done.15.refs_3_), custom_call_target="tpu_custom_call" | custom-call | bytes 1048576 | tf_op jit(solution)/shard_map/pallas_call | solution.py:333
  (29 shorter events, 6.1 us)
Async XLA Ops:
  1.3 1.2 %copy-start.1 = (f32[32,1,64,64]{3,2,1,0:T(8,128)S(1)}, f32[32,1,64,64]{3,2,1,0:T(8,128)}, u32[]{:S(2)}) copy-start(f32[32,1,64,64]{3,2,1,0:T(8,128)} %op.1) | copy-start | bytes 1572868
  2.5 0.9 %copy-start.3 = (f32[8,1,64,64]{3,2,1,0:T(8,128)S(1)}, f32[8,1,64,64]{3,2,1,0:T(8,128)}, u32[]{:S(2)}) copy-start(f32[8,1,64,64]{3,2,1,0:T(8,128)} %pro.1) | copy-start | bytes 393220
  3.5 0.7 copy-start.4
  4.1 0.7 copy-start.5
  4.8 0.7 copy-start.6
  5.4 0.7 copy-start.7
  6.7 17.9 %collective-permute-start.7 = (f32[1288,128]{1,0:T(8,128)S(1)}, f32[1288,128]{1,0:T(8,128)S(1)}, u32[]{:S(2)}, u32[]{:S(2)}) collective-permute-start(f32[1288,128]{1,0:T(8,128)S(1)} %get-tuple-element.14.refs_8_.refs_10_), channel_id=1, source_target_pairs={{0,1},{1,0},{2,3},{3,2},{4,5},{5,4},{6,7},{7,6},{8,9},{9,8},{10,11... | collective-permute-start | bytes 1978376 | tf_op jit(solution)/shard_map/ppermute | solution.py:246
  9.7 15.5 %collective-permute-start.8 = (f32[1288,128]{1,0:T(8,128)S(1)}, f32[1288,128]{1,0:T(8,128)S(1)}, u32[]{:S(2)}, u32[]{:S(2)}) collective-permute-start(f32[1288,128]{1,0:T(8,128)S(1)} %get-tuple-element.14.refs_8_.refs_10_), channel_id=1, source_target_pairs={{1,2},{2,1},{5,6},{6,5},{9,10},{10,9},{13,14},{14,13},{17,18},{18,... | collective-permute-start | bytes 1978376 | tf_op jit(solution)/shard_map/ppermute | solution.py:246
  24.6 2.0 %collective-permute-start.10 = (f32[1288,128]{1,0:T(8,128)S(1)}, f32[1288,128]{1,0:T(8,128)S(1)}, u32[]{:S(2)}, u32[]{:S(2)}) collective-permute-start(f32[1288,128]{1,0:T(8,128)S(1)} %collective-permute-done.7.refs_9_.refs_11_), channel_id=1, source_target_pairs={{1,2},{2,1},{5,6},{6,5},{9,10},{10,9},{13,14},{14,13},{17,18},{18,... | collective-permute-start | bytes 1978376 | tf_op jit(solution)/shard_map/ppermute | solution.py:246
  25.3 20.1 %collective-permute-start.9 = (f32[1288,128]{1,0:T(8,128)S(1)}, f32[1288,128]{1,0:T(8,128)S(1)}, u32[]{:S(2)}, u32[]{:S(2)}) collective-permute-start(f32[1288,128]{1,0:T(8,128)S(1)} %collective-permute-done.8.refs_10_.refs_12_), channel_id=1, source_target_pairs={{1,0},{2,3},{5,4},{6,7},{9,8},{10,11},{13,12},{14,15},{17,16},{18,... | collective-permute-start | bytes 1978376 | tf_op jit(solution)/shard_map/ppermute | solution.py:246
  26.6 32.3 %collective-permute-start.11 = (f32[1288,128]{1,0:T(8,128)S(1)}, f32[1288,128]{1,0:T(8,128)S(1)}, u32[]{:S(2)}, u32[]{:S(2)}) collective-permute-start(f32[1288,128]{1,0:T(8,128)S(1)} %collective-permute-done.10.refs_14_), channel_id=1, source_target_pairs={{1,0},{2,3},{5,4},{6,7},{9,8},{10,11},{13,12},{14,15},{17,16},{18,... | collective-permute-start | bytes 1978376 | tf_op jit(solution)/shard_map/ppermute | solution.py:246
  27.9 6.9 %collective-permute-start.5 = (f32[264,128]{1,0:T(8,128)S(1)}, f32[264,128]{1,0:T(8,128)S(1)}, u32[]{:S(2)}, u32[]{:S(2)}) collective-permute-start(f32[264,128]{1,0:T(8,128)S(1)} %get-tuple-element.13.refs_0_.refs_2_), channel_id=1, source_target_pairs={{0,24},{4,28},{8,16},{12,20},{16,8},{20,12},{24,0},{28,4},{1,25},{... | collective-permute-start | bytes 405512 | tf_op jit(solution)/shard_map/ppermute | solution.py:233
  30.6 6.0 %collective-permute-start.3 = (f32[264,128]{1,0:T(8,128)S(1)}, f32[264,128]{1,0:T(8,128)S(1)}, u32[]{:S(2)}, u32[]{:S(2)}) collective-permute-start(f32[264,128]{1,0:T(8,128)S(1)} %get-tuple-element.13.refs_0_.refs_2_), channel_id=1, source_target_pairs={{0,16},{4,20},{8,24},{12,28},{16,0},{20,4},{24,8},{28,12},{1,17},{... | collective-permute-start | bytes 405512 | tf_op jit(solution)/shard_map/ppermute | solution.py:233
  31.1 5.5 %collective-permute-start.1 = (f32[264,128]{1,0:T(8,128)S(1)}, f32[264,128]{1,0:T(8,128)S(1)}, u32[]{:S(2)}, u32[]{:S(2)}) collective-permute-start(f32[264,128]{1,0:T(8,128)S(1)} %get-tuple-element.13.refs_0_.refs_2_), channel_id=1, source_target_pairs={{0,8},{4,12},{8,0},{12,4},{16,24},{20,28},{24,16},{28,20},{1,9},{5... | collective-permute-start | bytes 405512 | tf_op jit(solution)/shard_map/ppermute | solution.py:233
  34.8 2.3 %collective-permute-start = (f32[264,128]{1,0:T(8,128)S(1)}, f32[264,128]{1,0:T(8,128)S(1)}, u32[]{:S(2)}, u32[]{:S(2)}) collective-permute-start(f32[264,128]{1,0:T(8,128)S(1)} %get-tuple-element.13.refs_0_.refs_2_), channel_id=1, source_target_pairs={{0,4},{4,0},{8,12},{12,8},{16,20},{20,16},{24,28},{28,24},{1,5},{5... | collective-permute-start | bytes 405512 | tf_op jit(solution)/shard_map/ppermute | solution.py:233
  36.5 1.4 %collective-permute-start.6 = (f32[264,128]{1,0:T(8,128)S(1)}, f32[264,128]{1,0:T(8,128)S(1)}, u32[]{:S(2)}, u32[]{:S(2)}) collective-permute-start(f32[264,128]{1,0:T(8,128)S(1)} %collective-permute-done.5.refs_6_.refs_8_), channel_id=1, source_target_pairs={{0,4},{4,0},{8,12},{12,8},{16,20},{20,16},{24,28},{28,24},{1,5},{5... | collective-permute-start | bytes 405512 | tf_op jit(solution)/shard_map/ppermute | solution.py:233
  36.5 1.5 %collective-permute-start.4 = (f32[264,128]{1,0:T(8,128)S(1)}, f32[264,128]{1,0:T(8,128)S(1)}, u32[]{:S(2)}, u32[]{:S(2)}) collective-permute-start(f32[264,128]{1,0:T(8,128)S(1)} %collective-permute-done.3.refs_4_.refs_6_), channel_id=1, source_target_pairs={{0,4},{4,0},{8,12},{12,8},{16,20},{20,16},{24,28},{28,24},{1,5},{5... | collective-permute-start | bytes 405512 | tf_op jit(solution)/shard_map/ppermute | solution.py:233
  37.0 1.4 %collective-permute-start.2 = (f32[264,128]{1,0:T(8,128)S(1)}, f32[264,128]{1,0:T(8,128)S(1)}, u32[]{:S(2)}, u32[]{:S(2)}) collective-permute-start(f32[264,128]{1,0:T(8,128)S(1)} %collective-permute-done.1.refs_2_.refs_4_), channel_id=1, source_target_pairs={{0,4},{4,0},{8,12},{12,8},{16,20},{20,16},{24,28},{28,24},{1,5},{5... | collective-permute-start | bytes 405512 | tf_op jit(solution)/shard_map/ppermute | solution.py:233
  41.6 1.0 %copy-start = (bf16[65,64,128]{2,1,0:T(8,128)(2,1)}, bf16[65,64,128]{2,1,0:T(8,128)(2,1)S(1)}, u32[]{:S(2)}) copy-start(bf16[65,64,128]{2,1,0:T(8,128)(2,1)S(1)} %get-tuple-element.16.refs_1_) | copy-start | bytes 3194884
  42.6 1.0 %copy-start.2 = (f32[32,64,128]{2,1,0:T(8,128)}, f32[32,64,128]{2,1,0:T(8,128)S(1)}, u32[]{:S(2)}) copy-start(f32[32,64,128]{2,1,0:T(8,128)S(1)} %get-tuple-element.15.refs_0_) | copy-start | bytes 3145732
  67.0 2.0 %collective-permute-start.12 = (f32[4,2,64,256]{3,2,1,0:T(8,128)S(1)}, f32[4,2,64,256]{3,2,1,0:T(8,128)S(1)}, u32[]{:S(2)}, u32[]{:S(2)}) collective-permute-start(f32[4,2,64,256]{3,2,1,0:T(8,128)S(1)} %get-tuple-element.19), channel_id=1, source_target_pairs={{0,4},{4,0},{8,12},{12,8},{16,20},{20,16},{24,28},{28,24},{1,5},{5... | collective-permute-start | bytes 1572872 | tf_op jit(solution)/shard_map/ppermute | solution.py:233
  69.0 5.7 %collective-permute-start.13 = (f32[2,64,256]{2,1,0:T(8,128)S(1)}, f32[2,64,256]{2,1,0:T(8,128)S(1)}, u32[]{:S(2)}, u32[]{:S(2)}) collective-permute-start(f32[2,64,256]{2,1,0:T(8,128)S(1)} %get-tuple-element.21), channel_id=1, source_target_pairs={{0,8},{4,12},{8,0},{12,4},{16,24},{20,28},{24,16},{28,20},{1,9},{5... | collective-permute-start | bytes 393224 | tf_op jit(solution)/shard_map/ppermute | solution.py:233
  70.1 7.9 %collective-permute-start.14 = (f32[2,64,256]{2,1,0:T(8,128)S(1)}, f32[2,64,256]{2,1,0:T(8,128)S(1)}, u32[]{:S(2)}, u32[]{:S(2)}) collective-permute-start(f32[2,64,256]{2,1,0:T(8,128)S(1)} %get-tuple-element.22), channel_id=1, source_target_pairs={{0,16},{4,20},{8,24},{12,28},{16,0},{20,4},{24,8},{28,12},{1,17},{... | collective-permute-start | bytes 393224 | tf_op jit(solution)/shard_map/ppermute | solution.py:233
  72.5 6.3 %collective-permute-start.15 = (f32[2,64,256]{2,1,0:T(8,128)S(1)}, f32[2,64,256]{2,1,0:T(8,128)S(1)}, u32[]{:S(2)}, u32[]{:S(2)}) collective-permute-start(f32[2,64,256]{2,1,0:T(8,128)S(1)} %get-tuple-element.23), channel_id=1, source_target_pairs={{0,24},{4,28},{8,16},{12,20},{16,8},{20,12},{24,0},{28,4},{1,25},{... | collective-permute-start | bytes 393224 | tf_op jit(solution)/shard_map/ppermute | solution.py:233

commit v2 on v1

v2 whole, which is shorter than its diff:
```python
import functools

import jax
import jax.numpy as jnp
from jax import lax
from jax.experimental import pallas as pl
from jax.experimental.pallas import tpu as pltpu
from jax.sharding import PartitionSpec as P

COARSEN = 4
GROUP = 16
META = 8
VMEM_BYTES = 48 * 2**20
FULL_BYTES = 63 * 2**20

f32, bf16, i32 = jnp.float32, jnp.bfloat16, jnp.int32
VMEM = pl.BlockSpec(memory_space=pltpu.VMEM)
HBM = pl.BlockSpec(memory_space=pltpu.HBM)


def call(kernel, out_shape, n_in, scratch=(), flops=0, nbytes=0, space=VMEM, limit=VMEM_BYTES):
    return pl.pallas_call(
        kernel,
        out_shape=out_shape,
        in_specs=[space] * n_in,
        out_specs=jax.tree.map(lambda _: VMEM, out_shape),
        scratch_shapes=list(scratch),
        compiler_params=pltpu.CompilerParams(vmem_limit_bytes=limit),
        cost_estimate=pl.CostEstimate(flops=flops, bytes_accessed=nbytes, transcendentals=0),
    )


def shape(*dims, dtype=f32):
    return jax.ShapeDtypeStruct(dims, dtype)


def divide(x, n):
    if n & (n - 1):
        return x // n, x % n
    return lax.shift_right_logical(x, n.bit_length() - 1), x & (n - 1)


def pack(fine_cols, coarse_cols, op, pro, rows, cols, count, pro_cols, pro_live, z_pay, r_pay, *scratch):
    sems = scratch[-1]
    sources = (pro, rows, cols, count, pro_cols, pro_live, op.at[pl.ds(0, GROUP)], op.at[pl.ds(GROUP, op.shape[0] - GROUP)])
    copies = [pltpu.make_async_copy(src, dst, sems.at[i]) for i, (src, dst) in enumerate(zip(sources, scratch))]
    for copy in copies:
        copy.start()
    for copy in copies[:-2]:
        copy.wait()
    pro, rows, cols, count, pro_cols, pro_live, low_tiles, high_tiles = scratch[:-1]
    list_len, tile = op.shape[0], op.shape[2]
    fine_rows = pro.shape[0]
    half, quarter = GROUP // 2, fine_rows // 2
    col_index = lax.axis_index("col")
    base = half * tile
    for k in range(quarter):
        pair = jnp.concatenate([pro[k, 0], pro[k + quarter, 0]], axis=1)
        r_pay[k * tile : (k + 1) * tile, :] = pair
        turned = pair.T
        z_pay[base + k * tile : base + (k + 1) * tile, :] = jnp.concatenate([turned[:tile], turned[tile:]], axis=1)
    meta = base + quarter * tile
    high_at = meta + META
    z_pay[meta : meta + META, :] = jnp.zeros((META, 2 * tile), f32)
    r_pay[quarter * tile : quarter * tile + META, :] = jnp.zeros((META, 2 * tile), f32)
    z_pay[meta : meta + 1, 0:list_len] = rows[...].astype(f32)
    z_pay[meta + 1 : meta + 2, 0:list_len] = (cols[...] + col_index * fine_cols).astype(f32)
    z_pay[meta + 2 : meta + 3, 0:1] = count[...].astype(f32)
    z_pay[meta + 2 : meta + 3, 1:2] = jnp.full((1, 1), col_index, i32).astype(f32)
    live = pro_live[...] > 0
    z_pay[meta + 3 : meta + 4, 0:fine_rows] = jnp.where(live, pro_cols[...] + col_index * coarse_cols, -1).astype(f32)
    r_pay[quarter * tile : quarter * tile + 1, 0:fine_rows] = jnp.where(live, pro_cols[...], -1).astype(f32)
    copies[-2].wait()
    for block in range(half):
        z_pay[block * tile : (block + 1) * tile, :] = jnp.concatenate([low_tiles[block, 0], low_tiles[block + half, 0]], axis=1)
    copies[-1].wait()
    for block in range((list_len - GROUP) // 2):
        slot = block // half * GROUP + block % half
        z_pay[high_at + block * tile : high_at + (block + 1) * tile, :] = jnp.concatenate([high_tiles[slot, 0], high_tiles[slot + half, 0]], axis=1)


def split(x):
    high = x.astype(bf16)
    return high, (x - high.astype(f32)).astype(bf16)


def halves(pair):
    tile = pair.shape[0]
    high = pair.astype(bf16).astype(f32)
    low = pair - high
    left = lax.broadcasted_iota(i32, pair.shape, 1) < tile
    first = jnp.where(left, high, pltpu.roll(low, tile, 1))
    second = jnp.where(left, pltpu.roll(high, tile, 1), low)
    return first.astype(bf16), second.astype(bf16)


def add_products(blocks, high_at, groups, meta, ids, panel, sizes, acc):
    tile, list_len, fine_rows, coarse_cols, fine_total, owned = sizes
    count = meta[2, 0].astype(i32)
    half = GROUP // 2
    row_index = lax.axis_index("row")
    for group in groups:

        @pl.when(count > group * GROUP)
        def _(group=group):
            for p in range(half):
                at = p * tile + (high_at + (group - 1) * half * tile if group else 0)
                high, low = split(blocks[at : at + tile, :])
                left = jnp.concatenate([high, low], axis=0)
                rights, places = [], []
                for slot in (group * GROUP + p, group * GROUP + p + half):
                    fine = meta[1, slot].astype(i32)
                    shard, within = divide(fine, fine_rows)
                    target = ids[shard ^ row_index, 0, within].astype(i32)
                    live = jnp.logical_and(slot < count, target >= 0)
                    rights.append(panel[jnp.where(live, fine, fine_total)])
                    places.append(jnp.where(live, meta[0, slot].astype(i32) * coarse_cols + target, 0))
                empty = jnp.zeros_like(rights[0])
                right = jnp.concatenate(
                    [jnp.concatenate([rights[0], empty], axis=0), jnp.concatenate([empty, rights[1]], axis=0)], axis=1
                )
                prods = jnp.dot(left, right, preferred_element_type=f32)
                for side, place in enumerate(places):
                    part = prods[:, side * 2 * tile : (side + 1) * 2 * tile]
                    acc[place] += part[:tile] + part[tile:]


def products(first, last, n_panel, n_prev, n_new, sizes, *refs):
    tile, list_len, fine_rows, coarse_cols, fine_total, owned = sizes
    refs = list(refs)
    take = lambda n: [refs.pop(0) for _ in range(n)]
    if first:
        r_pays = take(n_panel)
    else:
        acc_in, panel, weights_in, ids_in, metas_in = take(5)
    pays = take(n_new)
    if last:
        strips, keep, send = take(3)
        acc, weights, part, goals = take(4)
    elif first:
        acc, weights, metas_out, panel, ids_out = take(5)
    else:
        acc, weights, metas_out = take(3)
    ids, metas, sems = take(3)
    half, quarter = GROUP // 2, fine_rows // 2
    n_all = n_prev + n_new
    row_index = lax.axis_index("row")
    meta_at = (half + quarter) * tile

    moves = [(pay.at[pl.ds(meta_at, META)], metas.at[n_prev + i]) for i, pay in enumerate(pays)]
    if first:
        moves += [(pay.at[pl.ds(quarter * tile, META)], ids.at[m]) for m, pay in enumerate(r_pays)]
    else:
        moves += [(ids_in, ids), (metas_in, metas.at[pl.ds(0, n_prev)])]
    copies = [pltpu.make_async_copy(src, dst, sems.at[i]) for i, (src, dst) in enumerate(moves)]
    for copy in copies:
        copy.start()
    if first:
        acc[...] = jnp.zeros_like(acc)
        panel[fine_total] = jnp.zeros((tile, 2 * tile), bf16)
        for m, pay in enumerate(r_pays):
            at = (row_index ^ m) * fine_rows
            for k in range(quarter):
                panel[at + k], panel[at + k + quarter] = halves(pay[k * tile : (k + 1) * tile, :])
            ids_out[m] = pay[quarter * tile : quarter * tile + META, :]
    else:
        acc[...] = acc_in[...]
        weights[...] = weights_in[...]
    if not last:
        if n_prev:
            metas_out[:n_prev] = metas_in[...]
        for i, pay in enumerate(pays):
            metas_out[n_prev + i] = pay[meta_at : meta_at + META, :]
    for copy in copies:
        copy.wait()

    for i, pay in enumerate(pays):
        meta = metas.at[n_prev + i]

        @pl.when(meta[2, 0] > 0)
        def _(pay=pay, meta=meta):
            at = pl.multiple_of(meta[2, 1].astype(i32) * tile, tile)
            for k in range(quarter):
                block = half + k
                for kk, wide in zip((k, k + quarter), halves(pay[block * tile : (block + 1) * tile, :])):
                    weights[kk, pl.ds(at, tile), :] = wide

        groups = range(list_len // GROUP if pay.shape[0] > meta_at + META else 1)
        add_products(pay, meta_at + META, groups, meta, ids, panel, sizes, acc)
    if not last:
        return

    dump = part.shape[0] - 1
    n_chips = keep.shape[0] // owned
    for i in range(n_all):

        @pl.when(metas[i, 2, 0] > 0)
        def _(i=i):
            source = metas[i, 2, 1].astype(i32)
            for k in range(fine_rows):
                goal = metas[i, 3, k].astype(i32)
                owner, within = divide(jnp.maximum(goal, 0), owned)
                chip, core = divide(owner ^ row_index, 2)
                goals[source, k] = jnp.where(goal >= 0, (core * n_chips + chip) * owned + within, dump)

    part[...] = jnp.zeros_like(part)
    n_sources = weights.shape[1] // tile
    for k in range(fine_rows):
        sums = []
        for m in range(coarse_cols):
            both = acc[k * coarse_cols + m]
            sums.append(both + pltpu.roll(both, tile, 1))
        left = lax.broadcasted_iota(i32, sums[0].shape, 1) < tile
        strip = jnp.concatenate(
            [jnp.where(left, sums[m], sums[m + 1]) for m in range(0, coarse_cols, 2)], axis=1
        )
        strips[k] = strip
        high, low = split(strip)
        right = jnp.concatenate([high, high, low, low], axis=0)
        wide = weights[k]
        terms = jnp.dot(jnp.concatenate([wide, wide], axis=1), right, preferred_element_type=f32)
        for source in range(n_sources):
            part[goals[source, k]] += terms[source * tile : (source + 1) * tile]
    keep[...] = part[: n_chips * owned]
    send[...] = part[n_chips * owned : 2 * n_chips * owned]


def write_product(strips, product):
    fine_rows, coarse_cols, tile = product.shape[:3]
    for k in range(fine_rows):
        for m in range(coarse_cols):
            product[k, m] = strips[k, :, m * tile : (m + 1) * tile]


def add_pair(keep, received, *outs):
    owned = outs[0].shape[0]
    for m, out in enumerate(outs):
        out[...] = keep[m * owned : (m + 1) * owned] + received[m * owned : (m + 1) * owned]


def add_all(*refs):
    *parts, out = refs
    total = parts[0][...]
    for part in parts[1:]:
        total = total + part[...]
    tile = out.shape[2]
    for j in range(out.shape[0]):
        for m in range(out.shape[1]):
            out[j, m] = total[j, :, m * tile : (m + 1) * tile]


def swap(x, axis, mask):
    n = lax.axis_size(axis)
    return lax.ppermute(x, axis, [(i, i ^ mask) for i in range(n)])


def line_hops(own, step, before):
    n = lax.axis_size("col")

    def hop(x, first):
        pairs = []
        for i in range(first, n - 1, 2):
            if i - (step - 1) >= 0:
                pairs.append((i, i + 1))
            if i + step <= n - 1:
                pairs.append((i + 1, i))
        return lax.ppermute(x, "col", pairs) if pairs else None

    found = {}
    for name, other, first in (("even", "odd", 0), ("odd", "even", 1)):
        x = own if step == 1 else before.get((other, step - 1))
        found[name, step] = hop(x, first) if x is not None else None
    return {key: x for key, x in found.items() if x is not None}


def shards(op_tiles, op_rows, op_cols, op_count, pro_tiles, pro_cols, pro_live):
    list_len, tile = op_tiles.shape[0], op_tiles.shape[2]
    fine_rows = pro_tiles.shape[0]
    row_count, col_count = lax.axis_size("row"), lax.axis_size("col")
    fine_total = fine_rows * row_count
    fine_cols = fine_total // col_count
    coarse_total = fine_total // COARSEN
    coarse_cols = coarse_total // col_count
    owned = coarse_total // row_count
    n_chips = row_count // 2
    sizes = (tile, list_len, fine_rows, coarse_cols, fine_total, owned)
    first_rows = (GROUP // 2 + fine_rows // 2) * tile + META
    z_rows = first_rows + (list_len - GROUP) // 2 * tile
    r_rows = fine_rows // 2 * tile + META

    z_pay, r_pay = call(
        functools.partial(pack, fine_cols, coarse_cols),
        (shape(z_rows, 2 * tile), shape(r_rows, 2 * tile)),
        7,
        (
            pltpu.VMEM(pro_tiles.shape, f32),
            pltpu.VMEM((1, list_len), i32),
            pltpu.VMEM((1, list_len), i32),
            pltpu.VMEM((1, 1), i32),
            pltpu.VMEM((1, fine_rows), i32),
            pltpu.VMEM((1, fine_rows), i32),
            pltpu.VMEM((GROUP,) + op_tiles.shape[1:], f32),
            pltpu.VMEM((list_len - GROUP,) + op_tiles.shape[1:], f32),
            pltpu.SemaphoreType.DMA((8,)),
        ),
        nbytes=4 * 2**20,
        space=HBM,
        limit=FULL_BYTES,
    )(
        op_tiles,
        pro_tiles,
        op_rows.reshape(1, -1),
        op_cols.reshape(1, -1),
        op_count,
        pro_cols.reshape(1, -1),
        pro_live.reshape(1, -1),
    )

    found = [line_hops(z_pay, 1, {})]
    for step in range(2, col_count):
        found.append(line_hops(z_pay, step, found[-1]))
    chips = [r_pay] + [swap(r_pay, "row", m) for m in range(2, row_count, 2)]
    panel_pays = [x for pair in zip(chips, [swap(x, "row", 1) for x in chips]) for x in pair]

    def stage(first, last, n_prev, state, pays):
        n_all = n_prev + len(pays)
        out = [
            shape(fine_rows * coarse_cols, tile, 2 * tile),
            shape(fine_rows, col_count * tile, 2 * tile, dtype=bf16),
            shape(n_all, META, 2 * tile),
        ]
        scratch = [
            pltpu.SMEM((row_count, META, 2 * tile), f32),
            pltpu.SMEM((n_all, META, 2 * tile), f32),
            pltpu.SemaphoreType.DMA((row_count + n_all + 2,)),
        ]
        if first:
            out += [shape(fine_total + 1, tile, 2 * tile, dtype=bf16), shape(row_count, META, 2 * tile)]
        if last:
            spread = n_chips * owned
            scratch = [
                pltpu.VMEM(out[0].shape, f32),
                pltpu.VMEM(out[1].shape, bf16),
                pltpu.VMEM((2 * spread + 1, tile, coarse_cols * tile), f32),
                pltpu.SMEM((col_count, fine_rows), i32),
            ] + scratch
            out = [shape(fine_rows, tile, coarse_cols * tile)] + [shape(spread, tile, coarse_cols * tile)] * 2
        operands = list(state) + list(pays)
        kernel = functools.partial(products, first, last, row_count, n_prev, len(pays), sizes)
        return call(kernel, tuple(out), len(operands), scratch, flops=2**28, nbytes=4 * 2**20)(*operands)

    early = [z_pay] + list(found[0].values())
    middle = [x for step in found[1:-1] for x in step.values()]
    late = list(found[-1].values())
    acc, weights, metas, panel, ids = stage(True, False, 0, panel_pays, early)
    acc, weights, metas = stage(False, False, len(early), (acc, panel, weights, ids, metas), middle)
    strips, keep, send = stage(False, True, len(early + middle), (acc, panel, weights, ids, metas), late)

    received = swap(send, "row", 1)
    product = call(
        write_product, shape(fine_rows, coarse_cols, tile, tile), 1, flops=2**24, nbytes=2**20
    )(strips)
    part = shape(owned, tile, coarse_cols * tile)
    parts = call(add_pair, (part,) * n_chips, 2, nbytes=2**20)(keep, received)
    others = [swap(parts[m], "row", 2 * m) for m in range(1, n_chips)]
    coarse = call(add_all, shape(owned, coarse_cols, tile, tile), n_chips, nbytes=2**20)(parts[0], *others)
    return (product, coarse)


def solution(mesh):
    return jax.shard_map(
        shards,
        mesh=mesh,
        in_specs=(
            P("row", "col", None, None),
            P("row", "col"),
            P("row", "col"),
            P("row", "col"),
            P("row", "col", None, None),
            P("row", "col"),
            P("row", "col"),
        ),
        out_specs=(P("row", "col", None, None), P("row", "col", None, None)),
        check_vma=False,
    )
```

time: 79.7 us -> 72.5 us (0.910)
  local copies, waits for them, and re-layouts: 6.75 us -> 1.99 us
  waiting for transfers between devices: 44 us -> 41.4 us
    unnamed x16 -> x4, local copies, waits for them, and re-layouts: 6.75 us -> 1.99 us
    ppermute x5, waiting for transfers between devices: 29.4 us -> 26.8 us  [hop(): return lax.ppermute(x, 'col', pairs) if pairs else None]
    pallas_call x2 -> x4, Pallas kernels: 11.3 us -> 9.21 us  [the longest x3 8.04 us: stage(): call(kernel, tuple(out), len(operands), scratch, flops=2 ** 28, nbytes=4...]
    pallas_call x1, Pallas kernels: 0.57 us -> 2.42 us  [shards(): call(functools.partial(pack, fine_cols, coarse_cols), (shape(z_rows, 2 *...]
  transfers between devices with their start and end apart: 16 -> 16, of which waited for: 12 -> 11; matrix products, arithmetic and copies ran while one was open for 0% -> 0% of each run, Pallas kernels for 4% -> 8%
where the time goes in v2:
time: 72.5 us; the launch traced here: 72.1 us
  waiting for transfers between devices  41.4 us (57%)
  starting transfers between devices  14.8 us (20%)
  Pallas kernels  12.5 us (17%)
  local copies, waits for them, and re-layouts  1.99 us (3%)
  between operations  1.38 us (2%)
    ppermute x5, waiting for transfers between devices, hop(): return lax.ppermute(x, 'col', pairs) if pairs else None  26.8 us
    ppermute x11, waiting for transfers between devices, swap(): return lax.ppermute(x, axis, [(i, i ^ mask) for i in range(n)])  14.6 us
    pallas_call x3, Pallas kernels, stage(): call(kernel, tuple(out), len(operands), scratch, flops=2 ** 28, nbytes=4...  8.04 us
    ppermute x11, starting transfers between devices, swap(): return lax.ppermute(x, axis, [(i, i ^ mask) for i in range(n)])  7.76 us
    ppermute x5, starting transfers between devices, hop(): return lax.ppermute(x, 'col', pairs) if pairs else None  7.06 us
    pallas_call x1, Pallas kernels, shards(): call(functools.partial(pack, fine_cols, coarse_cols), (shape(z_rows, 2 *...  2.42 us
    unnamed x4, local copies, waits for them, and re-layouts  1.99 us
  transfers between devices with their start and end apart: 16, of which 11 were waited for; matrix products, arithmetic and copies ran while one was open for 0% of the time, Pallas kernels for 8%

profile of v2, /device:TPU:0, one launch (start us, length us, event | category | flops | bytes accessed | tf_op | source)
XLA Modules:
  0.0 72.1 jit_solution(9071083538351620350)
XLA Ops:
  1.3 2.4 %shard_map.86 = (f32[1288,128]{1,0:T(8,128)}, f32[264,128]{1,0:T(8,128)}) custom-call(f32[32,1,64,64]{3,2,1,0:T(8,128)} %op.1, f32[8,1,64,64]{3,2,1,0:T(8,128)} %pro.1, s32[1,32]{1,0:T(1,128)} %bitcast.4, s32[1,32]{1,0:T(1,128)} %bitcast.5, s32[1,1]{1,0:T(1,128)S(6)} %copy.9.count, s32[1,8]{1,0:T(1,128)} %bitcast.6, s32[1,8]{1,0:T(1,128)} %bitcast.7), custom_call_target="tpu_custom_call" | custom-call | bytes 4194304 | tf_op jit(solution)/shard_map/pallas_call | solution.py:291
  3.7 3.1 %collective-permute-start.7 = (f32[1288,128]{1,0:T(8,128)}, f32[1288,128]{1,0:T(8,128)S(1)}, u32[]{:S(2)}, u32[]{:S(2)}) collective-permute-start(f32[1288,128]{1,0:T(8,128)} %get-tuple-element.20.refs_8_), channel_id=1, source_target_pairs={{0,1},{1,0},{2,3},{3,2},{4,5},{5,4},{6,7},{7,6},{8,9},{9,8},{10,11... | collective-permute-start | bytes 1978376 | tf_op jit(solution)/shard_map/ppermute | solution.py:267
  7.5 14.3 %collective-permute-done.7.refs_9_ = f32[1288,128]{1,0:T(8,128)S(1)} collective-permute-done((f32[1288,128]{1,0:T(8,128)}, f32[1288,128]{1,0:T(8,128)S(1)}, u32[]{:S(2)}, u32[]{:S(2)}) %collective-permute-start.7) | collective-permute-done | bytes 659488 | tf_op jit(solution)/shard_map/ppermute | solution.py:267
  22.5 1.3 %collective-permute-start.9 = (f32[1288,128]{1,0:T(8,128)S(1)}, f32[1288,128]{1,0:T(8,128)S(1)}, u32[]{:S(2)}, u32[]{:S(2)}) collective-permute-start(f32[1288,128]{1,0:T(8,128)S(1)} %collective-permute-done.8.refs_10_), channel_id=1, source_target_pairs={{1,0},{2,3},{5,4},{6,7},{9,8},{10,11},{13,12},{14,15},{17,16},{18,... | collective-permute-start | bytes 1978376 | tf_op jit(solution)/shard_map/ppermute | solution.py:267
  23.8 1.3 %collective-permute-start.11 = (f32[1288,128]{1,0:T(8,128)S(1)}, f32[1288,128]{1,0:T(8,128)S(1)}, u32[]{:S(2)}, u32[]{:S(2)}) collective-permute-start(f32[1288,128]{1,0:T(8,128)S(1)} %collective-permute-done.10.refs_6_), channel_id=1, source_target_pairs={{1,0},{2,3},{5,4},{6,7},{9,8},{10,11},{13,12},{14,15},{17,16},{18,... | collective-permute-start | bytes 1978376 | tf_op jit(solution)/shard_map/ppermute | solution.py:267
  25.1 1.7 %collective-permute-start.1 = (f32[264,128]{1,0:T(8,128)}, f32[264,128]{1,0:T(8,128)S(1)}, u32[]{:S(2)}, u32[]{:S(2)}) collective-permute-start(f32[264,128]{1,0:T(8,128)} %get-tuple-element.19.refs_0_), channel_id=1, source_target_pairs={{0,8},{4,12},{8,0},{12,4},{16,24},{20,28},{24,16},{28,20},{1,9},{5... | collective-permute-start | bytes 405512 | tf_op jit(solution)/shard_map/ppermute | solution.py:254
  26.9 1.5 %collective-permute-start.3 = (f32[264,128]{1,0:T(8,128)}, f32[264,128]{1,0:T(8,128)S(1)}, u32[]{:S(2)}, u32[]{:S(2)}) collective-permute-start(f32[264,128]{1,0:T(8,128)} %get-tuple-element.19.refs_0_), channel_id=1, source_target_pairs={{0,16},{4,20},{8,24},{12,28},{16,0},{20,4},{24,8},{28,12},{1,17},{... | collective-permute-start | bytes 405512 | tf_op jit(solution)/shard_map/ppermute | solution.py:254
  28.7 2.7 %collective-permute-done.1.refs_2_ = f32[264,128]{1,0:T(8,128)S(1)} collective-permute-done((f32[264,128]{1,0:T(8,128)}, f32[264,128]{1,0:T(8,128)S(1)}, u32[]{:S(2)}, u32[]{:S(2)}) %collective-permute-start.1) | collective-permute-done | bytes 135200 | tf_op jit(solution)/shard_map/ppermute | solution.py:254
  31.4 3.5 %collective-permute-done.3.refs_4_ = f32[264,128]{1,0:T(8,128)S(1)} collective-permute-done((f32[264,128]{1,0:T(8,128)}, f32[264,128]{1,0:T(8,128)S(1)}, u32[]{:S(2)}, u32[]{:S(2)}) %collective-permute-start.3) | collective-permute-done | bytes 135200 | tf_op jit(solution)/shard_map/ppermute | solution.py:254
  35.5 0.8 %collective-permute-done.2.refs_3_ = f32[264,128]{1,0:T(8,128)S(1)} collective-permute-done((f32[264,128]{1,0:T(8,128)S(1)}, f32[264,128]{1,0:T(8,128)S(1)}, u32[]{:S(2)}, u32[]{:S(2)}) %collective-permute-start.2) | collective-permute-done | bytes 135200 | tf_op jit(solution)/shard_map/ppermute | solution.py:254
  36.7 1.1 %copy-done = f32[1288,128]{1,0:T(8,128)S(1)} copy-done((f32[1288,128]{1,0:T(8,128)S(1)}, f32[1288,128]{1,0:T(8,128)}, u32[]{:S(2)}) %copy-start) | copy-done | bytes 659480
  37.8 0.9 %copy-done.1 = f32[264,128]{1,0:T(8,128)S(1)} copy-done((f32[264,128]{1,0:T(8,128)S(1)}, f32[264,128]{1,0:T(8,128)}, u32[]{:S(2)}) %copy-start.1) | copy-done | bytes 135192
  38.7 2.9 %shard_map.87 = (f32[32,64,128]{2,1,0:T(8,128)S(1)}, bf16[8,256,128]{2,1,0:T(8,128)(2,1)S(1)}, f32[3,8,128]{2,1,0:T(8,128)S(1)}, bf16[65,64,128]{2,1,0:T(8,128)(2,1)S(1)}, f32[8,8,128]{2,1,0:T(8,128)S(1)}) custom-call(f32[264,128]{1,0:T(8,128)S(1)} %copy-done.1, f32[264,128]{1,0:T(8,128)S(1)} %collective-permute-done.refs_1_, ...), custom_call_target="tpu_custom_call" | custom-call | flops 268435456 | bytes 4194304 | tf_op jit(solution)/shard_map/pallas_call | solution.py:350
  41.7 1.0 %collective-permute-done.9.refs_5_ = f32[1288,128]{1,0:T(8,128)S(1)} collective-permute-done((f32[1288,128]{1,0:T(8,128)S(1)}, f32[1288,128]{1,0:T(8,128)S(1)}, u32[]{:S(2)}, u32[]{:S(2)}) %collective-permute-start.9) | collective-permute-done | bytes 659488 | tf_op jit(solution)/shard_map/ppermute | solution.py:267
  42.6 2.0 %shard_map.88 = (f32[32,64,128]{2,1,0:T(8,128)S(1)}, bf16[8,256,128]{2,1,0:T(8,128)(2,1)S(1)}, f32[5,8,128]{2,1,0:T(8,128)S(1)}) custom-call(f32[32,64,128]{2,1,0:T(8,128)S(1)} %get-tuple-element.21.refs_0_, bf16[65,64,128]{2,1,0:T(8,128)(2,1)S(1)} %get-tuple-element.22.refs_1_, bf16[8,256,128]{2,1,0:T(8,128)(2,1)S(1)} %get-tuple-element.23.refs_2_, ...), custom_call_target="tpu_custom_call" | custom-call | flops 268435456 | bytes 4194304 | tf_op jit(solution)/shard_map/pallas_call | solution.py:350
  44.7 11.5 %collective-permute-done.11.refs_5_ = f32[1288,128]{1,0:T(8,128)S(1)} collective-permute-done((f32[1288,128]{1,0:T(8,128)S(1)}, f32[1288,128]{1,0:T(8,128)S(1)}, u32[]{:S(2)}, u32[]{:S(2)}) %collective-permute-start.11) | collective-permute-done | bytes 659488 | tf_op jit(solution)/shard_map/ppermute | solution.py:267
  56.1 3.1 %shard_map.89 = (f32[8,64,256]{2,1,0:T(8,128)S(1)}, f32[8,64,256]{2,1,0:T(8,128)S(1)}, f32[8,64,256]{2,1,0:T(8,128)S(1)}) custom-call(f32[32,64,128]{2,1,0:T(8,128)S(1)} %get-tuple-element.26.refs_0_, bf16[65,64,128]{2,1,0:T(8,128)(2,1)S(1)} %get-tuple-element.22.refs_1_, bf16[8,256,128]{2,1,0:T(8,128)(2,1)S(1)} %get-tuple-element.27.refs_2_, ...), custom_call_target="tpu_custom_call" | custom-call | flops 268435456 | bytes 4194304 | tf_op jit(solution)/shard_map/pallas_call | solution.py:350
  59.3 1.9 %collective-permute-done.12.received = f32[8,64,256]{2,1,0:T(8,128)S(1)} collective-permute-done((f32[8,64,256]{2,1,0:T(8,128)S(1)}, f32[8,64,256]{2,1,0:T(8,128)S(1)}, u32[]{:S(2)}, u32[]{:S(2)}) %collective-permute-start.12) | collective-permute-done | bytes 524320 | tf_op jit(solution)/shard_map/ppermute | solution.py:254
  61.3 1.9 %collective-permute-start.13 = (f32[2,64,256]{2,1,0:T(8,128)S(1)}, f32[2,64,256]{2,1,0:T(8,128)S(1)}, u32[]{:S(2)}, u32[]{:S(2)}) collective-permute-start(f32[2,64,256]{2,1,0:T(8,128)S(1)} %get-tuple-element.33), channel_id=1, source_target_pairs={{0,8},{4,12},{8,0},{12,4},{16,24},{20,28},{24,16},{28,20},{1,9},{5... | collective-permute-start | bytes 393224 | tf_op jit(solution)/shard_map/ppermute | solution.py:254
  63.2 1.2 %collective-permute-start.14 = (f32[2,64,256]{2,1,0:T(8,128)S(1)}, f32[2,64,256]{2,1,0:T(8,128)S(1)}, u32[]{:S(2)}, u32[]{:S(2)}) collective-permute-start(f32[2,64,256]{2,1,0:T(8,128)S(1)} %get-tuple-element.34), channel_id=1, source_target_pairs={{0,16},{4,20},{8,24},{12,28},{16,0},{20,4},{24,8},{28,12},{1,17},{... | collective-permute-start | bytes 393224 | tf_op jit(solution)/shard_map/ppermute | solution.py:254
  64.8 1.2 %shard_map.90 = f32[8,4,64,64]{3,2,1,0:T(8,128)} custom-call(f32[8,64,256]{2,1,0:T(8,128)S(1)} %get-tuple-element.29.strips), custom_call_target="tpu_custom_call" | custom-call | flops 16777216 | bytes 1048576 | tf_op jit(solution)/shard_map/pallas_call | solution.py:360
  66.0 1.1 %collective-permute-done.13.refs_1_ = f32[2,64,256]{2,1,0:T(8,128)S(1)} collective-permute-done((f32[2,64,256]{2,1,0:T(8,128)S(1)}, f32[2,64,256]{2,1,0:T(8,128)S(1)}, u32[]{:S(2)}, u32[]{:S(2)}) %collective-permute-start.13) | collective-permute-done | bytes 131104 | tf_op jit(solution)/shard_map/ppermute | solution.py:254
  67.1 4.2 %collective-permute-done.14.refs_2_ = f32[2,64,256]{2,1,0:T(8,128)S(1)} collective-permute-done((f32[2,64,256]{2,1,0:T(8,128)S(1)}, f32[2,64,256]{2,1,0:T(8,128)S(1)}, u32[]{:S(2)}, u32[]{:S(2)}) %collective-permute-start.14) | collective-permute-done | bytes 131104 | tf_op jit(solution)/shard_map/ppermute | solution.py:254
  71.3 0.8 %shard_map.92 = f32[2,4,64,64]{3,2,1,0:T(8,128)} custom-call(f32[2,64,256]{2,1,0:T(8,128)S(1)} %get-tuple-element.32.refs_0_, f32[2,64,256]{2,1,0:T(8,128)S(1)} %collective-permute-done.13.refs_1_, f32[2,64,256]{2,1,0:T(8,128)S(1)} %collective-permute-done.14.refs_2_, f32[2,64,256]{2,1,0:T(8,128)S(1)} %collective-permute-done.15.refs_3_), custom_call_target="tpu_custom_call" | custom-call | bytes 1048576 | tf_op jit(solution)/shard_map/pallas_call | solution.py:366
  (19 shorter events, 3.4 us)
Async XLA Ops:
  3.7 18.1 %collective-permute-start.7 = (f32[1288,128]{1,0:T(8,128)}, f32[1288,128]{1,0:T(8,128)S(1)}, u32[]{:S(2)}, u32[]{:S(2)}) collective-permute-start(f32[1288,128]{1,0:T(8,128)} %get-tuple-element.20.refs_8_), channel_id=1, source_target_pairs={{0,1},{1,0},{2,3},{3,2},{4,5},{5,4},{6,7},{7,6},{8,9},{9,8},{10,11... | collective-permute-start | bytes 1978376 | tf_op jit(solution)/shard_map/ppermute | solution.py:267
  6.8 15.7 %collective-permute-start.8 = (f32[1288,128]{1,0:T(8,128)}, f32[1288,128]{1,0:T(8,128)S(1)}, u32[]{:S(2)}, u32[]{:S(2)}) collective-permute-start(f32[1288,128]{1,0:T(8,128)} %get-tuple-element.20.refs_8_), channel_id=1, source_target_pairs={{1,2},{2,1},{5,6},{6,5},{9,10},{10,9},{13,14},{14,13},{17,18},{18,... | collective-permute-start | bytes 1978376 | tf_op jit(solution)/shard_map/ppermute | solution.py:267
  21.8 2.0 %collective-permute-start.10 = (f32[1288,128]{1,0:T(8,128)S(1)}, f32[1288,128]{1,0:T(8,128)S(1)}, u32[]{:S(2)}, u32[]{:S(2)}) collective-permute-start(f32[1288,128]{1,0:T(8,128)S(1)} %collective-permute-done.7.refs_9_), channel_id=1, source_target_pairs={{1,2},{2,1},{5,6},{6,5},{9,10},{10,9},{13,14},{14,13},{17,18},{18,... | collective-permute-start | bytes 1978376 | tf_op jit(solution)/shard_map/ppermute | solution.py:267
  22.5 20.1 %collective-permute-start.9 = (f32[1288,128]{1,0:T(8,128)S(1)}, f32[1288,128]{1,0:T(8,128)S(1)}, u32[]{:S(2)}, u32[]{:S(2)}) collective-permute-start(f32[1288,128]{1,0:T(8,128)S(1)} %collective-permute-done.8.refs_10_), channel_id=1, source_target_pairs={{1,0},{2,3},{5,4},{6,7},{9,8},{10,11},{13,12},{14,15},{17,16},{18,... | collective-permute-start | bytes 1978376 | tf_op jit(solution)/shard_map/ppermute | solution.py:267
  23.8 32.3 %collective-permute-start.11 = (f32[1288,128]{1,0:T(8,128)S(1)}, f32[1288,128]{1,0:T(8,128)S(1)}, u32[]{:S(2)}, u32[]{:S(2)}) collective-permute-start(f32[1288,128]{1,0:T(8,128)S(1)} %collective-permute-done.10.refs_6_), channel_id=1, source_target_pairs={{1,0},{2,3},{5,4},{6,7},{9,8},{10,11},{13,12},{14,15},{17,16},{18,... | collective-permute-start | bytes 1978376 | tf_op jit(solution)/shard_map/ppermute | solution.py:267
  25.1 6.2 %collective-permute-start.1 = (f32[264,128]{1,0:T(8,128)}, f32[264,128]{1,0:T(8,128)S(1)}, u32[]{:S(2)}, u32[]{:S(2)}) collective-permute-start(f32[264,128]{1,0:T(8,128)} %get-tuple-element.19.refs_0_), channel_id=1, source_target_pairs={{0,8},{4,12},{8,0},{12,4},{16,24},{20,28},{24,16},{28,20},{1,9},{5... | collective-permute-start | bytes 405512 | tf_op jit(solution)/shard_map/ppermute | solution.py:254
  26.9 8.0 %collective-permute-start.3 = (f32[264,128]{1,0:T(8,128)}, f32[264,128]{1,0:T(8,128)S(1)}, u32[]{:S(2)}, u32[]{:S(2)}) collective-permute-start(f32[264,128]{1,0:T(8,128)} %get-tuple-element.19.refs_0_), channel_id=1, source_target_pairs={{0,16},{4,20},{8,24},{12,28},{16,0},{20,4},{24,8},{28,12},{1,17},{... | collective-permute-start | bytes 405512 | tf_op jit(solution)/shard_map/ppermute | solution.py:254
  28.4 6.5 %collective-permute-start.5 = (f32[264,128]{1,0:T(8,128)}, f32[264,128]{1,0:T(8,128)S(1)}, u32[]{:S(2)}, u32[]{:S(2)}) collective-permute-start(f32[264,128]{1,0:T(8,128)} %get-tuple-element.19.refs_0_), channel_id=1, source_target_pairs={{0,24},{4,28},{8,16},{12,20},{16,8},{20,12},{24,0},{28,4},{1,25},{... | collective-permute-start | bytes 405512 | tf_op jit(solution)/shard_map/ppermute | solution.py:254
  31.4 4.0 %collective-permute-start = (f32[264,128]{1,0:T(8,128)}, f32[264,128]{1,0:T(8,128)S(1)}, u32[]{:S(2)}, u32[]{:S(2)}) collective-permute-start(f32[264,128]{1,0:T(8,128)} %get-tuple-element.19.refs_0_), channel_id=1, source_target_pairs={{0,4},{4,0},{8,12},{12,8},{16,20},{20,16},{24,28},{28,24},{1,5},{5... | collective-permute-start | bytes 405512 | tf_op jit(solution)/shard_map/ppermute | solution.py:254
  34.9 1.4 %collective-permute-start.2 = (f32[264,128]{1,0:T(8,128)S(1)}, f32[264,128]{1,0:T(8,128)S(1)}, u32[]{:S(2)}, u32[]{:S(2)}) collective-permute-start(f32[264,128]{1,0:T(8,128)S(1)} %collective-permute-done.1.refs_2_), channel_id=1, source_target_pairs={{0,4},{4,0},{8,12},{12,8},{16,20},{20,16},{24,28},{28,24},{1,5},{5... | collective-permute-start | bytes 405512 | tf_op jit(solution)/shard_map/ppermute | solution.py:254
  34.9 1.5 %collective-permute-start.4 = (f32[264,128]{1,0:T(8,128)S(1)}, f32[264,128]{1,0:T(8,128)S(1)}, u32[]{:S(2)}, u32[]{:S(2)}) collective-permute-start(f32[264,128]{1,0:T(8,128)S(1)} %collective-permute-done.3.refs_4_), channel_id=1, source_target_pairs={{0,4},{4,0},{8,12},{12,8},{16,20},{20,16},{24,28},{28,24},{1,5},{5... | collective-permute-start | bytes 405512 | tf_op jit(solution)/shard_map/ppermute | solution.py:254
  35.4 1.4 %collective-permute-start.6 = (f32[264,128]{1,0:T(8,128)S(1)}, f32[264,128]{1,0:T(8,128)S(1)}, u32[]{:S(2)}, u32[]{:S(2)}) collective-permute-start(f32[264,128]{1,0:T(8,128)S(1)} %collective-permute-done.5.refs_6_), channel_id=1, source_target_pairs={{0,4},{4,0},{8,12},{12,8},{16,20},{20,16},{24,28},{28,24},{1,5},{5... | collective-permute-start | bytes 405512 | tf_op jit(solution)/shard_map/ppermute | solution.py:254
  36.7 1.1 %copy-start = (f32[1288,128]{1,0:T(8,128)S(1)}, f32[1288,128]{1,0:T(8,128)}, u32[]{:S(2)}) copy-start(f32[1288,128]{1,0:T(8,128)} %get-tuple-element.20.refs_8_) | copy-start | bytes 1978372
  37.8 0.9 %copy-start.1 = (f32[264,128]{1,0:T(8,128)S(1)}, f32[264,128]{1,0:T(8,128)}, u32[]{:S(2)}) copy-start(f32[264,128]{1,0:T(8,128)} %get-tuple-element.19.refs_0_) | copy-start | bytes 405508
  59.2 2.0 %collective-permute-start.12 = (f32[8,64,256]{2,1,0:T(8,128)S(1)}, f32[8,64,256]{2,1,0:T(8,128)S(1)}, u32[]{:S(2)}, u32[]{:S(2)}) collective-permute-start(f32[8,64,256]{2,1,0:T(8,128)S(1)} %get-tuple-element.31), channel_id=1, source_target_pairs={{0,4},{4,0},{8,12},{12,8},{16,20},{20,16},{24,28},{28,24},{1,5},{5... | collective-permute-start | bytes 1572872 | tf_op jit(solution)/shard_map/ppermute | solution.py:254
  61.3 5.8 %collective-permute-start.13 = (f32[2,64,256]{2,1,0:T(8,128)S(1)}, f32[2,64,256]{2,1,0:T(8,128)S(1)}, u32[]{:S(2)}, u32[]{:S(2)}) collective-permute-start(f32[2,64,256]{2,1,0:T(8,128)S(1)} %get-tuple-element.33), channel_id=1, source_target_pairs={{0,8},{4,12},{8,0},{12,4},{16,24},{20,28},{24,16},{28,20},{1,9},{5... | collective-permute-start | bytes 393224 | tf_op jit(solution)/shard_map/ppermute | solution.py:254
  63.2 8.1 %collective-permute-start.14 = (f32[2,64,256]{2,1,0:T(8,128)S(1)}, f32[2,64,256]{2,1,0:T(8,128)S(1)}, u32[]{:S(2)}, u32[]{:S(2)}) collective-permute-start(f32[2,64,256]{2,1,0:T(8,128)S(1)} %get-tuple-element.34), channel_id=1, source_target_pairs={{0,16},{4,20},{8,24},{12,28},{16,0},{20,4},{24,8},{28,12},{1,17},{... | collective-permute-start | bytes 393224 | tf_op jit(solution)/shard_map/ppermute | solution.py:254
  64.3 6.9 %collective-permute-start.15 = (f32[2,64,256]{2,1,0:T(8,128)S(1)}, f32[2,64,256]{2,1,0:T(8,128)S(1)}, u32[]{:S(2)}, u32[]{:S(2)}) collective-permute-start(f32[2,64,256]{2,1,0:T(8,128)S(1)} %get-tuple-element.35), channel_id=1, source_target_pairs={{0,24},{4,28},{8,16},{12,20},{16,8},{20,12},{24,0},{28,4},{1,25},{... | collective-permute-start | bytes 393224 | tf_op jit(solution)/shard_map/ppermute | solution.py:254

commit v3 on v2

--- a/solution.py
+++ b/solution.py
@@ -40,7 +40,7 @@
     return lax.shift_right_logical(x, n.bit_length() - 1), x & (n - 1)
 
 
-def pack(fine_cols, coarse_cols, op, pro, rows, cols, count, pro_cols, pro_live, z_pay, r_pay, *scratch):
+def pack(fine_cols, coarse_cols, op, pro, rows, cols, count, pro_cols, pro_live, whole, low, high, r_pay, *scratch):
     sems = scratch[-1]
     sources = (pro, rows, cols, count, pro_cols, pro_live, op.at[pl.ds(0, GROUP)], op.at[pl.ds(GROUP, op.shape[0] - GROUP)])
     copies = [pltpu.make_async_copy(src, dst, sems.at[i]) for i, (src, dst) in enumerate(zip(sources, scratch))]
@@ -54,29 +54,41 @@
     half, quarter = GROUP // 2, fine_rows // 2
     col_index = lax.axis_index("col")
     base = half * tile
+    eighth = quarter // 2
+    meta = base + eighth * tile
+    high_at = meta + META
+    high_base = (list_len - GROUP) // 2 * tile
     for k in range(quarter):
         pair = jnp.concatenate([pro[k, 0], pro[k + quarter, 0]], axis=1)
         r_pay[k * tile : (k + 1) * tile, :] = pair
         turned = pair.T
-        z_pay[base + k * tile : base + (k + 1) * tile, :] = jnp.concatenate([turned[:tile], turned[tile:]], axis=1)
-    meta = base + quarter * tile
-    high_at = meta + META
-    z_pay[meta : meta + META, :] = jnp.zeros((META, 2 * tile), f32)
+        turned = jnp.concatenate([turned[:tile], turned[tile:]], axis=1)
+        part, at = (low, base + k * tile) if k < eighth else (high, high_base + (k - eighth) * tile)
+        part[at : at + tile, :] = turned
+        at += 0 if k < eighth else high_at
+        whole[at : at + tile, :] = turned
     r_pay[quarter * tile : quarter * tile + META, :] = jnp.zeros((META, 2 * tile), f32)
-    z_pay[meta : meta + 1, 0:list_len] = rows[...].astype(f32)
-    z_pay[meta + 1 : meta + 2, 0:list_len] = (cols[...] + col_index * fine_cols).astype(f32)
-    z_pay[meta + 2 : meta + 3, 0:1] = count[...].astype(f32)
-    z_pay[meta + 2 : meta + 3, 1:2] = jnp.full((1, 1), col_index, i32).astype(f32)
     live = pro_live[...] > 0
-    z_pay[meta + 3 : meta + 4, 0:fine_rows] = jnp.where(live, pro_cols[...] + col_index * coarse_cols, -1).astype(f32)
     r_pay[quarter * tile : quarter * tile + 1, 0:fine_rows] = jnp.where(live, pro_cols[...], -1).astype(f32)
+    goals = jnp.where(live, pro_cols[...] + col_index * coarse_cols, -1).astype(f32)
+    for pay in (whole, low):
+        pay[meta : meta + META, :] = jnp.zeros((META, 2 * tile), f32)
+        pay[meta : meta + 1, 0:list_len] = rows[...].astype(f32)
+        pay[meta + 1 : meta + 2, 0:list_len] = (cols[...] + col_index * fine_cols).astype(f32)
+        pay[meta + 2 : meta + 3, 0:1] = count[...].astype(f32)
+        pay[meta + 2 : meta + 3, 1:2] = jnp.full((1, 1), col_index, i32).astype(f32)
+        pay[meta + 3 : meta + 4, 0:fine_rows] = goals
     copies[-2].wait()
     for block in range(half):
-        z_pay[block * tile : (block + 1) * tile, :] = jnp.concatenate([low_tiles[block, 0], low_tiles[block + half, 0]], axis=1)
+        both = jnp.concatenate([low_tiles[block, 0], low_tiles[block + half, 0]], axis=1)
+        for pay in (whole, low):
+            pay[block * tile : (block + 1) * tile, :] = both
     copies[-1].wait()
     for block in range((list_len - GROUP) // 2):
         slot = block // half * GROUP + block % half
-        z_pay[high_at + block * tile : high_at + (block + 1) * tile, :] = jnp.concatenate([high_tiles[slot, 0], high_tiles[slot + half, 0]], axis=1)
+        both = jnp.concatenate([high_tiles[slot, 0], high_tiles[slot + half, 0]], axis=1)
+        high[block * tile : (block + 1) * tile, :] = both
+        whole[high_at + block * tile : high_at + (block + 1) * tile, :] = both
 
 
 def split(x):
@@ -94,12 +106,13 @@
     return first.astype(bf16), second.astype(bf16)
 
 
-def add_products(blocks, high_at, groups, meta, ids, panel, sizes, acc):
+def add_products(low_pay, high_pay, high_at, meta, ids, panel, sizes, acc):
     tile, list_len, fine_rows, coarse_cols, fine_total, owned = sizes
     count = meta[2, 0].astype(i32)
     half = GROUP // 2
     row_index = lax.axis_index("row")
-    for group in groups:
+    for group in range(list_len // GROUP):
+        blocks = high_pay if group else low_pay
 
         @pl.when(count > group * GROUP)
         def _(group=group):
@@ -125,7 +138,7 @@
                     acc[place] += part[:tile] + part[tile:]
 
 
-def products(first, last, n_panel, n_prev, n_new, sizes, *refs):
+def products(first, last, n_panel, n_prev, parts, sizes, *refs):
     tile, list_len, fine_rows, coarse_cols, fine_total, owned = sizes
     refs = list(refs)
     take = lambda n: [refs.pop(0) for _ in range(n)]
@@ -133,7 +146,7 @@
         r_pays = take(n_panel)
     else:
         acc_in, panel, weights_in, ids_in, metas_in = take(5)
-    pays = take(n_new)
+    pays = [take(n) for n in parts]
     if last:
         strips, keep, send = take(3)
         acc, weights, part, goals = take(4)
@@ -143,11 +156,13 @@
         acc, weights, metas_out = take(3)
     ids, metas, sems = take(3)
     half, quarter = GROUP // 2, fine_rows // 2
-    n_all = n_prev + n_new
+    n_all = n_prev + len(pays)
     row_index = lax.axis_index("row")
-    meta_at = (half + quarter) * tile
-
-    moves = [(pay.at[pl.ds(meta_at, META)], metas.at[n_prev + i]) for i, pay in enumerate(pays)]
+    eighth = quarter // 2
+    meta_at = (half + eighth) * tile
+    high_base = (list_len - GROUP) // 2 * tile
+
+    moves = [(pay[0].at[pl.ds(meta_at, META)], metas.at[n_prev + i]) for i, pay in enumerate(pays)]
     if first:
         moves += [(pay.at[pl.ds(quarter * tile, META)], ids.at[m]) for m, pay in enumerate(r_pays)]
     else:
@@ -170,7 +185,7 @@
         if n_prev:
             metas_out[:n_prev] = metas_in[...]
         for i, pay in enumerate(pays):
-            metas_out[n_prev + i] = pay[meta_at : meta_at + META, :]
+            metas_out[n_prev + i] = pay[0][meta_at : meta_at + META, :]
     for copy in copies:
         copy.wait()
 
@@ -181,12 +196,16 @@
         def _(pay=pay, meta=meta):
             at = pl.multiple_of(meta[2, 1].astype(i32) * tile, tile)
             for k in range(quarter):
-                block = half + k
-                for kk, wide in zip((k, k + quarter), halves(pay[block * tile : (block + 1) * tile, :])):
+                if k < eighth:
+                    block = pay[0][(half + k) * tile : (half + k + 1) * tile, :]
+                else:
+                    from_row = high_base + (k - eighth) * tile + (0 if len(pay) > 1 else meta_at + META)
+                    block = pay[-1][from_row : from_row + tile, :]
+                for kk, wide in zip((k, k + quarter), halves(block)):
                     weights[kk, pl.ds(at, tile), :] = wide
 
-        groups = range(list_len // GROUP if pay.shape[0] > meta_at + META else 1)
-        add_products(pay, meta_at + META, groups, meta, ids, panel, sizes, acc)
+        high_at = 0 if len(pay) > 1 else meta_at + META
+        add_products(pay[0], pay[-1], high_at, meta, ids, panel, sizes, acc)
     if not last:
         return
 
@@ -254,23 +273,24 @@
     return lax.ppermute(x, axis, [(i, i ^ mask) for i in range(n)])
 
 
-def line_hops(own, step, before):
+def line_gather(own, odd, hook=None):
     n = lax.axis_size("col")
-
-    def hop(x, first):
+    found = []
+    for step in range(1, n):
         pairs = []
-        for i in range(first, n - 1, 2):
+        for i in range((step - 1 + odd) % 2, n - 1, 2):
             if i - (step - 1) >= 0:
                 pairs.append((i, i + 1))
             if i + step <= n - 1:
                 pairs.append((i + 1, i))
-        return lax.ppermute(x, "col", pairs) if pairs else None
-
-    found = {}
-    for name, other, first in (("even", "odd", 0), ("odd", "even", 1)):
-        x = own if step == 1 else before.get((other, step - 1))
-        found[name, step] = hop(x, first) if x is not None else None
-    return {key: x for key, x in found.items() if x is not None}
+        if not pairs:
+            break
+        own = lax.ppermute(own, "col", pairs)
+        if step == 2 and hook is not None:
+            own, *rest = lax.optimization_barrier((own, *hook))
+            hook[:] = rest
+        found.append(own)
+    return found
 
 
 def shards(op_tiles, op_rows, op_cols, op_count, pro_tiles, pro_cols, pro_live):
@@ -284,13 +304,13 @@
     owned = coarse_total // row_count
     n_chips = row_count // 2
     sizes = (tile, list_len, fine_rows, coarse_cols, fine_total, owned)
-    first_rows = (GROUP // 2 + fine_rows // 2) * tile + META
-    z_rows = first_rows + (list_len - GROUP) // 2 * tile
+    first_rows = (GROUP // 2 + fine_rows // 4) * tile + META
+    z_rows = (list_len // 2 + fine_rows // 2) * tile + META
     r_rows = fine_rows // 2 * tile + META
 
-    z_pay, r_pay = call(
+    whole, low, high, r_pay = call(
         functools.partial(pack, fine_cols, coarse_cols),
-        (shape(z_rows, 2 * tile), shape(r_rows, 2 * tile)),
+        (shape(z_rows, 2 * tile), shape(first_rows, 2 * tile), shape(z_rows - first_rows, 2 * tile), shape(r_rows, 2 * tile)),
         7,
         (
             pltpu.VMEM(pro_tiles.shape, f32),
@@ -316,12 +336,11 @@
         pro_live.reshape(1, -1),
     )
 
-    found = [line_hops(z_pay, 1, {})]
-    for step in range(2, col_count):
-        found.append(line_hops(z_pay, step, found[-1]))
     chips = [r_pay] + [swap(r_pay, "row", m) for m in range(2, row_count, 2)]
     panel_pays = [x for pair in zip(chips, [swap(x, "row", 1) for x in chips]) for x in pair]
 
+    split_chain = list(zip(line_gather(low, False, panel_pays), line_gather(high, False)))
+    whole_chain = [(x,) for x in line_gather(whole, True)]
     def stage(first, last, n_prev, state, pays):
         n_all = n_prev + len(pays)
         out = [
@@ -345,13 +364,14 @@
                 pltpu.SMEM((col_count, fine_rows), i32),
             ] + scratch
             out = [shape(fine_rows, tile, coarse_cols * tile)] + [shape(spread, tile, coarse_cols * tile)] * 2
-        operands = list(state) + list(pays)
-        kernel = functools.partial(products, first, last, row_count, n_prev, len(pays), sizes)
+        operands = list(state) + [x for pay in pays for x in pay]
+        parts = [len(pay) for pay in pays]
+        kernel = functools.partial(products, first, last, row_count, n_prev, parts, sizes)
         return call(kernel, tuple(out), len(operands), scratch, flops=2**28, nbytes=4 * 2**20)(*operands)
 
-    early = [z_pay] + list(found[0].values())
-    middle = [x for step in found[1:-1] for x in step.values()]
-    late = list(found[-1].values())
+    early = [(low, high)] + split_chain[:1] + whole_chain[:1]
+    middle = split_chain[1:-1] + whole_chain[1:]
+    late = split_chain[-1:]
     acc, weights, metas, panel, ids = stage(True, False, 0, panel_pays, early)
     acc, weights, metas = stage(False, False, len(early), (acc, panel, weights, ids, metas), middle)
     strips, keep, send = stage(False, True, len(early + middle), (acc, panel, weights, ids, metas), late)

time: 72.5 us -> 70.8 us (0.977)
  waiting for transfers between devices: 41.4 us -> 31.4 us
  starting transfers between devices: 14.8 us -> 22 us
  local copies, waits for them, and re-layouts: 1.99 us -> 2.84 us
    ppermute x5 -> x8, waiting for transfers between devices: 26.8 us -> 20.4 us  [line_gather(): own = lax.ppermute(own, 'col', pairs)]
    ppermute x5 -> x8, starting transfers between devices: 7.06 us -> 11.9 us  [line_gather(): own = lax.ppermute(own, 'col', pairs)]
    ppermute x11, waiting for transfers between devices: 14.6 us -> 11.1 us  [swap(): return lax.ppermute(x, axis, [(i, i ^ mask) for i in range(n)])]
    ppermute x11, starting transfers between devices: 7.76 us -> 10.2 us  [swap(): return lax.ppermute(x, axis, [(i, i ^ mask) for i in range(n)])]
    unnamed x4 -> x6, local copies, waits for them, and re-layouts: 1.99 us -> 2.84 us
  transfers between devices with their start and end apart: 16 -> 19, of which waited for: 11 -> 10; matrix products, arithmetic and copies ran while one was open for 0% -> 0% of each run, Pallas kernels for 8% -> 9%
where the time goes in v3:
time: 70.8 us; the launch traced here: 70.4 us
  waiting for transfers between devices  31.4 us (44%)
  starting transfers between devices  22 us (31%)
  Pallas kernels  12.7 us (18%)
  local copies, waits for them, and re-layouts  2.84 us (4%)
  between operations  1.43 us (2%)
    ppermute x8, waiting for transfers between devices, line_gather(): own = lax.ppermute(own, 'col', pairs)  20.4 us
    ppermute x8, starting transfers between devices, line_gather(): own = lax.ppermute(own, 'col', pairs)  11.9 us
    ppermute x11, waiting for transfers between devices, swap(): return lax.ppermute(x, axis, [(i, i ^ mask) for i in range(n)])  11.1 us
    ppermute x11, starting transfers between devices, swap(): return lax.ppermute(x, axis, [(i, i ^ mask) for i in range(n)])  10.2 us
    pallas_call x3, Pallas kernels, stage(): call(kernel, tuple(out), len(operands), scratch, flops=2 ** 28, nbytes=4...  8.1 us
    unnamed x6, local copies, waits for them, and re-layouts  2.84 us
    pallas_call x1, Pallas kernels, shards(): call(functools.partial(pack, fine_cols, coarse_cols), (shape(z_rows, 2 *...  2.54 us
  transfers between devices with their start and end apart: 19, of which 10 were waited for; matrix products, arithmetic and copies ran while one was open for 0% of the time, Pallas kernels for 9%

profile of v3, /device:TPU:0, one launch (start us, length us, event | category | flops | bytes accessed | tf_op | source)
XLA Modules:
  0.0 70.4 jit_solution(13411970018799243849)
XLA Ops:
  1.3 2.5 %shard_map.86 = (f32[1288,128]{1,0:T(8,128)}, f32[648,128]{1,0:T(8,128)}, f32[640,128]{1,0:T(8,128)}, f32[264,128]{1,0:T(8,128)}) custom-call(f32[32,1,64,64]{3,2,1,0:T(8,128)} %op.1, f32[8,1,64,64]{3,2,1,0:T(8,128)} %pro.1, s32[1,32]{1,0:T(1,128)} %bitcast.4, s32[1,32]{1,0:T(1,128)} %bitcast.5, s32[1,1]{1,0:T(1,128)S(6)} %copy.9.count, s32[1,8]{1,0:T(1,128)} %bitcast.6, ...), custom_call_target="tpu_custom_call" | custom-call | bytes 4194304 | tf_op jit(solution)/shard_map/pallas_call | solution.py:311
  4.5 5.9 %collective-permute-start = (f32[648,128]{1,0:T(8,128)}, f32[648,128]{1,0:T(8,128)S(1)}, u32[]{:S(2)}, u32[]{:S(2)}) collective-permute-start(f32[648,128]{1,0:T(8,128)} %get-tuple-element.30.refs_8_), channel_id=1, source_target_pairs={{0,1},{1,0},{2,3},{3,2},{4,5},{5,4},{6,7},{7,6},{8,9},{9,8},{10,11... | collective-permute-start | bytes 995336 | tf_op jit(solution)/shard_map/ppermute | solution.py:288
  10.5 1.5 %collective-permute-start.3 = (f32[264,128]{1,0:T(8,128)}, f32[264,128]{1,0:T(8,128)S(1)}, u32[]{:S(2)}, u32[]{:S(2)}) collective-permute-start(f32[264,128]{1,0:T(8,128)} %get-tuple-element.32.refs_0_), channel_id=1, source_target_pairs={{0,8},{4,12},{8,0},{12,4},{16,24},{20,28},{24,16},{28,20},{1,9},{5... | collective-permute-start | bytes 405512 | tf_op jit(solution)/shard_map/ppermute | solution.py:273
  12.0 1.5 %collective-permute-start.5 = (f32[264,128]{1,0:T(8,128)}, f32[264,128]{1,0:T(8,128)S(1)}, u32[]{:S(2)}, u32[]{:S(2)}) collective-permute-start(f32[264,128]{1,0:T(8,128)} %get-tuple-element.32.refs_0_), channel_id=1, source_target_pairs={{0,16},{4,20},{8,24},{12,28},{16,0},{20,4},{24,8},{28,12},{1,17},{... | collective-permute-start | bytes 405512 | tf_op jit(solution)/shard_map/ppermute | solution.py:273
  13.5 2.2 %collective-permute-done.3.refs_2_ = f32[264,128]{1,0:T(8,128)S(1)} collective-permute-done((f32[264,128]{1,0:T(8,128)}, f32[264,128]{1,0:T(8,128)S(1)}, u32[]{:S(2)}, u32[]{:S(2)}) %collective-permute-start.3) | collective-permute-done | bytes 135200 | tf_op jit(solution)/shard_map/ppermute | solution.py:273
  15.7 2.4 %collective-permute-start.7 = (f32[264,128]{1,0:T(8,128)}, f32[264,128]{1,0:T(8,128)S(1)}, u32[]{:S(2)}, u32[]{:S(2)}) collective-permute-start(f32[264,128]{1,0:T(8,128)} %get-tuple-element.32.refs_0_), channel_id=1, source_target_pairs={{0,24},{4,28},{8,16},{12,20},{16,8},{20,12},{24,0},{28,4},{1,25},{... | collective-permute-start | bytes 405512 | tf_op jit(solution)/shard_map/ppermute | solution.py:273
  18.2 1.3 %collective-permute-start.12 = (f32[1288,128]{1,0:T(8,128)S(1)}, f32[1288,128]{1,0:T(8,128)S(1)}, u32[]{:S(2)}, u32[]{:S(2)}) collective-permute-start(f32[1288,128]{1,0:T(8,128)S(1)} %collective-permute-done.10.refs_12_), channel_id=1, source_target_pairs={{1,0},{2,3},{5,4},{6,7},{9,8},{10,11},{13,12},{14,15},{17,16},{18,... | collective-permute-start | bytes 1978376 | tf_op jit(solution)/shard_map/ppermute | solution.py:288
  20.1 5.0 %collective-permute-done.9.refs_11_ = f32[640,128]{1,0:T(8,128)S(1)} collective-permute-done((f32[640,128]{1,0:T(8,128)}, f32[640,128]{1,0:T(8,128)S(1)}, u32[]{:S(2)}, u32[]{:S(2)}) %collective-permute-start.9) | collective-permute-done | bytes 327712 | tf_op jit(solution)/shard_map/ppermute | solution.py:288
  26.4 1.1 %collective-permute-done.2.refs_1_ = f32[264,128]{1,0:T(8,128)S(1)} collective-permute-done((f32[264,128]{1,0:T(8,128)}, f32[264,128]{1,0:T(8,128)S(1)}, u32[]{:S(2)}, u32[]{:S(2)}) %collective-permute-start.2) | collective-permute-done | bytes 135200 | tf_op jit(solution)/shard_map/ppermute | solution.py:273
  29.0 1.3 %collective-permute-start.13 = (f32[648,128]{1,0:T(8,128)S(1)}, f32[648,128]{1,0:T(8,128)S(1)}, u32[]{:S(2)}, u32[]{:S(2)}) collective-permute-start(f32[648,128]{1,0:T(8,128)S(1)} %collective-permute-done.1.refs_5_), channel_id=1, source_target_pairs={{1,0},{2,3},{5,4},{6,7},{9,8},{10,11},{13,12},{14,15},{17,16},{18,... | collective-permute-start | bytes 995336 | tf_op jit(solution)/shard_map/ppermute | solution.py:288
  30.3 1.3 %collective-permute-start.14 = (f32[640,128]{1,0:T(8,128)S(1)}, f32[640,128]{1,0:T(8,128)S(1)}, u32[]{:S(2)}, u32[]{:S(2)}) collective-permute-start(f32[640,128]{1,0:T(8,128)S(1)} %collective-permute-done.11.refs_6_), channel_id=1, source_target_pairs={{1,0},{2,3},{5,4},{6,7},{9,8},{10,11},{13,12},{14,15},{17,16},{18,... | collective-permute-start | bytes 983048 | tf_op jit(solution)/shard_map/ppermute | solution.py:288
  31.6 1.0 %copy-done = f32[648,128]{1,0:T(8,128)S(1)} copy-done((f32[648,128]{1,0:T(8,128)S(1)}, f32[648,128]{1,0:T(8,128)}, u32[]{:S(2)}) %copy-start) | copy-done | bytes 331800
  32.6 1.0 %copy-done.1 = f32[640,128]{1,0:T(8,128)S(1)} copy-done((f32[640,128]{1,0:T(8,128)S(1)}, f32[640,128]{1,0:T(8,128)}, u32[]{:S(2)}) %copy-start.1) | copy-done | bytes 327704
  34.5 2.6 %shard_map.87 = (f32[32,64,128]{2,1,0:T(8,128)S(1)}, bf16[8,256,128]{2,1,0:T(8,128)(2,1)S(1)}, f32[3,8,128]{2,1,0:T(8,128)S(1)}, bf16[65,64,128]{2,1,0:T(8,128)(2,1)S(1)}, f32[8,8,128]{2,1,0:T(8,128)S(1)}) custom-call(f32[264,128]{1,0:T(8,128)S(1)} %copy-done.2, f32[264,128]{1,0:T(8,128)S(1)} %collective-permute-done.2.refs_1_, ...), custom_call_target="tpu_custom_call" | custom-call | flops 268435456 | bytes 4194304 | tf_op jit(solution)/shard_map/pallas_call | solution.py:370
  37.1 5.4 %collective-permute-done.12.refs_7_ = f32[1288,128]{1,0:T(8,128)S(1)} collective-permute-done((f32[1288,128]{1,0:T(8,128)S(1)}, f32[1288,128]{1,0:T(8,128)S(1)}, u32[]{:S(2)}, u32[]{:S(2)}) %collective-permute-start.12) | collective-permute-done | bytes 659488 | tf_op jit(solution)/shard_map/ppermute | solution.py:288
  42.5 2.4 %shard_map.88 = (f32[32,64,128]{2,1,0:T(8,128)S(1)}, bf16[8,256,128]{2,1,0:T(8,128)(2,1)S(1)}, f32[5,8,128]{2,1,0:T(8,128)S(1)}) custom-call(f32[32,64,128]{2,1,0:T(8,128)S(1)} %get-tuple-element.42.refs_0_, bf16[65,64,128]{2,1,0:T(8,128)(2,1)S(1)} %get-tuple-element.43.refs_1_, bf16[8,256,128]{2,1,0:T(8,128)(2,1)S(1)} %get-tuple-element.44.refs_2_, ...), custom_call_target="tpu_custom_call" | custom-call | flops 268435456 | bytes 4194304 | tf_op jit(solution)/shard_map/pallas_call | solution.py:370
  44.9 9.9 %collective-permute-done.14.refs_6_ = f32[640,128]{1,0:T(8,128)S(1)} collective-permute-done((f32[640,128]{1,0:T(8,128)S(1)}, f32[640,128]{1,0:T(8,128)S(1)}, u32[]{:S(2)}, u32[]{:S(2)}) %collective-permute-start.14) | collective-permute-done | bytes 327712 | tf_op jit(solution)/shard_map/ppermute | solution.py:288
  54.9 3.1 %shard_map.89 = (f32[8,64,256]{2,1,0:T(8,128)S(1)}, f32[8,64,256]{2,1,0:T(8,128)S(1)}, f32[8,64,256]{2,1,0:T(8,128)S(1)}) custom-call(f32[32,64,128]{2,1,0:T(8,128)S(1)} %get-tuple-element.48.refs_0_, bf16[65,64,128]{2,1,0:T(8,128)(2,1)S(1)} %get-tuple-element.43.refs_1_, bf16[8,256,128]{2,1,0:T(8,128)(2,1)S(1)} %get-tuple-element.49.refs_2_, ...), custom_call_target="tpu_custom_call" | custom-call | flops 268435456 | bytes 4194304 | tf_op jit(solution)/shard_map/pallas_call | solution.py:370
  58.0 1.9 %collective-permute-done.15.received = f32[8,64,256]{2,1,0:T(8,128)S(1)} collective-permute-done((f32[8,64,256]{2,1,0:T(8,128)S(1)}, f32[8,64,256]{2,1,0:T(8,128)S(1)}, u32[]{:S(2)}, u32[]{:S(2)}) %collective-permute-start.15) | collective-permute-done | bytes 524320 | tf_op jit(solution)/shard_map/ppermute | solution.py:273
  60.0 1.5 %collective-permute-start.16 = (f32[2,64,256]{2,1,0:T(8,128)S(1)}, f32[2,64,256]{2,1,0:T(8,128)S(1)}, u32[]{:S(2)}, u32[]{:S(2)}) collective-permute-start(f32[2,64,256]{2,1,0:T(8,128)S(1)} %get-tuple-element.55), channel_id=1, source_target_pairs={{0,8},{4,12},{8,0},{12,4},{16,24},{20,28},{24,16},{28,20},{1,9},{5... | collective-permute-start | bytes 393224 | tf_op jit(solution)/shard_map/ppermute | solution.py:273
  61.5 1.5 %collective-permute-start.17 = (f32[2,64,256]{2,1,0:T(8,128)S(1)}, f32[2,64,256]{2,1,0:T(8,128)S(1)}, u32[]{:S(2)}, u32[]{:S(2)}) collective-permute-start(f32[2,64,256]{2,1,0:T(8,128)S(1)} %get-tuple-element.56), channel_id=1, source_target_pairs={{0,16},{4,20},{8,24},{12,28},{16,0},{20,4},{24,8},{28,12},{1,17},{... | collective-permute-start | bytes 393224 | tf_op jit(solution)/shard_map/ppermute | solution.py:273
  63.6 1.2 %shard_map.90 = f32[8,4,64,64]{3,2,1,0:T(8,128)} custom-call(f32[8,64,256]{2,1,0:T(8,128)S(1)} %get-tuple-element.51.strips), custom_call_target="tpu_custom_call" | custom-call | flops 16777216 | bytes 1048576 | tf_op jit(solution)/shard_map/pallas_call | solution.py:380
  64.7 1.2 %collective-permute-done.16.refs_1_ = f32[2,64,256]{2,1,0:T(8,128)S(1)} collective-permute-done((f32[2,64,256]{2,1,0:T(8,128)S(1)}, f32[2,64,256]{2,1,0:T(8,128)S(1)}, u32[]{:S(2)}, u32[]{:S(2)}) %collective-permute-start.16) | collective-permute-done | bytes 131104 | tf_op jit(solution)/shard_map/ppermute | solution.py:273
  66.0 3.7 %collective-permute-done.17.refs_2_ = f32[2,64,256]{2,1,0:T(8,128)S(1)} collective-permute-done((f32[2,64,256]{2,1,0:T(8,128)S(1)}, f32[2,64,256]{2,1,0:T(8,128)S(1)}, u32[]{:S(2)}, u32[]{:S(2)}) %collective-permute-start.17) | collective-permute-done | bytes 131104 | tf_op jit(solution)/shard_map/ppermute | solution.py:273
  (27 shorter events, 6.6 us)
Async XLA Ops:
  3.8 14.3 %collective-permute-start.10 = (f32[1288,128]{1,0:T(8,128)}, f32[1288,128]{1,0:T(8,128)S(1)}, u32[]{:S(2)}, u32[]{:S(2)}) collective-permute-start(f32[1288,128]{1,0:T(8,128)} %get-tuple-element.41), channel_id=1, source_target_pairs={{1,2},{2,1},{5,6},{6,5},{9,10},{10,9},{13,14},{14,13},{17,18},{18,... | collective-permute-start | bytes 1978376 | tf_op jit(solution)/shard_map/ppermute | solution.py:288
  4.5 14.9 %collective-permute-start = (f32[648,128]{1,0:T(8,128)}, f32[648,128]{1,0:T(8,128)S(1)}, u32[]{:S(2)}, u32[]{:S(2)}) collective-permute-start(f32[648,128]{1,0:T(8,128)} %get-tuple-element.30.refs_8_), channel_id=1, source_target_pairs={{0,1},{1,0},{2,3},{3,2},{4,5},{5,4},{6,7},{7,6},{8,9},{9,8},{10,11... | collective-permute-start | bytes 995336 | tf_op jit(solution)/shard_map/ppermute | solution.py:288
  10.4 14.7 %collective-permute-start.9 = (f32[640,128]{1,0:T(8,128)}, f32[640,128]{1,0:T(8,128)S(1)}, u32[]{:S(2)}, u32[]{:S(2)}) collective-permute-start(f32[640,128]{1,0:T(8,128)} %get-tuple-element.40.refs_9_), channel_id=1, source_target_pairs={{0,1},{1,0},{2,3},{3,2},{4,5},{5,4},{6,7},{7,6},{8,9},{9,8},{10,11... | collective-permute-start | bytes 983048 | tf_op jit(solution)/shard_map/ppermute | solution.py:288
  10.5 5.2 %collective-permute-start.3 = (f32[264,128]{1,0:T(8,128)}, f32[264,128]{1,0:T(8,128)S(1)}, u32[]{:S(2)}, u32[]{:S(2)}) collective-permute-start(f32[264,128]{1,0:T(8,128)} %get-tuple-element.32.refs_0_), channel_id=1, source_target_pairs={{0,8},{4,12},{8,0},{12,4},{16,24},{20,28},{24,16},{28,20},{1,9},{5... | collective-permute-start | bytes 405512 | tf_op jit(solution)/shard_map/ppermute | solution.py:273
  12.0 13.9 %collective-permute-start.5 = (f32[264,128]{1,0:T(8,128)}, f32[264,128]{1,0:T(8,128)S(1)}, u32[]{:S(2)}, u32[]{:S(2)}) collective-permute-start(f32[264,128]{1,0:T(8,128)} %get-tuple-element.32.refs_0_), channel_id=1, source_target_pairs={{0,16},{4,20},{8,24},{12,28},{16,0},{20,4},{24,8},{28,12},{1,17},{... | collective-permute-start | bytes 405512 | tf_op jit(solution)/shard_map/ppermute | solution.py:273
  15.7 10.2 %collective-permute-start.7 = (f32[264,128]{1,0:T(8,128)}, f32[264,128]{1,0:T(8,128)S(1)}, u32[]{:S(2)}, u32[]{:S(2)}) collective-permute-start(f32[264,128]{1,0:T(8,128)} %get-tuple-element.32.refs_0_), channel_id=1, source_target_pairs={{0,24},{4,28},{8,16},{12,20},{16,8},{20,12},{24,0},{28,4},{1,25},{... | collective-permute-start | bytes 405512 | tf_op jit(solution)/shard_map/ppermute | solution.py:273
  18.2 24.4 %collective-permute-start.12 = (f32[1288,128]{1,0:T(8,128)S(1)}, f32[1288,128]{1,0:T(8,128)S(1)}, u32[]{:S(2)}, u32[]{:S(2)}) collective-permute-start(f32[1288,128]{1,0:T(8,128)S(1)} %collective-permute-done.10.refs_12_), channel_id=1, source_target_pairs={{1,0},{2,3},{5,4},{6,7},{9,8},{10,11},{13,12},{14,15},{17,16},{18,... | collective-permute-start | bytes 1978376 | tf_op jit(solution)/shard_map/ppermute | solution.py:288
  19.5 9.6 %collective-permute-start.1 = (f32[648,128]{1,0:T(8,128)S(1)}, f32[648,128]{1,0:T(8,128)S(1)}, u32[]{:S(2)}, u32[]{:S(2)}) collective-permute-start(f32[648,128]{1,0:T(8,128)S(1)} %collective-permute-done.refs_10_), channel_id=1, source_target_pairs={{1,2},{2,1},{5,6},{6,5},{9,10},{10,9},{13,14},{14,13},{17,18},{18,... | collective-permute-start | bytes 995336 | tf_op jit(solution)/shard_map/ppermute | solution.py:288
  25.2 5.2 %collective-permute-start.11 = (f32[640,128]{1,0:T(8,128)S(1)}, f32[640,128]{1,0:T(8,128)S(1)}, u32[]{:S(2)}, u32[]{:S(2)}) collective-permute-start(f32[640,128]{1,0:T(8,128)S(1)} %collective-permute-done.9.refs_11_), channel_id=1, source_target_pairs={{1,2},{2,1},{5,6},{6,5},{9,10},{10,9},{13,14},{14,13},{17,18},{18,... | collective-permute-start | bytes 983048 | tf_op jit(solution)/shard_map/ppermute | solution.py:288
  25.8 1.6 %collective-permute-start.2 = (f32[264,128]{1,0:T(8,128)}, f32[264,128]{1,0:T(8,128)S(1)}, u32[]{:S(2)}, u32[]{:S(2)}) collective-permute-start(f32[264,128]{1,0:T(8,128)} %get-tuple-element.32.refs_0_), channel_id=1, source_target_pairs={{0,4},{4,0},{8,12},{12,8},{16,20},{20,16},{24,28},{28,24},{1,5},{5... | collective-permute-start | bytes 405512 | tf_op jit(solution)/shard_map/ppermute | solution.py:273
  25.9 1.7 %collective-permute-start.4 = (f32[264,128]{1,0:T(8,128)S(1)}, f32[264,128]{1,0:T(8,128)S(1)}, u32[]{:S(2)}, u32[]{:S(2)}) collective-permute-start(f32[264,128]{1,0:T(8,128)S(1)} %collective-permute-done.3.refs_2_), channel_id=1, source_target_pairs={{0,4},{4,0},{8,12},{12,8},{16,20},{20,16},{24,28},{28,24},{1,5},{5... | collective-permute-start | bytes 405512 | tf_op jit(solution)/shard_map/ppermute | solution.py:273
  27.5 1.4 %collective-permute-start.6 = (f32[264,128]{1,0:T(8,128)S(1)}, f32[264,128]{1,0:T(8,128)S(1)}, u32[]{:S(2)}, u32[]{:S(2)}) collective-permute-start(f32[264,128]{1,0:T(8,128)S(1)} %collective-permute-done.5.refs_4_), channel_id=1, source_target_pairs={{0,4},{4,0},{8,12},{12,8},{16,20},{20,16},{24,28},{28,24},{1,5},{5... | collective-permute-start | bytes 405512 | tf_op jit(solution)/shard_map/ppermute | solution.py:273
  27.6 1.4 %collective-permute-start.8 = (f32[264,128]{1,0:T(8,128)S(1)}, f32[264,128]{1,0:T(8,128)S(1)}, u32[]{:S(2)}, u32[]{:S(2)}) collective-permute-start(f32[264,128]{1,0:T(8,128)S(1)} %collective-permute-done.7.refs_6_), channel_id=1, source_target_pairs={{0,4},{4,0},{8,12},{12,8},{16,20},{20,16},{24,28},{28,24},{1,5},{5... | collective-permute-start | bytes 405512 | tf_op jit(solution)/shard_map/ppermute | solution.py:273
  29.0 25.8 %collective-permute-start.13 = (f32[648,128]{1,0:T(8,128)S(1)}, f32[648,128]{1,0:T(8,128)S(1)}, u32[]{:S(2)}, u32[]{:S(2)}) collective-permute-start(f32[648,128]{1,0:T(8,128)S(1)} %collective-permute-done.1.refs_5_), channel_id=1, source_target_pairs={{1,0},{2,3},{5,4},{6,7},{9,8},{10,11},{13,12},{14,15},{17,16},{18,... | collective-permute-start | bytes 995336 | tf_op jit(solution)/shard_map/ppermute | solution.py:288
  30.3 24.5 %collective-permute-start.14 = (f32[640,128]{1,0:T(8,128)S(1)}, f32[640,128]{1,0:T(8,128)S(1)}, u32[]{:S(2)}, u32[]{:S(2)}) collective-permute-start(f32[640,128]{1,0:T(8,128)S(1)} %collective-permute-done.11.refs_6_), channel_id=1, source_target_pairs={{1,0},{2,3},{5,4},{6,7},{9,8},{10,11},{13,12},{14,15},{17,16},{18,... | collective-permute-start | bytes 983048 | tf_op jit(solution)/shard_map/ppermute | solution.py:288
  31.6 1.0 %copy-start = (f32[648,128]{1,0:T(8,128)S(1)}, f32[648,128]{1,0:T(8,128)}, u32[]{:S(2)}) copy-start(f32[648,128]{1,0:T(8,128)} %get-tuple-element.30.refs_8_) | copy-start | bytes 995332
  32.6 1.0 %copy-start.1 = (f32[640,128]{1,0:T(8,128)S(1)}, f32[640,128]{1,0:T(8,128)}, u32[]{:S(2)}) copy-start(f32[640,128]{1,0:T(8,128)} %get-tuple-element.40.refs_9_) | copy-start | bytes 983044
  33.6 0.9 %copy-start.2 = (f32[264,128]{1,0:T(8,128)S(1)}, f32[264,128]{1,0:T(8,128)}, u32[]{:S(2)}) copy-start(f32[264,128]{1,0:T(8,128)} %get-tuple-element.32.refs_0_) | copy-start | bytes 405508
  57.9 2.0 %collective-permute-start.15 = (f32[8,64,256]{2,1,0:T(8,128)S(1)}, f32[8,64,256]{2,1,0:T(8,128)S(1)}, u32[]{:S(2)}, u32[]{:S(2)}) collective-permute-start(f32[8,64,256]{2,1,0:T(8,128)S(1)} %get-tuple-element.53), channel_id=1, source_target_pairs={{0,4},{4,0},{8,12},{12,8},{16,20},{20,16},{24,28},{28,24},{1,5},{5... | collective-permute-start | bytes 1572872 | tf_op jit(solution)/shard_map/ppermute | solution.py:273
  60.0 6.0 %collective-permute-start.16 = (f32[2,64,256]{2,1,0:T(8,128)S(1)}, f32[2,64,256]{2,1,0:T(8,128)S(1)}, u32[]{:S(2)}, u32[]{:S(2)}) collective-permute-start(f32[2,64,256]{2,1,0:T(8,128)S(1)} %get-tuple-element.55), channel_id=1, source_target_pairs={{0,8},{4,12},{8,0},{12,4},{16,24},{20,28},{24,16},{28,20},{1,9},{5... | collective-permute-start | bytes 393224 | tf_op jit(solution)/shard_map/ppermute | solution.py:273
  61.5 8.1 %collective-permute-start.17 = (f32[2,64,256]{2,1,0:T(8,128)S(1)}, f32[2,64,256]{2,1,0:T(8,128)S(1)}, u32[]{:S(2)}, u32[]{:S(2)}) collective-permute-start(f32[2,64,256]{2,1,0:T(8,128)S(1)} %get-tuple-element.56), channel_id=1, source_target_pairs={{0,16},{4,20},{8,24},{12,28},{16,0},{20,4},{24,8},{28,12},{1,17},{... | collective-permute-start | bytes 393224 | tf_op jit(solution)/shard_map/ppermute | solution.py:273
  63.1 6.5 %collective-permute-start.18 = (f32[2,64,256]{2,1,0:T(8,128)S(1)}, f32[2,64,256]{2,1,0:T(8,128)S(1)}, u32[]{:S(2)}, u32[]{:S(2)}) collective-permute-start(f32[2,64,256]{2,1,0:T(8,128)S(1)} %get-tuple-element.57), channel_id=1, source_target_pairs={{0,24},{4,28},{8,16},{12,20},{16,8},{20,12},{24,0},{28,4},{1,25},{... | collective-permute-start | bytes 393224 | tf_op jit(solution)/shard_map/ppermute | solution.py:273

commit v4 on v3

--- a/solution.py
+++ b/solution.py
@@ -76,8 +76,9 @@
         pay[meta : meta + 1, 0:list_len] = rows[...].astype(f32)
         pay[meta + 1 : meta + 2, 0:list_len] = (cols[...] + col_index * fine_cols).astype(f32)
         pay[meta + 2 : meta + 3, 0:1] = count[...].astype(f32)
-        pay[meta + 2 : meta + 3, 1:2] = jnp.full((1, 1), col_index, i32).astype(f32)
         pay[meta + 3 : meta + 4, 0:fine_rows] = goals
+        pay[meta + 3 : meta + 4, fine_rows : fine_rows + 1] = jnp.ones((1, 1), f32)
+        pay[meta + 3 : meta + 4, fine_rows + 1 : fine_rows + 2] = jnp.full((1, 1), col_index, i32).astype(f32)
     copies[-2].wait()
     for block in range(half):
         both = jnp.concatenate([low_tiles[block, 0], low_tiles[block + half, 0]], axis=1)
@@ -124,7 +125,7 @@
                 for slot in (group * GROUP + p, group * GROUP + p + half):
                     fine = meta[1, slot].astype(i32)
                     shard, within = divide(fine, fine_rows)
-                    target = ids[shard ^ row_index, 0, within].astype(i32)
+                    target = ids[shard ^ row_index, within].astype(i32)
                     live = jnp.logical_and(slot < count, target >= 0)
                     rights.append(panel[jnp.where(live, fine, fine_total)])
                     places.append(jnp.where(live, meta[0, slot].astype(i32) * coarse_cols + target, 0))
@@ -145,28 +146,29 @@
     if first:
         r_pays = take(n_panel)
     else:
-        acc_in, panel, weights_in, ids_in, metas_in = take(5)
+        acc_in, panel, weights_in, ids_in, goals_in = take(5)
     pays = [take(n) for n in parts]
     if last:
         strips, keep, send = take(3)
-        acc, weights, part, goals = take(4)
+        acc, weights, part, places = take(4)
     elif first:
-        acc, weights, metas_out, panel, ids_out = take(5)
+        acc, weights, goals_out, panel, ids_in = take(5)
     else:
-        acc, weights, metas_out = take(3)
-    ids, metas, sems = take(3)
+        acc, weights, goals_out = take(3)
+    ids, metas, goals, sems = take(4)
     half, quarter = GROUP // 2, fine_rows // 2
-    n_all = n_prev + len(pays)
     row_index = lax.axis_index("row")
     eighth = quarter // 2
     meta_at = (half + eighth) * tile
     high_base = (list_len - GROUP) // 2 * tile
 
-    moves = [(pay[0].at[pl.ds(meta_at, META)], metas.at[n_prev + i]) for i, pay in enumerate(pays)]
     if first:
-        moves += [(pay.at[pl.ds(quarter * tile, META)], ids.at[m]) for m, pay in enumerate(r_pays)]
-    else:
-        moves += [(ids_in, ids), (metas_in, metas.at[pl.ds(0, n_prev)])]
+        for m, pay in enumerate(r_pays):
+            ids_in[m : m + 1, :] = pay[quarter * tile : quarter * tile + 1, :]
+    moves = [(ids_in, ids)]
+    moves += [(pay[0].at[pl.ds(meta_at, META)], metas.at[i]) for i, pay in enumerate(pays)]
+    if last:
+        moves += [(goals_in, goals)]
     copies = [pltpu.make_async_copy(src, dst, sems.at[i]) for i, (src, dst) in enumerate(moves)]
     for copy in copies:
         copy.start()
@@ -177,24 +179,23 @@
             at = (row_index ^ m) * fine_rows
             for k in range(quarter):
                 panel[at + k], panel[at + k + quarter] = halves(pay[k * tile : (k + 1) * tile, :])
-            ids_out[m] = pay[quarter * tile : quarter * tile + META, :]
     else:
         acc[...] = acc_in[...]
         weights[...] = weights_in[...]
     if not last:
-        if n_prev:
-            metas_out[:n_prev] = metas_in[...]
+        if not first:
+            goals_out[...] = goals_in[...]
         for i, pay in enumerate(pays):
-            metas_out[n_prev + i] = pay[0][meta_at : meta_at + META, :]
+            goals_out[n_prev + i : n_prev + i + 1, :] = pay[0][meta_at + 3 : meta_at + 4, :]
     for copy in copies:
         copy.wait()
 
     for i, pay in enumerate(pays):
-        meta = metas.at[n_prev + i]
-
-        @pl.when(meta[2, 0] > 0)
+        meta = metas.at[i]
+
+        @pl.when(meta[3, fine_rows] > 0)
         def _(pay=pay, meta=meta):
-            at = pl.multiple_of(meta[2, 1].astype(i32) * tile, tile)
+            at = pl.multiple_of(meta[3, fine_rows + 1].astype(i32) * tile, tile)
             for k in range(quarter):
                 if k < eighth:
                     block = pay[0][(half + k) * tile : (half + k + 1) * tile, :]
@@ -211,16 +212,16 @@
 
     dump = part.shape[0] - 1
     n_chips = keep.shape[0] // owned
-    for i in range(n_all):
-
-        @pl.when(metas[i, 2, 0] > 0)
-        def _(i=i):
-            source = metas[i, 2, 1].astype(i32)
+    for read in [goals.at[i] for i in range(n_prev)] + [metas.at[i, 3] for i in range(len(pays))]:
+
+        @pl.when(read[fine_rows] > 0)
+        def _(read=read):
+            source = read[fine_rows + 1].astype(i32)
             for k in range(fine_rows):
-                goal = metas[i, 3, k].astype(i32)
+                goal = read[k].astype(i32)
                 owner, within = divide(jnp.maximum(goal, 0), owned)
                 chip, core = divide(owner ^ row_index, 2)
-                goals[source, k] = jnp.where(goal >= 0, (core * n_chips + chip) * owned + within, dump)
+                places[source, k] = jnp.where(goal >= 0, (core * n_chips + chip) * owned + within, dump)
 
     part[...] = jnp.zeros_like(part)
     n_sources = weights.shape[1] // tile
@@ -239,7 +240,7 @@
         wide = weights[k]
         terms = jnp.dot(jnp.concatenate([wide, wide], axis=1), right, preferred_element_type=f32)
         for source in range(n_sources):
-            part[goals[source, k]] += terms[source * tile : (source + 1) * tile]
+            part[places[source, k]] += terms[source * tile : (source + 1) * tile]
     keep[...] = part[: n_chips * owned]
     send[...] = part[n_chips * owned : 2 * n_chips * owned]
 
@@ -341,20 +342,22 @@
 
     split_chain = list(zip(line_gather(low, False, panel_pays), line_gather(high, False)))
     whole_chain = [(x,) for x in line_gather(whole, True)]
+    n_ids, n_goals = (-(-n // META) * META for n in (row_count, 2 * col_count))
+
     def stage(first, last, n_prev, state, pays):
-        n_all = n_prev + len(pays)
         out = [
             shape(fine_rows * coarse_cols, tile, 2 * tile),
             shape(fine_rows, col_count * tile, 2 * tile, dtype=bf16),
-            shape(n_all, META, 2 * tile),
+            shape(n_goals, 2 * tile),
         ]
         scratch = [
-            pltpu.SMEM((row_count, META, 2 * tile), f32),
-            pltpu.SMEM((n_all, META, 2 * tile), f32),
-            pltpu.SemaphoreType.DMA((row_count + n_all + 2,)),
+            pltpu.SMEM((n_ids, 2 * tile), f32),
+            pltpu.SMEM((len(pays), META, 2 * tile), f32),
+            pltpu.SMEM((n_goals, 2 * tile), f32),
+            pltpu.SemaphoreType.DMA((len(pays) + 2,)),
         ]
         if first:
-            out += [shape(fine_total + 1, tile, 2 * tile, dtype=bf16), shape(row_count, META, 2 * tile)]
+            out += [shape(fine_total + 1, tile, 2 * tile, dtype=bf16), shape(n_ids, 2 * tile)]
         if last:
             spread = n_chips * owned
             scratch = [
@@ -372,9 +375,9 @@
     early = [(low, high)] + split_chain[:1] + whole_chain[:1]
     middle = split_chain[1:-1] + whole_chain[1:]
     late = split_chain[-1:]
-    acc, weights, metas, panel, ids = stage(True, False, 0, panel_pays, early)
-    acc, weights, metas = stage(False, False, len(early), (acc, panel, weights, ids, metas), middle)
-    strips, keep, send = stage(False, True, len(early + middle), (acc, panel, weights, ids, metas), late)
+    acc, weights, goals, panel, ids = stage(True, False, 0, panel_pays, early)
+    acc, weights, goals = stage(False, False, len(early), (acc, panel, weights, ids, goals), middle)
+    strips, keep, send = stage(False, True, len(early + middle), (acc, panel, weights, ids, goals), late)
 
     received = swap(send, "row", 1)
     product = call(

time: 70.8 us -> 69.9 us (0.987)
  Pallas kernels: 12.7 us -> 10.1 us
  waiting for transfers between devices: 31.4 us -> 33.2 us
    pallas_call x3, Pallas kernels: 8.1 us -> 5.55 us  [stage(): call(kernel, tuple(out), len(operands), scratch, flops=2 ** 28, nbytes=4...]
    ppermute x8, waiting for transfers between devices: 20.4 us -> 22 us  [line_gather(): own = lax.ppermute(own, 'col', pairs)]
  transfers between devices with their start and end apart: 19 -> 19, of which waited for: 10 -> 11; matrix products, arithmetic and copies ran while one was open for 0% -> 0% of each run, Pallas kernels for 9% -> 7%
where the time goes in v4:
time: 69.9 us; the launch traced here: 69.6 us
  waiting for transfers between devices  33.2 us (47%)
  starting transfers between devices  22 us (31%)
  Pallas kernels  10.1 us (14%)
  local copies, waits for them, and re-layouts  2.84 us (4%)
  between operations  1.43 us (2%)
    ppermute x8, waiting for transfers between devices, line_gather(): own = lax.ppermute(own, 'col', pairs)  22 us
    ppermute x8, starting transfers between devices, line_gather(): own = lax.ppermute(own, 'col', pairs)  11.9 us
    ppermute x11, waiting for transfers between devices, swap(): return lax.ppermute(x, axis, [(i, i ^ mask) for i in range(n)])  11.2 us
    ppermute x11, starting transfers between devices, swap(): return lax.ppermute(x, axis, [(i, i ^ mask) for i in range(n)])  10.2 us
    pallas_call x3, Pallas kernels, stage(): call(kernel, tuple(out), len(operands), scratch, flops=2 ** 28, nbytes=4...  5.55 us
    unnamed x6, local copies, waits for them, and re-layouts  2.84 us
    pallas_call x1, Pallas kernels, shards(): call(functools.partial(pack, fine_cols, coarse_cols), (shape(z_rows, 2 *...  2.54 us
  transfers between devices with their start and end apart: 19, of which 11 were waited for; matrix products, arithmetic and copies ran while one was open for 0% of the time, Pallas kernels for 7%

profile of v4, /device:TPU:0, one launch (start us, length us, event | category | flops | bytes accessed | tf_op | source)
XLA Modules:
  0.0 69.6 jit_solution(10305937028340324453)
XLA Ops:
  1.3 2.5 %shard_map.86 = (f32[1288,128]{1,0:T(8,128)}, f32[648,128]{1,0:T(8,128)}, f32[640,128]{1,0:T(8,128)}, f32[264,128]{1,0:T(8,128)}) custom-call(f32[32,1,64,64]{3,2,1,0:T(8,128)} %op.1, f32[8,1,64,64]{3,2,1,0:T(8,128)} %pro.1, s32[1,32]{1,0:T(1,128)} %bitcast.4, s32[1,32]{1,0:T(1,128)} %bitcast.5, s32[1,1]{1,0:T(1,128)S(6)} %copy.9.count, s32[1,8]{1,0:T(1,128)} %bitcast.6, ...), custom_call_target="tpu_custom_call" | custom-call | bytes 4194304 | tf_op jit(solution)/shard_map/pallas_call | solution.py:312
  4.5 5.9 %collective-permute-start = (f32[648,128]{1,0:T(8,128)}, f32[648,128]{1,0:T(8,128)S(1)}, u32[]{:S(2)}, u32[]{:S(2)}) collective-permute-start(f32[648,128]{1,0:T(8,128)} %get-tuple-element.30.refs_8_), channel_id=1, source_target_pairs={{0,1},{1,0},{2,3},{3,2},{4,5},{5,4},{6,7},{7,6},{8,9},{9,8},{10,11... | collective-permute-start | bytes 995336 | tf_op jit(solution)/shard_map/ppermute | solution.py:289
  10.5 1.5 %collective-permute-start.3 = (f32[264,128]{1,0:T(8,128)}, f32[264,128]{1,0:T(8,128)S(1)}, u32[]{:S(2)}, u32[]{:S(2)}) collective-permute-start(f32[264,128]{1,0:T(8,128)} %get-tuple-element.32.refs_0_), channel_id=1, source_target_pairs={{0,8},{4,12},{8,0},{12,4},{16,24},{20,28},{24,16},{28,20},{1,9},{5... | collective-permute-start | bytes 405512 | tf_op jit(solution)/shard_map/ppermute | solution.py:274
  12.0 1.5 %collective-permute-start.5 = (f32[264,128]{1,0:T(8,128)}, f32[264,128]{1,0:T(8,128)S(1)}, u32[]{:S(2)}, u32[]{:S(2)}) collective-permute-start(f32[264,128]{1,0:T(8,128)} %get-tuple-element.32.refs_0_), channel_id=1, source_target_pairs={{0,16},{4,20},{8,24},{12,28},{16,0},{20,4},{24,8},{28,12},{1,17},{... | collective-permute-start | bytes 405512 | tf_op jit(solution)/shard_map/ppermute | solution.py:274
  13.5 2.2 %collective-permute-done.3.refs_2_ = f32[264,128]{1,0:T(8,128)S(1)} collective-permute-done((f32[264,128]{1,0:T(8,128)}, f32[264,128]{1,0:T(8,128)S(1)}, u32[]{:S(2)}, u32[]{:S(2)}) %collective-permute-start.3) | collective-permute-done | bytes 135200 | tf_op jit(solution)/shard_map/ppermute | solution.py:274
  15.7 2.4 %collective-permute-start.7 = (f32[264,128]{1,0:T(8,128)}, f32[264,128]{1,0:T(8,128)S(1)}, u32[]{:S(2)}, u32[]{:S(2)}) collective-permute-start(f32[264,128]{1,0:T(8,128)} %get-tuple-element.32.refs_0_), channel_id=1, source_target_pairs={{0,24},{4,28},{8,16},{12,20},{16,8},{20,12},{24,0},{28,4},{1,25},{... | collective-permute-start | bytes 405512 | tf_op jit(solution)/shard_map/ppermute | solution.py:274
  18.2 1.3 %collective-permute-start.12 = (f32[1288,128]{1,0:T(8,128)S(1)}, f32[1288,128]{1,0:T(8,128)S(1)}, u32[]{:S(2)}, u32[]{:S(2)}) collective-permute-start(f32[1288,128]{1,0:T(8,128)S(1)} %collective-permute-done.10.refs_12_), channel_id=1, source_target_pairs={{1,0},{2,3},{5,4},{6,7},{9,8},{10,11},{13,12},{14,15},{17,16},{18,... | collective-permute-start | bytes 1978376 | tf_op jit(solution)/shard_map/ppermute | solution.py:289
  20.1 5.0 %collective-permute-done.9.refs_11_ = f32[640,128]{1,0:T(8,128)S(1)} collective-permute-done((f32[640,128]{1,0:T(8,128)}, f32[640,128]{1,0:T(8,128)S(1)}, u32[]{:S(2)}, u32[]{:S(2)}) %collective-permute-start.9) | collective-permute-done | bytes 327712 | tf_op jit(solution)/shard_map/ppermute | solution.py:289
  26.4 1.1 %collective-permute-done.2.refs_1_ = f32[264,128]{1,0:T(8,128)S(1)} collective-permute-done((f32[264,128]{1,0:T(8,128)}, f32[264,128]{1,0:T(8,128)S(1)}, u32[]{:S(2)}, u32[]{:S(2)}) %collective-permute-start.2) | collective-permute-done | bytes 135200 | tf_op jit(solution)/shard_map/ppermute | solution.py:274
  29.0 1.3 %collective-permute-start.13 = (f32[648,128]{1,0:T(8,128)S(1)}, f32[648,128]{1,0:T(8,128)S(1)}, u32[]{:S(2)}, u32[]{:S(2)}) collective-permute-start(f32[648,128]{1,0:T(8,128)S(1)} %collective-permute-done.1.refs_5_), channel_id=1, source_target_pairs={{1,0},{2,3},{5,4},{6,7},{9,8},{10,11},{13,12},{14,15},{17,16},{18,... | collective-permute-start | bytes 995336 | tf_op jit(solution)/shard_map/ppermute | solution.py:289
  30.3 1.3 %collective-permute-start.14 = (f32[640,128]{1,0:T(8,128)S(1)}, f32[640,128]{1,0:T(8,128)S(1)}, u32[]{:S(2)}, u32[]{:S(2)}) collective-permute-start(f32[640,128]{1,0:T(8,128)S(1)} %collective-permute-done.11.refs_6_), channel_id=1, source_target_pairs={{1,0},{2,3},{5,4},{6,7},{9,8},{10,11},{13,12},{14,15},{17,16},{18,... | collective-permute-start | bytes 983048 | tf_op jit(solution)/shard_map/ppermute | solution.py:289
  32.6 1.0 %copy-done.1 = f32[640,128]{1,0:T(8,128)S(1)} copy-done((f32[640,128]{1,0:T(8,128)S(1)}, f32[640,128]{1,0:T(8,128)}, u32[]{:S(2)}) %copy-start.1) | copy-done | bytes 327704
  34.5 2.1 %shard_map.87 = (f32[32,64,128]{2,1,0:T(8,128)S(1)}, bf16[8,256,128]{2,1,0:T(8,128)(2,1)S(1)}, f32[8,128]{1,0:T(8,128)S(1)}, bf16[65,64,128]{2,1,0:T(8,128)(2,1)S(1)}, f32[8,128]{1,0:T(8,128)S(1)}) custom-call(f32[264,128]{1,0:T(8,128)S(1)} %copy-done.2, f32[264,128]{1,0:T(8,128)S(1)} %collective-permute-done.2.refs_1_, ...), custom_call_target="tpu_custom_call" | custom-call | flops 268435456 | bytes 4194304 | tf_op jit(solution)/shard_map/pallas_call | solution.py:373
  36.6 5.9 %collective-permute-done.12.refs_7_ = f32[1288,128]{1,0:T(8,128)S(1)} collective-permute-done((f32[1288,128]{1,0:T(8,128)S(1)}, f32[1288,128]{1,0:T(8,128)S(1)}, u32[]{:S(2)}, u32[]{:S(2)}) %collective-permute-start.12) | collective-permute-done | bytes 659488 | tf_op jit(solution)/shard_map/ppermute | solution.py:289
  42.5 1.3 %shard_map.88 = (f32[32,64,128]{2,1,0:T(8,128)S(1)}, bf16[8,256,128]{2,1,0:T(8,128)(2,1)S(1)}, f32[8,128]{1,0:T(8,128)S(1)}) custom-call(f32[32,64,128]{2,1,0:T(8,128)S(1)} %get-tuple-element.42.refs_0_, bf16[65,64,128]{2,1,0:T(8,128)(2,1)S(1)} %get-tuple-element.43.refs_1_, bf16[8,256,128]{2,1,0:T(8,128)(2,1)S(1)} %get-tuple-element.44.refs_2_, ...), custom_call_target="tpu_custom_call" | custom-call | flops 268435456 | bytes 4194304 | tf_op jit(solution)/shard_map/pallas_call | solution.py:373
  43.8 11.1 %collective-permute-done.14.refs_6_ = f32[640,128]{1,0:T(8,128)S(1)} collective-permute-done((f32[640,128]{1,0:T(8,128)S(1)}, f32[640,128]{1,0:T(8,128)S(1)}, u32[]{:S(2)}, u32[]{:S(2)}) %collective-permute-start.14) | collective-permute-done | bytes 327712 | tf_op jit(solution)/shard_map/ppermute | solution.py:289
  54.9 2.2 %shard_map.89 = (f32[8,64,256]{2,1,0:T(8,128)S(1)}, f32[8,64,256]{2,1,0:T(8,128)S(1)}, f32[8,64,256]{2,1,0:T(8,128)S(1)}) custom-call(f32[32,64,128]{2,1,0:T(8,128)S(1)} %get-tuple-element.48.refs_0_, bf16[65,64,128]{2,1,0:T(8,128)(2,1)S(1)} %get-tuple-element.43.refs_1_, bf16[8,256,128]{2,1,0:T(8,128)(2,1)S(1)} %get-tuple-element.49.refs_2_, ...), custom_call_target="tpu_custom_call" | custom-call | flops 268435456 | bytes 4194304 | tf_op jit(solution)/shard_map/pallas_call | solution.py:373
  57.1 1.9 %collective-permute-done.15.received = f32[8,64,256]{2,1,0:T(8,128)S(1)} collective-permute-done((f32[8,64,256]{2,1,0:T(8,128)S(1)}, f32[8,64,256]{2,1,0:T(8,128)S(1)}, u32[]{:S(2)}, u32[]{:S(2)}) %collective-permute-start.15) | collective-permute-done | bytes 524320 | tf_op jit(solution)/shard_map/ppermute | solution.py:274
  59.1 1.6 %collective-permute-start.16 = (f32[2,64,256]{2,1,0:T(8,128)S(1)}, f32[2,64,256]{2,1,0:T(8,128)S(1)}, u32[]{:S(2)}, u32[]{:S(2)}) collective-permute-start(f32[2,64,256]{2,1,0:T(8,128)S(1)} %get-tuple-element.55), channel_id=1, source_target_pairs={{0,8},{4,12},{8,0},{12,4},{16,24},{20,28},{24,16},{28,20},{1,9},{5... | collective-permute-start | bytes 393224 | tf_op jit(solution)/shard_map/ppermute | solution.py:274
  60.7 1.5 %collective-permute-start.17 = (f32[2,64,256]{2,1,0:T(8,128)S(1)}, f32[2,64,256]{2,1,0:T(8,128)S(1)}, u32[]{:S(2)}, u32[]{:S(2)}) collective-permute-start(f32[2,64,256]{2,1,0:T(8,128)S(1)} %get-tuple-element.56), channel_id=1, source_target_pairs={{0,16},{4,20},{8,24},{12,28},{16,0},{20,4},{24,8},{28,12},{1,17},{... | collective-permute-start | bytes 393224 | tf_op jit(solution)/shard_map/ppermute | solution.py:274
  62.6 1.2 %shard_map.90 = f32[8,4,64,64]{3,2,1,0:T(8,128)} custom-call(f32[8,64,256]{2,1,0:T(8,128)S(1)} %get-tuple-element.51.strips), custom_call_target="tpu_custom_call" | custom-call | flops 16777216 | bytes 1048576 | tf_op jit(solution)/shard_map/pallas_call | solution.py:383
  63.8 1.2 %collective-permute-done.16.refs_1_ = f32[2,64,256]{2,1,0:T(8,128)S(1)} collective-permute-done((f32[2,64,256]{2,1,0:T(8,128)S(1)}, f32[2,64,256]{2,1,0:T(8,128)S(1)}, u32[]{:S(2)}, u32[]{:S(2)}) %collective-permute-start.16) | collective-permute-done | bytes 131104 | tf_op jit(solution)/shard_map/ppermute | solution.py:274
  65.0 2.7 %collective-permute-done.17.refs_2_ = f32[2,64,256]{2,1,0:T(8,128)S(1)} collective-permute-done((f32[2,64,256]{2,1,0:T(8,128)S(1)}, f32[2,64,256]{2,1,0:T(8,128)S(1)}, u32[]{:S(2)}, u32[]{:S(2)}) %collective-permute-start.17) | collective-permute-done | bytes 131104 | tf_op jit(solution)/shard_map/ppermute | solution.py:274
  67.7 1.1 %collective-permute-done.18.refs_3_ = f32[2,64,256]{2,1,0:T(8,128)S(1)} collective-permute-done((f32[2,64,256]{2,1,0:T(8,128)S(1)}, f32[2,64,256]{2,1,0:T(8,128)S(1)}, u32[]{:S(2)}, u32[]{:S(2)}) %collective-permute-start.18) | collective-permute-done | bytes 131104 | tf_op jit(solution)/shard_map/ppermute | solution.py:274
  (27 shorter events, 7.6 us)
Async XLA Ops:
  3.8 14.3 %collective-permute-start.10 = (f32[1288,128]{1,0:T(8,128)}, f32[1288,128]{1,0:T(8,128)S(1)}, u32[]{:S(2)}, u32[]{:S(2)}) collective-permute-start(f32[1288,128]{1,0:T(8,128)} %get-tuple-element.41), channel_id=1, source_target_pairs={{1,2},{2,1},{5,6},{6,5},{9,10},{10,9},{13,14},{14,13},{17,18},{18,... | collective-permute-start | bytes 1978376 | tf_op jit(solution)/shard_map/ppermute | solution.py:289
  4.5 14.9 %collective-permute-start = (f32[648,128]{1,0:T(8,128)}, f32[648,128]{1,0:T(8,128)S(1)}, u32[]{:S(2)}, u32[]{:S(2)}) collective-permute-start(f32[648,128]{1,0:T(8,128)} %get-tuple-element.30.refs_8_), channel_id=1, source_target_pairs={{0,1},{1,0},{2,3},{3,2},{4,5},{5,4},{6,7},{7,6},{8,9},{9,8},{10,11... | collective-permute-start | bytes 995336 | tf_op jit(solution)/shard_map/ppermute | solution.py:289
  10.4 14.7 %collective-permute-start.9 = (f32[640,128]{1,0:T(8,128)}, f32[640,128]{1,0:T(8,128)S(1)}, u32[]{:S(2)}, u32[]{:S(2)}) collective-permute-start(f32[640,128]{1,0:T(8,128)} %get-tuple-element.40.refs_9_), channel_id=1, source_target_pairs={{0,1},{1,0},{2,3},{3,2},{4,5},{5,4},{6,7},{7,6},{8,9},{9,8},{10,11... | collective-permute-start | bytes 983048 | tf_op jit(solution)/shard_map/ppermute | solution.py:289
  10.5 5.2 %collective-permute-start.3 = (f32[264,128]{1,0:T(8,128)}, f32[264,128]{1,0:T(8,128)S(1)}, u32[]{:S(2)}, u32[]{:S(2)}) collective-permute-start(f32[264,128]{1,0:T(8,128)} %get-tuple-element.32.refs_0_), channel_id=1, source_target_pairs={{0,8},{4,12},{8,0},{12,4},{16,24},{20,28},{24,16},{28,20},{1,9},{5... | collective-permute-start | bytes 405512 | tf_op jit(solution)/shard_map/ppermute | solution.py:274
  12.0 13.9 %collective-permute-start.5 = (f32[264,128]{1,0:T(8,128)}, f32[264,128]{1,0:T(8,128)S(1)}, u32[]{:S(2)}, u32[]{:S(2)}) collective-permute-start(f32[264,128]{1,0:T(8,128)} %get-tuple-element.32.refs_0_), channel_id=1, source_target_pairs={{0,16},{4,20},{8,24},{12,28},{16,0},{20,4},{24,8},{28,12},{1,17},{... | collective-permute-start | bytes 405512 | tf_op jit(solution)/shard_map/ppermute | solution.py:274
  15.7 10.2 %collective-permute-start.7 = (f32[264,128]{1,0:T(8,128)}, f32[264,128]{1,0:T(8,128)S(1)}, u32[]{:S(2)}, u32[]{:S(2)}) collective-permute-start(f32[264,128]{1,0:T(8,128)} %get-tuple-element.32.refs_0_), channel_id=1, source_target_pairs={{0,24},{4,28},{8,16},{12,20},{16,8},{20,12},{24,0},{28,4},{1,25},{... | collective-permute-start | bytes 405512 | tf_op jit(solution)/shard_map/ppermute | solution.py:274
  18.2 24.4 %collective-permute-start.12 = (f32[1288,128]{1,0:T(8,128)S(1)}, f32[1288,128]{1,0:T(8,128)S(1)}, u32[]{:S(2)}, u32[]{:S(2)}) collective-permute-start(f32[1288,128]{1,0:T(8,128)S(1)} %collective-permute-done.10.refs_12_), channel_id=1, source_target_pairs={{1,0},{2,3},{5,4},{6,7},{9,8},{10,11},{13,12},{14,15},{17,16},{18,... | collective-permute-start | bytes 1978376 | tf_op jit(solution)/shard_map/ppermute | solution.py:289
  19.5 9.6 %collective-permute-start.1 = (f32[648,128]{1,0:T(8,128)S(1)}, f32[648,128]{1,0:T(8,128)S(1)}, u32[]{:S(2)}, u32[]{:S(2)}) collective-permute-start(f32[648,128]{1,0:T(8,128)S(1)} %collective-permute-done.refs_10_), channel_id=1, source_target_pairs={{1,2},{2,1},{5,6},{6,5},{9,10},{10,9},{13,14},{14,13},{17,18},{18,... | collective-permute-start | bytes 995336 | tf_op jit(solution)/shard_map/ppermute | solution.py:289
  25.2 5.2 %collective-permute-start.11 = (f32[640,128]{1,0:T(8,128)S(1)}, f32[640,128]{1,0:T(8,128)S(1)}, u32[]{:S(2)}, u32[]{:S(2)}) collective-permute-start(f32[640,128]{1,0:T(8,128)S(1)} %collective-permute-done.9.refs_11_), channel_id=1, source_target_pairs={{1,2},{2,1},{5,6},{6,5},{9,10},{10,9},{13,14},{14,13},{17,18},{18,... | collective-permute-start | bytes 983048 | tf_op jit(solution)/shard_map/ppermute | solution.py:289
  25.8 1.6 %collective-permute-start.2 = (f32[264,128]{1,0:T(8,128)}, f32[264,128]{1,0:T(8,128)S(1)}, u32[]{:S(2)}, u32[]{:S(2)}) collective-permute-start(f32[264,128]{1,0:T(8,128)} %get-tuple-element.32.refs_0_), channel_id=1, source_target_pairs={{0,4},{4,0},{8,12},{12,8},{16,20},{20,16},{24,28},{28,24},{1,5},{5... | collective-permute-start | bytes 405512 | tf_op jit(solution)/shard_map/ppermute | solution.py:274
  25.9 1.7 %collective-permute-start.4 = (f32[264,128]{1,0:T(8,128)S(1)}, f32[264,128]{1,0:T(8,128)S(1)}, u32[]{:S(2)}, u32[]{:S(2)}) collective-permute-start(f32[264,128]{1,0:T(8,128)S(1)} %collective-permute-done.3.refs_2_), channel_id=1, source_target_pairs={{0,4},{4,0},{8,12},{12,8},{16,20},{20,16},{24,28},{28,24},{1,5},{5... | collective-permute-start | bytes 405512 | tf_op jit(solution)/shard_map/ppermute | solution.py:274
  27.5 1.4 %collective-permute-start.6 = (f32[264,128]{1,0:T(8,128)S(1)}, f32[264,128]{1,0:T(8,128)S(1)}, u32[]{:S(2)}, u32[]{:S(2)}) collective-permute-start(f32[264,128]{1,0:T(8,128)S(1)} %collective-permute-done.5.refs_4_), channel_id=1, source_target_pairs={{0,4},{4,0},{8,12},{12,8},{16,20},{20,16},{24,28},{28,24},{1,5},{5... | collective-permute-start | bytes 405512 | tf_op jit(solution)/shard_map/ppermute | solution.py:274
  27.6 1.4 %collective-permute-start.8 = (f32[264,128]{1,0:T(8,128)S(1)}, f32[264,128]{1,0:T(8,128)S(1)}, u32[]{:S(2)}, u32[]{:S(2)}) collective-permute-start(f32[264,128]{1,0:T(8,128)S(1)} %collective-permute-done.7.refs_6_), channel_id=1, source_target_pairs={{0,4},{4,0},{8,12},{12,8},{16,20},{20,16},{24,28},{28,24},{1,5},{5... | collective-permute-start | bytes 405512 | tf_op jit(solution)/shard_map/ppermute | solution.py:274
  29.0 25.8 %collective-permute-start.13 = (f32[648,128]{1,0:T(8,128)S(1)}, f32[648,128]{1,0:T(8,128)S(1)}, u32[]{:S(2)}, u32[]{:S(2)}) collective-permute-start(f32[648,128]{1,0:T(8,128)S(1)} %collective-permute-done.1.refs_5_), channel_id=1, source_target_pairs={{1,0},{2,3},{5,4},{6,7},{9,8},{10,11},{13,12},{14,15},{17,16},{18,... | collective-permute-start | bytes 995336 | tf_op jit(solution)/shard_map/ppermute | solution.py:289
  30.3 24.5 %collective-permute-start.14 = (f32[640,128]{1,0:T(8,128)S(1)}, f32[640,128]{1,0:T(8,128)S(1)}, u32[]{:S(2)}, u32[]{:S(2)}) collective-permute-start(f32[640,128]{1,0:T(8,128)S(1)} %collective-permute-done.11.refs_6_), channel_id=1, source_target_pairs={{1,0},{2,3},{5,4},{6,7},{9,8},{10,11},{13,12},{14,15},{17,16},{18,... | collective-permute-start | bytes 983048 | tf_op jit(solution)/shard_map/ppermute | solution.py:289
  31.6 1.0 %copy-start = (f32[648,128]{1,0:T(8,128)S(1)}, f32[648,128]{1,0:T(8,128)}, u32[]{:S(2)}) copy-start(f32[648,128]{1,0:T(8,128)} %get-tuple-element.30.refs_8_) | copy-start | bytes 995332
  32.6 1.0 %copy-start.1 = (f32[640,128]{1,0:T(8,128)S(1)}, f32[640,128]{1,0:T(8,128)}, u32[]{:S(2)}) copy-start(f32[640,128]{1,0:T(8,128)} %get-tuple-element.40.refs_9_) | copy-start | bytes 983044
  33.6 0.9 %copy-start.2 = (f32[264,128]{1,0:T(8,128)S(1)}, f32[264,128]{1,0:T(8,128)}, u32[]{:S(2)}) copy-start(f32[264,128]{1,0:T(8,128)} %get-tuple-element.32.refs_0_) | copy-start | bytes 405508
  57.1 2.0 %collective-permute-start.15 = (f32[8,64,256]{2,1,0:T(8,128)S(1)}, f32[8,64,256]{2,1,0:T(8,128)S(1)}, u32[]{:S(2)}, u32[]{:S(2)}) collective-permute-start(f32[8,64,256]{2,1,0:T(8,128)S(1)} %get-tuple-element.53), channel_id=1, source_target_pairs={{0,4},{4,0},{8,12},{12,8},{16,20},{20,16},{24,28},{28,24},{1,5},{5... | collective-permute-start | bytes 1572872 | tf_op jit(solution)/shard_map/ppermute | solution.py:274
  59.1 5.9 %collective-permute-start.16 = (f32[2,64,256]{2,1,0:T(8,128)S(1)}, f32[2,64,256]{2,1,0:T(8,128)S(1)}, u32[]{:S(2)}, u32[]{:S(2)}) collective-permute-start(f32[2,64,256]{2,1,0:T(8,128)S(1)} %get-tuple-element.55), channel_id=1, source_target_pairs={{0,8},{4,12},{8,0},{12,4},{16,24},{20,28},{24,16},{28,20},{1,9},{5... | collective-permute-start | bytes 393224 | tf_op jit(solution)/shard_map/ppermute | solution.py:274
  60.7 7.1 %collective-permute-start.17 = (f32[2,64,256]{2,1,0:T(8,128)S(1)}, f32[2,64,256]{2,1,0:T(8,128)S(1)}, u32[]{:S(2)}, u32[]{:S(2)}) collective-permute-start(f32[2,64,256]{2,1,0:T(8,128)S(1)} %get-tuple-element.56), channel_id=1, source_target_pairs={{0,16},{4,20},{8,24},{12,28},{16,0},{20,4},{24,8},{28,12},{1,17},{... | collective-permute-start | bytes 393224 | tf_op jit(solution)/shard_map/ppermute | solution.py:274
  62.2 6.6 %collective-permute-start.18 = (f32[2,64,256]{2,1,0:T(8,128)S(1)}, f32[2,64,256]{2,1,0:T(8,128)S(1)}, u32[]{:S(2)}, u32[]{:S(2)}) collective-permute-start(f32[2,64,256]{2,1,0:T(8,128)S(1)} %get-tuple-element.57), channel_id=1, source_target_pairs={{0,24},{4,28},{8,16},{12,20},{16,8},{20,12},{24,0},{28,4},{1,25},{... | collective-permute-start | bytes 393224 | tf_op jit(solution)/shard_map/ppermute | solution.py:274

commit v5 on v4

--- a/solution.py
+++ b/solution.py
@@ -40,7 +40,7 @@
     return lax.shift_right_logical(x, n.bit_length() - 1), x & (n - 1)
 
 
-def pack(fine_cols, coarse_cols, op, pro, rows, cols, count, pro_cols, pro_live, whole, low, high, r_pay, *scratch):
+def pack(fine_cols, coarse_cols, op, pro, rows, cols, count, pro_cols, pro_live, low, high, r_pay, *scratch):
     sems = scratch[-1]
     sources = (pro, rows, cols, count, pro_cols, pro_live, op.at[pl.ds(0, GROUP)], op.at[pl.ds(GROUP, op.shape[0] - GROUP)])
     copies = [pltpu.make_async_copy(src, dst, sems.at[i]) for i, (src, dst) in enumerate(zip(sources, scratch))]
@@ -56,7 +56,6 @@
     base = half * tile
     eighth = quarter // 2
     meta = base + eighth * tile
-    high_at = meta + META
     high_base = (list_len - GROUP) // 2 * tile
     for k in range(quarter):
         pair = jnp.concatenate([pro[k, 0], pro[k + quarter, 0]], axis=1)
@@ -65,31 +64,24 @@
         turned = jnp.concatenate([turned[:tile], turned[tile:]], axis=1)
         part, at = (low, base + k * tile) if k < eighth else (high, high_base + (k - eighth) * tile)
         part[at : at + tile, :] = turned
-        at += 0 if k < eighth else high_at
-        whole[at : at + tile, :] = turned
     r_pay[quarter * tile : quarter * tile + META, :] = jnp.zeros((META, 2 * tile), f32)
     live = pro_live[...] > 0
     r_pay[quarter * tile : quarter * tile + 1, 0:fine_rows] = jnp.where(live, pro_cols[...], -1).astype(f32)
     goals = jnp.where(live, pro_cols[...] + col_index * coarse_cols, -1).astype(f32)
-    for pay in (whole, low):
-        pay[meta : meta + META, :] = jnp.zeros((META, 2 * tile), f32)
-        pay[meta : meta + 1, 0:list_len] = rows[...].astype(f32)
-        pay[meta + 1 : meta + 2, 0:list_len] = (cols[...] + col_index * fine_cols).astype(f32)
-        pay[meta + 2 : meta + 3, 0:1] = count[...].astype(f32)
-        pay[meta + 3 : meta + 4, 0:fine_rows] = goals
-        pay[meta + 3 : meta + 4, fine_rows : fine_rows + 1] = jnp.ones((1, 1), f32)
-        pay[meta + 3 : meta + 4, fine_rows + 1 : fine_rows + 2] = jnp.full((1, 1), col_index, i32).astype(f32)
+    low[meta : meta + META, :] = jnp.zeros((META, 2 * tile), f32)
+    low[meta : meta + 1, 0:list_len] = rows[...].astype(f32)
+    low[meta + 1 : meta + 2, 0:list_len] = (cols[...] + col_index * fine_cols).astype(f32)
+    low[meta + 2 : meta + 3, 0:1] = count[...].astype(f32)
+    low[meta + 3 : meta + 4, 0:fine_rows] = goals
+    low[meta + 3 : meta + 4, fine_rows : fine_rows + 1] = jnp.ones((1, 1), f32)
+    low[meta + 3 : meta + 4, fine_rows + 1 : fine_rows + 2] = jnp.full((1, 1), col_index, i32).astype(f32)
     copies[-2].wait()
     for block in range(half):
-        both = jnp.concatenate([low_tiles[block, 0], low_tiles[block + half, 0]], axis=1)
-        for pay in (whole, low):
-            pay[block * tile : (block + 1) * tile, :] = both
+        low[block * tile : (block + 1) * tile, :] = jnp.concatenate([low_tiles[block, 0], low_tiles[block + half, 0]], axis=1)
     copies[-1].wait()
     for block in range((list_len - GROUP) // 2):
         slot = block // half * GROUP + block % half
-        both = jnp.concatenate([high_tiles[slot, 0], high_tiles[slot + half, 0]], axis=1)
-        high[block * tile : (block + 1) * tile, :] = both
-        whole[high_at + block * tile : high_at + (block + 1) * tile, :] = both
+        high[block * tile : (block + 1) * tile, :] = jnp.concatenate([high_tiles[slot, 0], high_tiles[slot + half, 0]], axis=1)
 
 
 def split(x):
@@ -107,7 +99,7 @@
     return first.astype(bf16), second.astype(bf16)
 
 
-def add_products(low_pay, high_pay, high_at, meta, ids, panel, sizes, acc):
+def add_products(low_pay, high_pay, meta, ids, panel, sizes, acc):
     tile, list_len, fine_rows, coarse_cols, fine_total, owned = sizes
     count = meta[2, 0].astype(i32)
     half = GROUP // 2
@@ -118,7 +110,7 @@
         @pl.when(count > group * GROUP)
         def _(group=group):
             for p in range(half):
-                at = p * tile + (high_at + (group - 1) * half * tile if group else 0)
+                at = (p + max(group - 1, 0) * half) * tile
                 high, low = split(blocks[at : at + tile, :])
                 left = jnp.concatenate([high, low], axis=0)
                 rights, places = [], []
@@ -139,7 +131,7 @@
                     acc[place] += part[:tile] + part[tile:]
 
 
-def products(first, last, n_panel, n_prev, parts, sizes, *refs):
+def products(first, last, n_panel, n_prev, n_new, sizes, *refs):
     tile, list_len, fine_rows, coarse_cols, fine_total, owned = sizes
     refs = list(refs)
     take = lambda n: [refs.pop(0) for _ in range(n)]
@@ -147,7 +139,7 @@
         r_pays = take(n_panel)
     else:
         acc_in, panel, weights_in, ids_in, goals_in = take(5)
-    pays = [take(n) for n in parts]
+    pays = [take(2) for _ in range(n_new)]
     if last:
         strips, keep, send = take(3)
         acc, weights, part, places = take(4)
@@ -200,13 +192,11 @@
                 if k < eighth:
                     block = pay[0][(half + k) * tile : (half + k + 1) * tile, :]
                 else:
-                    from_row = high_base + (k - eighth) * tile + (0 if len(pay) > 1 else meta_at + META)
-                    block = pay[-1][from_row : from_row + tile, :]
+                    block = pay[1][high_base + (k - eighth) * tile : high_base + (k - eighth + 1) * tile, :]
                 for kk, wide in zip((k, k + quarter), halves(block)):
                     weights[kk, pl.ds(at, tile), :] = wide
 
-        high_at = 0 if len(pay) > 1 else meta_at + META
-        add_products(pay[0], pay[-1], high_at, meta, ids, panel, sizes, acc)
+        add_products(pay[0], pay[1], meta, ids, panel, sizes, acc)
     if not last:
         return
 
@@ -274,24 +264,15 @@
     return lax.ppermute(x, axis, [(i, i ^ mask) for i in range(n)])
 
 
-def line_gather(own, odd, hook=None):
+def hop(x, odd, step):
     n = lax.axis_size("col")
-    found = []
-    for step in range(1, n):
-        pairs = []
-        for i in range((step - 1 + odd) % 2, n - 1, 2):
-            if i - (step - 1) >= 0:
-                pairs.append((i, i + 1))
-            if i + step <= n - 1:
-                pairs.append((i + 1, i))
-        if not pairs:
-            break
-        own = lax.ppermute(own, "col", pairs)
-        if step == 2 and hook is not None:
-            own, *rest = lax.optimization_barrier((own, *hook))
-            hook[:] = rest
-        found.append(own)
-    return found
+    pairs = []
+    for i in range((step - 1 + odd) % 2, n - 1, 2):
+        if i - (step - 1) >= 0:
+            pairs.append((i, i + 1))
+        if i + step <= n - 1:
+            pairs.append((i + 1, i))
+    return lax.ppermute(x, "col", pairs) if pairs else None
 
 
 def shards(op_tiles, op_rows, op_cols, op_count, pro_tiles, pro_cols, pro_live):
@@ -305,13 +286,13 @@
     owned = coarse_total // row_count
     n_chips = row_count // 2
     sizes = (tile, list_len, fine_rows, coarse_cols, fine_total, owned)
-    first_rows = (GROUP // 2 + fine_rows // 4) * tile + META
-    z_rows = (list_len // 2 + fine_rows // 2) * tile + META
+    low_rows = (GROUP // 2 + fine_rows // 4) * tile + META
+    high_rows = ((list_len - GROUP) // 2 + fine_rows // 4) * tile
     r_rows = fine_rows // 2 * tile + META
 
-    whole, low, high, r_pay = call(
+    low, high, r_pay = call(
         functools.partial(pack, fine_cols, coarse_cols),
-        (shape(z_rows, 2 * tile), shape(first_rows, 2 * tile), shape(z_rows - first_rows, 2 * tile), shape(r_rows, 2 * tile)),
+        (shape(low_rows, 2 * tile), shape(high_rows, 2 * tile), shape(r_rows, 2 * tile)),
         7,
         (
             pltpu.VMEM(pro_tiles.shape, f32),
@@ -337,12 +318,24 @@
         pro_live.reshape(1, -1),
     )
 
-    chips = [r_pay] + [swap(r_pay, "row", m) for m in range(2, row_count, 2)]
+    even = [[hop(x, 0, 1)] for x in (low, high)]
+    odd = [[hop(x, 1, 1)] for x in (low, high)]
+    odd[0][0], _ = lax.optimization_barrier((odd[0][0], even[0][0]))
+    for chains, side in ((even, 0), (odd, 1)):
+        for chain in chains:
+            for step in range(2, col_count):
+                x = hop(chain[-1], side, step)
+                if x is not None:
+                    chain.append(x)
+    split_chain, other_chain = list(zip(*even)), list(zip(*odd))
+    n_ids, n_goals = (-(-n // META) * META for n in (row_count, 2 * col_count))
+    one = swap(r_pay, "row", 2)
+    r_later, *rest = lax.optimization_barrier((r_pay, other_chain[1][0]))
+    other_chain[1] = (rest[0], other_chain[1][1])
+    chips = [r_pay, one] + [swap(r_later, "row", m) for m in range(4, row_count, 2)]
+    chips, *rest = lax.optimization_barrier((chips, other_chain[1][1]))
+    other_chain[1] = (other_chain[1][0], rest[0])
     panel_pays = [x for pair in zip(chips, [swap(x, "row", 1) for x in chips]) for x in pair]
-
-    split_chain = list(zip(line_gather(low, False, panel_pays), line_gather(high, False)))
-    whole_chain = [(x,) for x in line_gather(whole, True)]
-    n_ids, n_goals = (-(-n // META) * META for n in (row_count, 2 * col_count))
 
     def stage(first, last, n_prev, state, pays):
         out = [
@@ -368,12 +361,11 @@
             ] + scratch
             out = [shape(fine_rows, tile, coarse_cols * tile)] + [shape(spread, tile, coarse_cols * tile)] * 2
         operands = list(state) + [x for pay in pays for x in pay]
-        parts = [len(pay) for pay in pays]
-        kernel = functools.partial(products, first, last, row_count, n_prev, parts, sizes)
+        kernel = functools.partial(products, first, last, row_count, n_prev, len(pays), sizes)
         return call(kernel, tuple(out), len(operands), scratch, flops=2**28, nbytes=4 * 2**20)(*operands)
 
-    early = [(low, high)] + split_chain[:1] + whole_chain[:1]
-    middle = split_chain[1:-1] + whole_chain[1:]
+    early = [(low, high)] + split_chain[:1] + other_chain[:1]
+    middle = split_chain[1:-1] + other_chain[1:]
     late = split_chain[-1:]
     acc, weights, goals, panel, ids = stage(True, False, 0, panel_pays, early)
     acc, weights, goals = stage(False, False, len(early), (acc, panel, weights, ids, goals), middle)

time: 69.9 us -> 65.2 us (0.933)
  waiting for transfers between devices: 33.2 us -> 25.3 us
  starting transfers between devices: 22 us -> 25 us
    ppermute x8 -> x10, waiting for transfers between devices: 22 us -> 15.1 us  [hop(): return lax.ppermute(x, 'col', pairs) if pairs else None]
    ppermute x8 -> x10, starting transfers between devices: 11.9 us -> 15.4 us  [hop(): return lax.ppermute(x, 'col', pairs) if pairs else None]
    ppermute x11, waiting for transfers between devices: 11.2 us -> 10.3 us  [swap(): return lax.ppermute(x, axis, [(i, i ^ mask) for i in range(n)])]
  transfers between devices with their start and end apart: 19 -> 21, of which waited for: 11 -> 13; matrix products, arithmetic and copies ran while one was open for 0% -> 0% of each run, Pallas kernels for 7% -> 8%
where the time goes in v5:
time: 65.2 us; the launch traced here: 64.9 us
  waiting for transfers between devices  25.3 us (39%)
  starting transfers between devices  25 us (38%)
  Pallas kernels  10.3 us (16%)
  local copies, waits for them, and re-layouts  2.85 us (4%)
  between operations  1.42 us (2%)
    ppermute x10, starting transfers between devices, hop(): return lax.ppermute(x, 'col', pairs) if pairs else None  15.4 us
    ppermute x10, waiting for transfers between devices, hop(): return lax.ppermute(x, 'col', pairs) if pairs else None  15.1 us
    ppermute x11, waiting for transfers between devices, swap(): return lax.ppermute(x, axis, [(i, i ^ mask) for i in range(n)])  10.3 us
    ppermute x11, starting transfers between devices, swap(): return lax.ppermute(x, axis, [(i, i ^ mask) for i in range(n)])  9.61 us
    pallas_call x3, Pallas kernels, stage(): call(kernel, tuple(out), len(operands), scratch, flops=2 ** 28, nbytes=4...  5.89 us
    unnamed x6, local copies, waits for them, and re-layouts  2.85 us
    pallas_call x1, Pallas kernels, shards(): call(functools.partial(pack, fine_cols, coarse_cols), (shape(low_rows, 2...  2.35 us
  transfers between devices with their start and end apart: 21, of which 13 were waited for; matrix products, arithmetic and copies ran while one was open for 0% of the time, Pallas kernels for 8%

profile of v5, /device:TPU:0, one launch (start us, length us, event | category | flops | bytes accessed | tf_op | source)
XLA Modules:
  0.0 64.9 jit_solution(2956201560005273878)
XLA Ops:
  1.3 2.3 %shard_map.86 = (f32[648,128]{1,0:T(8,128)}, f32[640,128]{1,0:T(8,128)}, f32[264,128]{1,0:T(8,128)}) custom-call(f32[32,1,64,64]{3,2,1,0:T(8,128)} %op.1, f32[8,1,64,64]{3,2,1,0:T(8,128)} %pro.1, s32[1,32]{1,0:T(1,128)} %bitcast.4, s32[1,32]{1,0:T(1,128)} %bitcast.5, s32[1,1]{1,0:T(1,128)S(6)} %copy.9.count, s32[1,8]{1,0:T(1,128)} %bitcast.6, s32[1,8]{1,0:T(1,128)} %bitcast.7), custom_call_target="tpu_custom_call" | custom-call | bytes 4194304 | tf_op jit(solution)/shard_map/pallas_call | solution.py:293
  3.6 3.1 %collective-permute-start.2 = (f32[648,128]{1,0:T(8,128)}, f32[648,128]{1,0:T(8,128)S(1)}, u32[]{:S(2)}, u32[]{:S(2)}) collective-permute-start(f32[648,128]{1,0:T(8,128)} %get-tuple-element.29.refs_8_), channel_id=1, source_target_pairs={{0,1},{1,0},{2,3},{3,2},{4,5},{5,4},{6,7},{7,6},{8,9},{9,8},{10,11... | collective-permute-start | bytes 995336 | tf_op jit(solution)/shard_map/ppermute | solution.py:275
  7.4 4.4 %collective-permute-start.12 = (f32[640,128]{1,0:T(8,128)}, f32[640,128]{1,0:T(8,128)S(1)}, u32[]{:S(2)}, u32[]{:S(2)}) collective-permute-start(f32[640,128]{1,0:T(8,128)} %get-tuple-element.32.refs_9_), channel_id=1, source_target_pairs={{0,1},{1,0},{2,3},{3,2},{4,5},{5,4},{6,7},{7,6},{8,9},{9,8},{10,11... | collective-permute-start | bytes 983048 | tf_op jit(solution)/shard_map/ppermute | solution.py:275
  12.5 3.0 %collective-permute-done.2.refs_10_ = f32[648,128]{1,0:T(8,128)S(1)} collective-permute-done((f32[648,128]{1,0:T(8,128)}, f32[648,128]{1,0:T(8,128)S(1)}, u32[]{:S(2)}, u32[]{:S(2)}) %collective-permute-start.2) | collective-permute-done | bytes 331808 | tf_op jit(solution)/shard_map/ppermute | solution.py:275
  15.6 1.3 %collective-permute-start.3 = (f32[648,128]{1,0:T(8,128)S(1)}, f32[648,128]{1,0:T(8,128)S(1)}, u32[]{:S(2)}, u32[]{:S(2)}) collective-permute-start(f32[648,128]{1,0:T(8,128)S(1)} %collective-permute-done.1.refs_12_), channel_id=1, source_target_pairs={{1,0},{2,3},{5,4},{6,7},{9,8},{10,11},{13,12},{14,15},{17,16},{18,... | collective-permute-start | bytes 995336 | tf_op jit(solution)/shard_map/ppermute | solution.py:275
  17.5 5.0 %collective-permute-done.12.refs_11_ = f32[640,128]{1,0:T(8,128)S(1)} collective-permute-done((f32[640,128]{1,0:T(8,128)}, f32[640,128]{1,0:T(8,128)S(1)}, u32[]{:S(2)}, u32[]{:S(2)}) %collective-permute-start.12) | collective-permute-done | bytes 327712 | tf_op jit(solution)/shard_map/ppermute | solution.py:275
  23.3 1.3 %collective-permute-start.7 = (f32[640,128]{1,0:T(8,128)S(1)}, f32[640,128]{1,0:T(8,128)S(1)}, u32[]{:S(2)}, u32[]{:S(2)}) collective-permute-start(f32[640,128]{1,0:T(8,128)S(1)} %collective-permute-done.6.refs_13_), channel_id=1, source_target_pairs={{1,0},{2,3},{5,4},{6,7},{9,8},{10,11},{13,12},{14,15},{17,16},{18,... | collective-permute-start | bytes 983048 | tf_op jit(solution)/shard_map/ppermute | solution.py:275
  24.6 2.0 %collective-permute-start = (f32[264,128]{1,0:T(8,128)}, f32[264,128]{1,0:T(8,128)S(1)}, u32[]{:S(2)}, u32[]{:S(2)}) collective-permute-start(f32[264,128]{1,0:T(8,128)} %get-tuple-element.33.refs_0_), channel_id=1, source_target_pairs={{0,8},{4,12},{8,0},{12,4},{16,24},{20,28},{24,16},{28,20},{1,9},{5... | collective-permute-start | bytes 405512 | tf_op jit(solution)/shard_map/ppermute | solution.py:264
  26.6 3.3 %collective-permute-done.3.refs_7_ = f32[648,128]{1,0:T(8,128)S(1)} collective-permute-done((f32[648,128]{1,0:T(8,128)S(1)}, f32[648,128]{1,0:T(8,128)S(1)}, u32[]{:S(2)}, u32[]{:S(2)}) %collective-permute-start.3) | collective-permute-done | bytes 331808 | tf_op jit(solution)/shard_map/ppermute | solution.py:275
  29.9 1.8 %collective-permute-start.4 = (f32[264,128]{1,0:T(8,128)}, f32[264,128]{1,0:T(8,128)S(1)}, u32[]{:S(2)}, u32[]{:S(2)}) collective-permute-start(f32[264,128]{1,0:T(8,128)} %get-tuple-element.33.refs_0_), channel_id=1, source_target_pairs={{0,16},{4,20},{8,24},{12,28},{16,0},{20,4},{24,8},{28,12},{1,17},{... | collective-permute-start | bytes 405512 | tf_op jit(solution)/shard_map/ppermute | solution.py:264
  31.7 1.4 %collective-permute-start.5 = (f32[264,128]{1,0:T(8,128)}, f32[264,128]{1,0:T(8,128)S(1)}, u32[]{:S(2)}, u32[]{:S(2)}) collective-permute-start(f32[264,128]{1,0:T(8,128)} %get-tuple-element.33.refs_0_), channel_id=1, source_target_pairs={{0,24},{4,28},{8,16},{12,20},{16,8},{20,12},{24,0},{28,4},{1,25},{... | collective-permute-start | bytes 405512 | tf_op jit(solution)/shard_map/ppermute | solution.py:264
  33.1 1.3 %collective-permute-start.15 = (f32[648,128]{1,0:T(8,128)S(1)}, f32[648,128]{1,0:T(8,128)S(1)}, u32[]{:S(2)}, u32[]{:S(2)}) collective-permute-start(f32[648,128]{1,0:T(8,128)S(1)} %collective-permute-done.13.refs_5_), channel_id=1, source_target_pairs={{1,0},{2,3},{5,4},{6,7},{9,8},{10,11},{13,12},{14,15},{17,16},{18,... | collective-permute-start | bytes 995336 | tf_op jit(solution)/shard_map/ppermute | solution.py:275
  34.4 1.3 %collective-permute-start.16 = (f32[640,128]{1,0:T(8,128)S(1)}, f32[640,128]{1,0:T(8,128)S(1)}, u32[]{:S(2)}, u32[]{:S(2)}) collective-permute-start(f32[640,128]{1,0:T(8,128)S(1)} %collective-permute-done.14.refs_6_), channel_id=1, source_target_pairs={{1,0},{2,3},{5,4},{6,7},{9,8},{10,11},{13,12},{14,15},{17,16},{18,... | collective-permute-start | bytes 983048 | tf_op jit(solution)/shard_map/ppermute | solution.py:275
  36.0 1.8 %collective-permute-done.5.refs_6_ = f32[264,128]{1,0:T(8,128)S(1)} collective-permute-done((f32[264,128]{1,0:T(8,128)}, f32[264,128]{1,0:T(8,128)S(1)}, u32[]{:S(2)}, u32[]{:S(2)}) %collective-permute-start.5) | collective-permute-done | bytes 135200 | tf_op jit(solution)/shard_map/ppermute | solution.py:264
  43.4 2.4 %shard_map.87 = (f32[32,64,128]{2,1,0:T(8,128)S(1)}, bf16[8,256,128]{2,1,0:T(8,128)(2,1)S(1)}, f32[8,128]{1,0:T(8,128)S(1)}, bf16[65,64,128]{2,1,0:T(8,128)(2,1)S(1)}, f32[8,128]{1,0:T(8,128)S(1)}) custom-call(f32[264,128]{1,0:T(8,128)S(1)} %copy-done.2, f32[264,128]{1,0:T(8,128)S(1)} %collective-permute-done.8.refs_1_, ...), custom_call_target="tpu_custom_call" | custom-call | flops 268435456 | bytes 4194304 | tf_op jit(solution)/shard_map/pallas_call | solution.py:365
  45.8 1.3 %shard_map.88 = (f32[32,64,128]{2,1,0:T(8,128)S(1)}, bf16[8,256,128]{2,1,0:T(8,128)(2,1)S(1)}, f32[8,128]{1,0:T(8,128)S(1)}) custom-call(f32[32,64,128]{2,1,0:T(8,128)S(1)} %get-tuple-element.37.refs_0_, bf16[65,64,128]{2,1,0:T(8,128)(2,1)S(1)} %get-tuple-element.38.refs_1_, bf16[8,256,128]{2,1,0:T(8,128)(2,1)S(1)} %get-tuple-element.39.refs_2_, ...), custom_call_target="tpu_custom_call" | custom-call | flops 268435456 | bytes 4194304 | tf_op jit(solution)/shard_map/pallas_call | solution.py:365
  47.1 3.5 %collective-permute-done.16.refs_6_ = f32[640,128]{1,0:T(8,128)S(1)} collective-permute-done((f32[640,128]{1,0:T(8,128)S(1)}, f32[640,128]{1,0:T(8,128)S(1)}, u32[]{:S(2)}, u32[]{:S(2)}) %collective-permute-start.16) | collective-permute-done | bytes 327712 | tf_op jit(solution)/shard_map/ppermute | solution.py:275
  50.6 2.2 %shard_map.89 = (f32[8,64,256]{2,1,0:T(8,128)S(1)}, f32[8,64,256]{2,1,0:T(8,128)S(1)}, f32[8,64,256]{2,1,0:T(8,128)S(1)}) custom-call(f32[32,64,128]{2,1,0:T(8,128)S(1)} %get-tuple-element.44.refs_0_, bf16[65,64,128]{2,1,0:T(8,128)(2,1)S(1)} %get-tuple-element.38.refs_1_, bf16[8,256,128]{2,1,0:T(8,128)(2,1)S(1)} %get-tuple-element.45.refs_2_, ...), custom_call_target="tpu_custom_call" | custom-call | flops 268435456 | bytes 4194304 | tf_op jit(solution)/shard_map/pallas_call | solution.py:365
  52.9 1.9 %collective-permute-done.17.received = f32[8,64,256]{2,1,0:T(8,128)S(1)} collective-permute-done((f32[8,64,256]{2,1,0:T(8,128)S(1)}, f32[8,64,256]{2,1,0:T(8,128)S(1)}, u32[]{:S(2)}, u32[]{:S(2)}) %collective-permute-start.17) | collective-permute-done | bytes 524320 | tf_op jit(solution)/shard_map/ppermute | solution.py:264
  54.8 1.2 %collective-permute-start.18 = (f32[2,64,256]{2,1,0:T(8,128)S(1)}, f32[2,64,256]{2,1,0:T(8,128)S(1)}, u32[]{:S(2)}, u32[]{:S(2)}) collective-permute-start(f32[2,64,256]{2,1,0:T(8,128)S(1)} %get-tuple-element.51), channel_id=1, source_target_pairs={{0,8},{4,12},{8,0},{12,4},{16,24},{20,28},{24,16},{28,20},{1,9},{5... | collective-permute-start | bytes 393224 | tf_op jit(solution)/shard_map/ppermute | solution.py:264
  56.0 1.5 %collective-permute-start.19 = (f32[2,64,256]{2,1,0:T(8,128)S(1)}, f32[2,64,256]{2,1,0:T(8,128)S(1)}, u32[]{:S(2)}, u32[]{:S(2)}) collective-permute-start(f32[2,64,256]{2,1,0:T(8,128)S(1)} %get-tuple-element.52), channel_id=1, source_target_pairs={{0,16},{4,20},{8,24},{12,28},{16,0},{20,4},{24,8},{28,12},{1,17},{... | collective-permute-start | bytes 393224 | tf_op jit(solution)/shard_map/ppermute | solution.py:264
  58.4 1.2 %shard_map.90 = f32[8,4,64,64]{3,2,1,0:T(8,128)} custom-call(f32[8,64,256]{2,1,0:T(8,128)S(1)} %get-tuple-element.47.strips), custom_call_target="tpu_custom_call" | custom-call | flops 16777216 | bytes 1048576 | tf_op jit(solution)/shard_map/pallas_call | solution.py:375
  59.5 1.7 %collective-permute-done.18.refs_1_ = f32[2,64,256]{2,1,0:T(8,128)S(1)} collective-permute-done((f32[2,64,256]{2,1,0:T(8,128)S(1)}, f32[2,64,256]{2,1,0:T(8,128)S(1)}, u32[]{:S(2)}, u32[]{:S(2)}) %collective-permute-start.18) | collective-permute-done | bytes 131104 | tf_op jit(solution)/shard_map/ppermute | solution.py:264
  61.2 2.8 %collective-permute-done.19.refs_2_ = f32[2,64,256]{2,1,0:T(8,128)S(1)} collective-permute-done((f32[2,64,256]{2,1,0:T(8,128)S(1)}, f32[2,64,256]{2,1,0:T(8,128)S(1)}, u32[]{:S(2)}, u32[]{:S(2)}) %collective-permute-start.19) | collective-permute-done | bytes 131104 | tf_op jit(solution)/shard_map/ppermute | solution.py:264
  (31 shorter events, 10.4 us)
Async XLA Ops:
  3.6 11.9 %collective-permute-start.2 = (f32[648,128]{1,0:T(8,128)}, f32[648,128]{1,0:T(8,128)S(1)}, u32[]{:S(2)}, u32[]{:S(2)}) collective-permute-start(f32[648,128]{1,0:T(8,128)} %get-tuple-element.29.refs_8_), channel_id=1, source_target_pairs={{0,1},{1,0},{2,3},{3,2},{4,5},{5,4},{6,7},{7,6},{8,9},{9,8},{10,11... | collective-permute-start | bytes 995336 | tf_op jit(solution)/shard_map/ppermute | solution.py:275
  6.7 8.8 %collective-permute-start.1 = (f32[648,128]{1,0:T(8,128)}, f32[648,128]{1,0:T(8,128)S(1)}, u32[]{:S(2)}, u32[]{:S(2)}) collective-permute-start(f32[648,128]{1,0:T(8,128)} %get-tuple-element.29.refs_8_), channel_id=1, source_target_pairs={{1,2},{2,1},{5,6},{6,5},{9,10},{10,9},{13,14},{14,13},{17,18},{18,... | collective-permute-start | bytes 995336 | tf_op jit(solution)/shard_map/ppermute | solution.py:275
  7.4 15.2 %collective-permute-start.12 = (f32[640,128]{1,0:T(8,128)}, f32[640,128]{1,0:T(8,128)S(1)}, u32[]{:S(2)}, u32[]{:S(2)}) collective-permute-start(f32[640,128]{1,0:T(8,128)} %get-tuple-element.32.refs_9_), channel_id=1, source_target_pairs={{0,1},{1,0},{2,3},{3,2},{4,5},{5,4},{6,7},{7,6},{8,9},{9,8},{10,11... | collective-permute-start | bytes 983048 | tf_op jit(solution)/shard_map/ppermute | solution.py:275
  11.8 11.4 %collective-permute-start.6 = (f32[640,128]{1,0:T(8,128)}, f32[640,128]{1,0:T(8,128)S(1)}, u32[]{:S(2)}, u32[]{:S(2)}) collective-permute-start(f32[640,128]{1,0:T(8,128)} %get-tuple-element.32.refs_9_), channel_id=1, source_target_pairs={{1,2},{2,1},{5,6},{6,5},{9,10},{10,9},{13,14},{14,13},{17,18},{18,... | collective-permute-start | bytes 983048 | tf_op jit(solution)/shard_map/ppermute | solution.py:275
  15.6 14.3 %collective-permute-start.3 = (f32[648,128]{1,0:T(8,128)S(1)}, f32[648,128]{1,0:T(8,128)S(1)}, u32[]{:S(2)}, u32[]{:S(2)}) collective-permute-start(f32[648,128]{1,0:T(8,128)S(1)} %collective-permute-done.1.refs_12_), channel_id=1, source_target_pairs={{1,0},{2,3},{5,4},{6,7},{9,8},{10,11},{13,12},{14,15},{17,16},{18,... | collective-permute-start | bytes 995336 | tf_op jit(solution)/shard_map/ppermute | solution.py:275
  16.8 16.3 %collective-permute-start.13 = (f32[648,128]{1,0:T(8,128)S(1)}, f32[648,128]{1,0:T(8,128)S(1)}, u32[]{:S(2)}, u32[]{:S(2)}) collective-permute-start(f32[648,128]{1,0:T(8,128)S(1)} %collective-permute-done.2.refs_10_), channel_id=1, source_target_pairs={{1,2},{2,1},{5,6},{6,5},{9,10},{10,9},{13,14},{14,13},{17,18},{18,... | collective-permute-start | bytes 995336 | tf_op jit(solution)/shard_map/ppermute | solution.py:275
  22.6 11.9 %collective-permute-start.14 = (f32[640,128]{1,0:T(8,128)S(1)}, f32[640,128]{1,0:T(8,128)S(1)}, u32[]{:S(2)}, u32[]{:S(2)}) collective-permute-start(f32[640,128]{1,0:T(8,128)S(1)} %collective-permute-done.12.refs_11_), channel_id=1, source_target_pairs={{1,2},{2,1},{5,6},{6,5},{9,10},{10,9},{13,14},{14,13},{17,18},{18,... | collective-permute-start | bytes 983048 | tf_op jit(solution)/shard_map/ppermute | solution.py:275
  23.3 12.7 %collective-permute-start.7 = (f32[640,128]{1,0:T(8,128)S(1)}, f32[640,128]{1,0:T(8,128)S(1)}, u32[]{:S(2)}, u32[]{:S(2)}) collective-permute-start(f32[640,128]{1,0:T(8,128)S(1)} %collective-permute-done.6.refs_13_), channel_id=1, source_target_pairs={{1,0},{2,3},{5,4},{6,7},{9,8},{10,11},{13,12},{14,15},{17,16},{18,... | collective-permute-start | bytes 983048 | tf_op jit(solution)/shard_map/ppermute | solution.py:275
  24.6 7.1 %collective-permute-start = (f32[264,128]{1,0:T(8,128)}, f32[264,128]{1,0:T(8,128)S(1)}, u32[]{:S(2)}, u32[]{:S(2)}) collective-permute-start(f32[264,128]{1,0:T(8,128)} %get-tuple-element.33.refs_0_), channel_id=1, source_target_pairs={{0,8},{4,12},{8,0},{12,4},{16,24},{20,28},{24,16},{28,20},{1,9},{5... | collective-permute-start | bytes 405512 | tf_op jit(solution)/shard_map/ppermute | solution.py:264
  29.9 6.2 %collective-permute-start.4 = (f32[264,128]{1,0:T(8,128)}, f32[264,128]{1,0:T(8,128)S(1)}, u32[]{:S(2)}, u32[]{:S(2)}) collective-permute-start(f32[264,128]{1,0:T(8,128)} %get-tuple-element.33.refs_0_), channel_id=1, source_target_pairs={{0,16},{4,20},{8,24},{12,28},{16,0},{20,4},{24,8},{28,12},{1,17},{... | collective-permute-start | bytes 405512 | tf_op jit(solution)/shard_map/ppermute | solution.py:264
  31.7 6.1 %collective-permute-start.5 = (f32[264,128]{1,0:T(8,128)}, f32[264,128]{1,0:T(8,128)S(1)}, u32[]{:S(2)}, u32[]{:S(2)}) collective-permute-start(f32[264,128]{1,0:T(8,128)} %get-tuple-element.33.refs_0_), channel_id=1, source_target_pairs={{0,24},{4,28},{8,16},{12,20},{16,8},{20,12},{24,0},{28,4},{1,25},{... | collective-permute-start | bytes 405512 | tf_op jit(solution)/shard_map/ppermute | solution.py:264
  33.1 17.4 %collective-permute-start.15 = (f32[648,128]{1,0:T(8,128)S(1)}, f32[648,128]{1,0:T(8,128)S(1)}, u32[]{:S(2)}, u32[]{:S(2)}) collective-permute-start(f32[648,128]{1,0:T(8,128)S(1)} %collective-permute-done.13.refs_5_), channel_id=1, source_target_pairs={{1,0},{2,3},{5,4},{6,7},{9,8},{10,11},{13,12},{14,15},{17,16},{18,... | collective-permute-start | bytes 995336 | tf_op jit(solution)/shard_map/ppermute | solution.py:275
  34.4 16.1 %collective-permute-start.16 = (f32[640,128]{1,0:T(8,128)S(1)}, f32[640,128]{1,0:T(8,128)S(1)}, u32[]{:S(2)}, u32[]{:S(2)}) collective-permute-start(f32[640,128]{1,0:T(8,128)S(1)} %collective-permute-done.14.refs_6_), channel_id=1, source_target_pairs={{1,0},{2,3},{5,4},{6,7},{9,8},{10,11},{13,12},{14,15},{17,16},{18,... | collective-permute-start | bytes 983048 | tf_op jit(solution)/shard_map/ppermute | solution.py:275
  37.8 1.4 %collective-permute-start.10 = (f32[264,128]{1,0:T(8,128)S(1)}, f32[264,128]{1,0:T(8,128)S(1)}, u32[]{:S(2)}, u32[]{:S(2)}) collective-permute-start(f32[264,128]{1,0:T(8,128)S(1)} %collective-permute-done.4.refs_4_), channel_id=1, source_target_pairs={{0,4},{4,0},{8,12},{12,8},{16,20},{20,16},{24,28},{28,24},{1,5},{5... | collective-permute-start | bytes 405512 | tf_op jit(solution)/shard_map/ppermute | solution.py:264
  37.8 1.6 %collective-permute-start.11 = (f32[264,128]{1,0:T(8,128)S(1)}, f32[264,128]{1,0:T(8,128)S(1)}, u32[]{:S(2)}, u32[]{:S(2)}) collective-permute-start(f32[264,128]{1,0:T(8,128)S(1)} %collective-permute-done.5.refs_6_), channel_id=1, source_target_pairs={{0,4},{4,0},{8,12},{12,8},{16,20},{20,16},{24,28},{28,24},{1,5},{5... | collective-permute-start | bytes 405512 | tf_op jit(solution)/shard_map/ppermute | solution.py:264
  38.3 1.6 %collective-permute-start.8 = (f32[264,128]{1,0:T(8,128)}, f32[264,128]{1,0:T(8,128)S(1)}, u32[]{:S(2)}, u32[]{:S(2)}) collective-permute-start(f32[264,128]{1,0:T(8,128)} %get-tuple-element.33.refs_0_), channel_id=1, source_target_pairs={{0,4},{4,0},{8,12},{12,8},{16,20},{20,16},{24,28},{28,24},{1,5},{5... | collective-permute-start | bytes 405512 | tf_op jit(solution)/shard_map/ppermute | solution.py:264
  39.2 1.4 %collective-permute-start.9 = (f32[264,128]{1,0:T(8,128)S(1)}, f32[264,128]{1,0:T(8,128)S(1)}, u32[]{:S(2)}, u32[]{:S(2)}) collective-permute-start(f32[264,128]{1,0:T(8,128)S(1)} %collective-permute-done.refs_2_), channel_id=1, source_target_pairs={{0,4},{4,0},{8,12},{12,8},{16,20},{20,16},{24,28},{28,24},{1,5},{5... | collective-permute-start | bytes 405512 | tf_op jit(solution)/shard_map/ppermute | solution.py:264
  40.5 1.0 %copy-start = (f32[648,128]{1,0:T(8,128)S(1)}, f32[648,128]{1,0:T(8,128)}, u32[]{:S(2)}) copy-start(f32[648,128]{1,0:T(8,128)} %get-tuple-element.29.refs_8_) | copy-start | bytes 995332
  41.5 1.0 %copy-start.1 = (f32[640,128]{1,0:T(8,128)S(1)}, f32[640,128]{1,0:T(8,128)}, u32[]{:S(2)}) copy-start(f32[640,128]{1,0:T(8,128)} %get-tuple-element.32.refs_9_) | copy-start | bytes 983044
  42.5 0.9 %copy-start.2 = (f32[264,128]{1,0:T(8,128)S(1)}, f32[264,128]{1,0:T(8,128)}, u32[]{:S(2)}) copy-start(f32[264,128]{1,0:T(8,128)} %get-tuple-element.33.refs_0_) | copy-start | bytes 405508
  52.8 2.0 %collective-permute-start.17 = (f32[8,64,256]{2,1,0:T(8,128)S(1)}, f32[8,64,256]{2,1,0:T(8,128)S(1)}, u32[]{:S(2)}, u32[]{:S(2)}) collective-permute-start(f32[8,64,256]{2,1,0:T(8,128)S(1)} %get-tuple-element.49), channel_id=1, source_target_pairs={{0,4},{4,0},{8,12},{12,8},{16,20},{20,16},{24,28},{28,24},{1,5},{5... | collective-permute-start | bytes 1572872 | tf_op jit(solution)/shard_map/ppermute | solution.py:264
  54.8 6.4 %collective-permute-start.18 = (f32[2,64,256]{2,1,0:T(8,128)S(1)}, f32[2,64,256]{2,1,0:T(8,128)S(1)}, u32[]{:S(2)}, u32[]{:S(2)}) collective-permute-start(f32[2,64,256]{2,1,0:T(8,128)S(1)} %get-tuple-element.51), channel_id=1, source_target_pairs={{0,8},{4,12},{8,0},{12,4},{16,24},{20,28},{24,16},{28,20},{1,9},{5... | collective-permute-start | bytes 393224 | tf_op jit(solution)/shard_map/ppermute | solution.py:264
  56.0 8.1 %collective-permute-start.19 = (f32[2,64,256]{2,1,0:T(8,128)S(1)}, f32[2,64,256]{2,1,0:T(8,128)S(1)}, u32[]{:S(2)}, u32[]{:S(2)}) collective-permute-start(f32[2,64,256]{2,1,0:T(8,128)S(1)} %get-tuple-element.52), channel_id=1, source_target_pairs={{0,16},{4,20},{8,24},{12,28},{16,0},{20,4},{24,8},{28,12},{1,17},{... | collective-permute-start | bytes 393224 | tf_op jit(solution)/shard_map/ppermute | solution.py:264
  57.5 6.6 %collective-permute-start.20 = (f32[2,64,256]{2,1,0:T(8,128)S(1)}, f32[2,64,256]{2,1,0:T(8,128)S(1)}, u32[]{:S(2)}, u32[]{:S(2)}) collective-permute-start(f32[2,64,256]{2,1,0:T(8,128)S(1)} %get-tuple-element.53), channel_id=1, source_target_pairs={{0,24},{4,28},{8,16},{12,20},{16,8},{20,12},{24,0},{28,4},{1,25},{... | collective-permute-start | bytes 393224 | tf_op jit(solution)/shard_map/ppermute | solution.py:264

commit v6 on v5

--- a/solution.py
+++ b/solution.py
@@ -18,12 +18,12 @@
 HBM = pl.BlockSpec(memory_space=pltpu.HBM)
 
 
-def call(kernel, out_shape, n_in, scratch=(), flops=0, nbytes=0, space=VMEM, limit=VMEM_BYTES):
+def call(kernel, out_shape, n_in, scratch=(), flops=0, nbytes=0, space=VMEM, limit=VMEM_BYTES, out_space=VMEM):
     return pl.pallas_call(
         kernel,
         out_shape=out_shape,
         in_specs=[space] * n_in,
-        out_specs=jax.tree.map(lambda _: VMEM, out_shape),
+        out_specs=jax.tree.map(lambda _: out_space, out_shape),
         scratch_shapes=list(scratch),
         compiler_params=pltpu.CompilerParams(vmem_limit_bytes=limit),
         cost_estimate=pl.CostEstimate(flops=flops, bytes_accessed=nbytes, transcendentals=0),
@@ -40,15 +40,20 @@
     return lax.shift_right_logical(x, n.bit_length() - 1), x & (n - 1)
 
 
-def pack(fine_cols, coarse_cols, op, pro, rows, cols, count, pro_cols, pro_live, low, high, r_pay, *scratch):
-    sems = scratch[-1]
+def pack(fine_cols, coarse_cols, op, pro, rows, cols, count, pro_cols, pro_live, low_out, high_out, r_out, *scratch):
+    low, high, r_pay, sems = scratch[-4:]
+    scratch = scratch[:-4]
+    outward = [
+        pltpu.make_async_copy(src, dst, sems.at[len(scratch) + i])
+        for i, (src, dst) in enumerate(((r_pay, r_out), (low, low_out), (high, high_out)))
+    ]
     sources = (pro, rows, cols, count, pro_cols, pro_live, op.at[pl.ds(0, GROUP)], op.at[pl.ds(GROUP, op.shape[0] - GROUP)])
     copies = [pltpu.make_async_copy(src, dst, sems.at[i]) for i, (src, dst) in enumerate(zip(sources, scratch))]
     for copy in copies:
         copy.start()
     for copy in copies[:-2]:
         copy.wait()
-    pro, rows, cols, count, pro_cols, pro_live, low_tiles, high_tiles = scratch[:-1]
+    pro, rows, cols, count, pro_cols, pro_live, low_tiles, high_tiles = scratch
     list_len, tile = op.shape[0], op.shape[2]
     fine_rows = pro.shape[0]
     half, quarter = GROUP // 2, fine_rows // 2
@@ -75,13 +80,18 @@
     low[meta + 3 : meta + 4, 0:fine_rows] = goals
     low[meta + 3 : meta + 4, fine_rows : fine_rows + 1] = jnp.ones((1, 1), f32)
     low[meta + 3 : meta + 4, fine_rows + 1 : fine_rows + 2] = jnp.full((1, 1), col_index, i32).astype(f32)
+    outward[0].start()
     copies[-2].wait()
     for block in range(half):
         low[block * tile : (block + 1) * tile, :] = jnp.concatenate([low_tiles[block, 0], low_tiles[block + half, 0]], axis=1)
+    outward[1].start()
     copies[-1].wait()
     for block in range((list_len - GROUP) // 2):
         slot = block // half * GROUP + block % half
         high[block * tile : (block + 1) * tile, :] = jnp.concatenate([high_tiles[slot, 0], high_tiles[slot + half, 0]], axis=1)
+    outward[2].start()
+    for copy in outward:
+        copy.wait()
 
 
 def split(x):
@@ -179,6 +189,8 @@
             goals_out[...] = goals_in[...]
         for i, pay in enumerate(pays):
             goals_out[n_prev + i : n_prev + i + 1, :] = pay[0][meta_at + 3 : meta_at + 4, :]
+    if last:
+        part[...] = jnp.zeros_like(part)
     for copy in copies:
         copy.wait()
 
@@ -213,7 +225,6 @@
                 chip, core = divide(owner ^ row_index, 2)
                 places[source, k] = jnp.where(goal >= 0, (core * n_chips + chip) * owned + within, dump)
 
-    part[...] = jnp.zeros_like(part)
     n_sources = weights.shape[1] // tile
     for k in range(fine_rows):
         sums = []
@@ -303,10 +314,14 @@
             pltpu.VMEM((1, fine_rows), i32),
             pltpu.VMEM((GROUP,) + op_tiles.shape[1:], f32),
             pltpu.VMEM((list_len - GROUP,) + op_tiles.shape[1:], f32),
-            pltpu.SemaphoreType.DMA((8,)),
+            pltpu.VMEM((low_rows, 2 * tile), f32),
+            pltpu.VMEM((high_rows, 2 * tile), f32),
+            pltpu.VMEM((r_rows, 2 * tile), f32),
+            pltpu.SemaphoreType.DMA((11,)),
         ),
         nbytes=4 * 2**20,
         space=HBM,
+        out_space=HBM,
         limit=FULL_BYTES,
     )(
         op_tiles,
@@ -377,7 +392,7 @@
     )(strips)
     part = shape(owned, tile, coarse_cols * tile)
     parts = call(add_pair, (part,) * n_chips, 2, nbytes=2**20)(keep, received)
-    others = [swap(parts[m], "row", 2 * m) for m in range(1, n_chips)]
+    others = [swap(parts[m], "row", 2 * m) for m in reversed(range(1, n_chips))]
     coarse = call(add_all, shape(owned, coarse_cols, tile, tile), n_chips, nbytes=2**20)(parts[0], *others)
     return (product, coarse)
 

time: 65.2 us -> 65.3 us (level)
  transfers between devices with their start and end apart: 21 -> 21, of which waited for: 13 -> 13; matrix products, arithmetic and copies ran while one was open for 0% -> 0% of each run, Pallas kernels for 8% -> 7%
where the time goes in v6:
time: 65.3 us; the launch traced here: 64.9 us
  waiting for transfers between devices  25.8 us (40%)
  starting transfers between devices  25 us (38%)
  Pallas kernels  9.84 us (15%)
  local copies, waits for them, and re-layouts  2.85 us (4%)
  between operations  1.42 us (2%)
    ppermute x10, waiting for transfers between devices, hop(): return lax.ppermute(x, 'col', pairs) if pairs else None  15.4 us
    ppermute x10, starting transfers between devices, hop(): return lax.ppermute(x, 'col', pairs) if pairs else None  15.4 us
    ppermute x11, waiting for transfers between devices, swap(): return lax.ppermute(x, axis, [(i, i ^ mask) for i in range(n)])  10.4 us
    ppermute x11, starting transfers between devices, swap(): return lax.ppermute(x, axis, [(i, i ^ mask) for i in range(n)])  9.61 us
    pallas_call x3, Pallas kernels, stage(): call(kernel, tuple(out), len(operands), scratch, flops=2 ** 28, nbytes=4...  5.47 us
    unnamed x6, local copies, waits for them, and re-layouts  2.85 us
    pallas_call x1, Pallas kernels, shards(): call(functools.partial(pack, fine_cols, coarse_cols), (shape(low_rows, 2...  2.34 us
  transfers between devices with their start and end apart: 21, of which 13 were waited for; matrix products, arithmetic and copies ran while one was open for 0% of the time, Pallas kernels for 7%

profile of v6, /device:TPU:0, one launch (start us, length us, event | category | flops | bytes accessed | tf_op | source)
XLA Modules:
  0.0 64.9 jit_solution(11293170262617712972)
XLA Ops:
  1.3 2.3 %shard_map.86 = (f32[648,128]{1,0:T(8,128)}, f32[640,128]{1,0:T(8,128)}, f32[264,128]{1,0:T(8,128)}) custom-call(f32[32,1,64,64]{3,2,1,0:T(8,128)} %op.1, f32[8,1,64,64]{3,2,1,0:T(8,128)} %pro.1, s32[1,32]{1,0:T(1,128)} %bitcast.4, s32[1,32]{1,0:T(1,128)} %bitcast.5, s32[1,1]{1,0:T(1,128)S(6)} %copy.9.count, s32[1,8]{1,0:T(1,128)} %bitcast.6, s32[1,8]{1,0:T(1,128)} %bitcast.7), custom_call_target="tpu_custom_call" | custom-call | bytes 4194304 | tf_op jit(solution)/shard_map/pallas_call | solution.py:304
  3.6 3.1 %collective-permute-start.2 = (f32[648,128]{1,0:T(8,128)}, f32[648,128]{1,0:T(8,128)S(1)}, u32[]{:S(2)}, u32[]{:S(2)}) collective-permute-start(f32[648,128]{1,0:T(8,128)} %get-tuple-element.29.refs_8_), channel_id=1, source_target_pairs={{0,1},{1,0},{2,3},{3,2},{4,5},{5,4},{6,7},{7,6},{8,9},{9,8},{10,11... | collective-permute-start | bytes 995336 | tf_op jit(solution)/shard_map/ppermute | solution.py:286
  7.4 4.4 %collective-permute-start.12 = (f32[640,128]{1,0:T(8,128)}, f32[640,128]{1,0:T(8,128)S(1)}, u32[]{:S(2)}, u32[]{:S(2)}) collective-permute-start(f32[640,128]{1,0:T(8,128)} %get-tuple-element.32.refs_9_), channel_id=1, source_target_pairs={{0,1},{1,0},{2,3},{3,2},{4,5},{5,4},{6,7},{7,6},{8,9},{9,8},{10,11... | collective-permute-start | bytes 983048 | tf_op jit(solution)/shard_map/ppermute | solution.py:286
  12.5 3.0 %collective-permute-done.2.refs_10_ = f32[648,128]{1,0:T(8,128)S(1)} collective-permute-done((f32[648,128]{1,0:T(8,128)}, f32[648,128]{1,0:T(8,128)S(1)}, u32[]{:S(2)}, u32[]{:S(2)}) %collective-permute-start.2) | collective-permute-done | bytes 331808 | tf_op jit(solution)/shard_map/ppermute | solution.py:286
  15.6 1.3 %collective-permute-start.3 = (f32[648,128]{1,0:T(8,128)S(1)}, f32[648,128]{1,0:T(8,128)S(1)}, u32[]{:S(2)}, u32[]{:S(2)}) collective-permute-start(f32[648,128]{1,0:T(8,128)S(1)} %collective-permute-done.1.refs_12_), channel_id=1, source_target_pairs={{1,0},{2,3},{5,4},{6,7},{9,8},{10,11},{13,12},{14,15},{17,16},{18,... | collective-permute-start | bytes 995336 | tf_op jit(solution)/shard_map/ppermute | solution.py:286
  17.5 5.0 %collective-permute-done.12.refs_11_ = f32[640,128]{1,0:T(8,128)S(1)} collective-permute-done((f32[640,128]{1,0:T(8,128)}, f32[640,128]{1,0:T(8,128)S(1)}, u32[]{:S(2)}, u32[]{:S(2)}) %collective-permute-start.12) | collective-permute-done | bytes 327712 | tf_op jit(solution)/shard_map/ppermute | solution.py:286
  23.3 1.3 %collective-permute-start.7 = (f32[640,128]{1,0:T(8,128)S(1)}, f32[640,128]{1,0:T(8,128)S(1)}, u32[]{:S(2)}, u32[]{:S(2)}) collective-permute-start(f32[640,128]{1,0:T(8,128)S(1)} %collective-permute-done.6.refs_13_), channel_id=1, source_target_pairs={{1,0},{2,3},{5,4},{6,7},{9,8},{10,11},{13,12},{14,15},{17,16},{18,... | collective-permute-start | bytes 983048 | tf_op jit(solution)/shard_map/ppermute | solution.py:286
  24.6 2.0 %collective-permute-start = (f32[264,128]{1,0:T(8,128)}, f32[264,128]{1,0:T(8,128)S(1)}, u32[]{:S(2)}, u32[]{:S(2)}) collective-permute-start(f32[264,128]{1,0:T(8,128)} %get-tuple-element.33.refs_0_), channel_id=1, source_target_pairs={{0,8},{4,12},{8,0},{12,4},{16,24},{20,28},{24,16},{28,20},{1,9},{5... | collective-permute-start | bytes 405512 | tf_op jit(solution)/shard_map/ppermute | solution.py:275
  26.6 3.3 %collective-permute-done.3.refs_7_ = f32[648,128]{1,0:T(8,128)S(1)} collective-permute-done((f32[648,128]{1,0:T(8,128)S(1)}, f32[648,128]{1,0:T(8,128)S(1)}, u32[]{:S(2)}, u32[]{:S(2)}) %collective-permute-start.3) | collective-permute-done | bytes 331808 | tf_op jit(solution)/shard_map/ppermute | solution.py:286
  29.9 1.8 %collective-permute-start.4 = (f32[264,128]{1,0:T(8,128)}, f32[264,128]{1,0:T(8,128)S(1)}, u32[]{:S(2)}, u32[]{:S(2)}) collective-permute-start(f32[264,128]{1,0:T(8,128)} %get-tuple-element.33.refs_0_), channel_id=1, source_target_pairs={{0,16},{4,20},{8,24},{12,28},{16,0},{20,4},{24,8},{28,12},{1,17},{... | collective-permute-start | bytes 405512 | tf_op jit(solution)/shard_map/ppermute | solution.py:275
  31.7 1.4 %collective-permute-start.5 = (f32[264,128]{1,0:T(8,128)}, f32[264,128]{1,0:T(8,128)S(1)}, u32[]{:S(2)}, u32[]{:S(2)}) collective-permute-start(f32[264,128]{1,0:T(8,128)} %get-tuple-element.33.refs_0_), channel_id=1, source_target_pairs={{0,24},{4,28},{8,16},{12,20},{16,8},{20,12},{24,0},{28,4},{1,25},{... | collective-permute-start | bytes 405512 | tf_op jit(solution)/shard_map/ppermute | solution.py:275
  33.1 1.3 %collective-permute-start.15 = (f32[648,128]{1,0:T(8,128)S(1)}, f32[648,128]{1,0:T(8,128)S(1)}, u32[]{:S(2)}, u32[]{:S(2)}) collective-permute-start(f32[648,128]{1,0:T(8,128)S(1)} %collective-permute-done.13.refs_5_), channel_id=1, source_target_pairs={{1,0},{2,3},{5,4},{6,7},{9,8},{10,11},{13,12},{14,15},{17,16},{18,... | collective-permute-start | bytes 995336 | tf_op jit(solution)/shard_map/ppermute | solution.py:286
  34.4 1.3 %collective-permute-start.16 = (f32[640,128]{1,0:T(8,128)S(1)}, f32[640,128]{1,0:T(8,128)S(1)}, u32[]{:S(2)}, u32[]{:S(2)}) collective-permute-start(f32[640,128]{1,0:T(8,128)S(1)} %collective-permute-done.14.refs_6_), channel_id=1, source_target_pairs={{1,0},{2,3},{5,4},{6,7},{9,8},{10,11},{13,12},{14,15},{17,16},{18,... | collective-permute-start | bytes 983048 | tf_op jit(solution)/shard_map/ppermute | solution.py:286
  36.0 1.8 %collective-permute-done.5.refs_6_ = f32[264,128]{1,0:T(8,128)S(1)} collective-permute-done((f32[264,128]{1,0:T(8,128)}, f32[264,128]{1,0:T(8,128)S(1)}, u32[]{:S(2)}, u32[]{:S(2)}) %collective-permute-start.5) | collective-permute-done | bytes 135200 | tf_op jit(solution)/shard_map/ppermute | solution.py:275
  40.5 1.0 %copy-done = f32[648,128]{1,0:T(8,128)S(1)} copy-done((f32[648,128]{1,0:T(8,128)S(1)}, f32[648,128]{1,0:T(8,128)}, u32[]{:S(2)}) %copy-start) | copy-done | bytes 331800
  43.4 2.1 %shard_map.87 = (f32[32,64,128]{2,1,0:T(8,128)S(1)}, bf16[8,256,128]{2,1,0:T(8,128)(2,1)S(1)}, f32[8,128]{1,0:T(8,128)S(1)}, bf16[65,64,128]{2,1,0:T(8,128)(2,1)S(1)}, f32[8,128]{1,0:T(8,128)S(1)}) custom-call(f32[264,128]{1,0:T(8,128)S(1)} %copy-done.2, f32[264,128]{1,0:T(8,128)S(1)} %collective-permute-done.8.refs_1_, ...), custom_call_target="tpu_custom_call" | custom-call | flops 268435456 | bytes 4194304 | tf_op jit(solution)/shard_map/pallas_call | solution.py:380
  45.5 1.3 %shard_map.88 = (f32[32,64,128]{2,1,0:T(8,128)S(1)}, bf16[8,256,128]{2,1,0:T(8,128)(2,1)S(1)}, f32[8,128]{1,0:T(8,128)S(1)}) custom-call(f32[32,64,128]{2,1,0:T(8,128)S(1)} %get-tuple-element.37.refs_0_, bf16[65,64,128]{2,1,0:T(8,128)(2,1)S(1)} %get-tuple-element.38.refs_1_, bf16[8,256,128]{2,1,0:T(8,128)(2,1)S(1)} %get-tuple-element.39.refs_2_, ...), custom_call_target="tpu_custom_call" | custom-call | flops 268435456 | bytes 4194304 | tf_op jit(solution)/shard_map/pallas_call | solution.py:380
  46.8 3.8 %collective-permute-done.16.refs_6_ = f32[640,128]{1,0:T(8,128)S(1)} collective-permute-done((f32[640,128]{1,0:T(8,128)S(1)}, f32[640,128]{1,0:T(8,128)S(1)}, u32[]{:S(2)}, u32[]{:S(2)}) %collective-permute-start.16) | collective-permute-done | bytes 327712 | tf_op jit(solution)/shard_map/ppermute | solution.py:286
  50.6 2.1 %shard_map.89 = (f32[8,64,256]{2,1,0:T(8,128)S(1)}, f32[8,64,256]{2,1,0:T(8,128)S(1)}, f32[8,64,256]{2,1,0:T(8,128)S(1)}) custom-call(f32[32,64,128]{2,1,0:T(8,128)S(1)} %get-tuple-element.44.refs_0_, bf16[65,64,128]{2,1,0:T(8,128)(2,1)S(1)} %get-tuple-element.38.refs_1_, bf16[8,256,128]{2,1,0:T(8,128)(2,1)S(1)} %get-tuple-element.45.refs_2_, ...), custom_call_target="tpu_custom_call" | custom-call | flops 268435456 | bytes 4194304 | tf_op jit(solution)/shard_map/pallas_call | solution.py:380
  52.8 1.9 %collective-permute-done.17.received = f32[8,64,256]{2,1,0:T(8,128)S(1)} collective-permute-done((f32[8,64,256]{2,1,0:T(8,128)S(1)}, f32[8,64,256]{2,1,0:T(8,128)S(1)}, u32[]{:S(2)}, u32[]{:S(2)}) %collective-permute-start.17) | collective-permute-done | bytes 524320 | tf_op jit(solution)/shard_map/ppermute | solution.py:275
  54.7 2.1 %collective-permute-start.18 = (f32[2,64,256]{2,1,0:T(8,128)S(1)}, f32[2,64,256]{2,1,0:T(8,128)S(1)}, u32[]{:S(2)}, u32[]{:S(2)}) collective-permute-start(f32[2,64,256]{2,1,0:T(8,128)S(1)} %get-tuple-element.51), channel_id=1, source_target_pairs={{0,24},{4,28},{8,16},{12,20},{16,8},{20,12},{24,0},{28,4},{1,25},{... | collective-permute-start | bytes 393224 | tf_op jit(solution)/shard_map/ppermute | solution.py:275
  58.3 1.2 %shard_map.90 = f32[8,4,64,64]{3,2,1,0:T(8,128)} custom-call(f32[8,64,256]{2,1,0:T(8,128)S(1)} %get-tuple-element.47.strips), custom_call_target="tpu_custom_call" | custom-call | flops 16777216 | bytes 1048576 | tf_op jit(solution)/shard_map/pallas_call | solution.py:390
  59.5 2.5 %collective-permute-done.18.refs_1_ = f32[2,64,256]{2,1,0:T(8,128)S(1)} collective-permute-done((f32[2,64,256]{2,1,0:T(8,128)S(1)}, f32[2,64,256]{2,1,0:T(8,128)S(1)}, u32[]{:S(2)}, u32[]{:S(2)}) %collective-permute-start.18) | collective-permute-done | bytes 131104 | tf_op jit(solution)/shard_map/ppermute | solution.py:275
  62.0 2.1 %collective-permute-done.19.refs_2_ = f32[2,64,256]{2,1,0:T(8,128)S(1)} collective-permute-done((f32[2,64,256]{2,1,0:T(8,128)S(1)}, f32[2,64,256]{2,1,0:T(8,128)S(1)}, u32[]{:S(2)}, u32[]{:S(2)}) %collective-permute-start.19) | collective-permute-done | bytes 131104 | tf_op jit(solution)/shard_map/ppermute | solution.py:275
  (31 shorter events, 10.0 us)
Async XLA Ops:
  3.6 11.9 %collective-permute-start.2 = (f32[648,128]{1,0:T(8,128)}, f32[648,128]{1,0:T(8,128)S(1)}, u32[]{:S(2)}, u32[]{:S(2)}) collective-permute-start(f32[648,128]{1,0:T(8,128)} %get-tuple-element.29.refs_8_), channel_id=1, source_target_pairs={{0,1},{1,0},{2,3},{3,2},{4,5},{5,4},{6,7},{7,6},{8,9},{9,8},{10,11... | collective-permute-start | bytes 995336 | tf_op jit(solution)/shard_map/ppermute | solution.py:286
  6.7 8.8 %collective-permute-start.1 = (f32[648,128]{1,0:T(8,128)}, f32[648,128]{1,0:T(8,128)S(1)}, u32[]{:S(2)}, u32[]{:S(2)}) collective-permute-start(f32[648,128]{1,0:T(8,128)} %get-tuple-element.29.refs_8_), channel_id=1, source_target_pairs={{1,2},{2,1},{5,6},{6,5},{9,10},{10,9},{13,14},{14,13},{17,18},{18,... | collective-permute-start | bytes 995336 | tf_op jit(solution)/shard_map/ppermute | solution.py:286
  7.4 15.2 %collective-permute-start.12 = (f32[640,128]{1,0:T(8,128)}, f32[640,128]{1,0:T(8,128)S(1)}, u32[]{:S(2)}, u32[]{:S(2)}) collective-permute-start(f32[640,128]{1,0:T(8,128)} %get-tuple-element.32.refs_9_), channel_id=1, source_target_pairs={{0,1},{1,0},{2,3},{3,2},{4,5},{5,4},{6,7},{7,6},{8,9},{9,8},{10,11... | collective-permute-start | bytes 983048 | tf_op jit(solution)/shard_map/ppermute | solution.py:286
  11.8 11.4 %collective-permute-start.6 = (f32[640,128]{1,0:T(8,128)}, f32[640,128]{1,0:T(8,128)S(1)}, u32[]{:S(2)}, u32[]{:S(2)}) collective-permute-start(f32[640,128]{1,0:T(8,128)} %get-tuple-element.32.refs_9_), channel_id=1, source_target_pairs={{1,2},{2,1},{5,6},{6,5},{9,10},{10,9},{13,14},{14,13},{17,18},{18,... | collective-permute-start | bytes 983048 | tf_op jit(solution)/shard_map/ppermute | solution.py:286
  15.6 14.3 %collective-permute-start.3 = (f32[648,128]{1,0:T(8,128)S(1)}, f32[648,128]{1,0:T(8,128)S(1)}, u32[]{:S(2)}, u32[]{:S(2)}) collective-permute-start(f32[648,128]{1,0:T(8,128)S(1)} %collective-permute-done.1.refs_12_), channel_id=1, source_target_pairs={{1,0},{2,3},{5,4},{6,7},{9,8},{10,11},{13,12},{14,15},{17,16},{18,... | collective-permute-start | bytes 995336 | tf_op jit(solution)/shard_map/ppermute | solution.py:286
  16.8 16.3 %collective-permute-start.13 = (f32[648,128]{1,0:T(8,128)S(1)}, f32[648,128]{1,0:T(8,128)S(1)}, u32[]{:S(2)}, u32[]{:S(2)}) collective-permute-start(f32[648,128]{1,0:T(8,128)S(1)} %collective-permute-done.2.refs_10_), channel_id=1, source_target_pairs={{1,2},{2,1},{5,6},{6,5},{9,10},{10,9},{13,14},{14,13},{17,18},{18,... | collective-permute-start | bytes 995336 | tf_op jit(solution)/shard_map/ppermute | solution.py:286
  22.6 11.9 %collective-permute-start.14 = (f32[640,128]{1,0:T(8,128)S(1)}, f32[640,128]{1,0:T(8,128)S(1)}, u32[]{:S(2)}, u32[]{:S(2)}) collective-permute-start(f32[640,128]{1,0:T(8,128)S(1)} %collective-permute-done.12.refs_11_), channel_id=1, source_target_pairs={{1,2},{2,1},{5,6},{6,5},{9,10},{10,9},{13,14},{14,13},{17,18},{18,... | collective-permute-start | bytes 983048 | tf_op jit(solution)/shard_map/ppermute | solution.py:286
  23.3 12.7 %collective-permute-start.7 = (f32[640,128]{1,0:T(8,128)S(1)}, f32[640,128]{1,0:T(8,128)S(1)}, u32[]{:S(2)}, u32[]{:S(2)}) collective-permute-start(f32[640,128]{1,0:T(8,128)S(1)} %collective-permute-done.6.refs_13_), channel_id=1, source_target_pairs={{1,0},{2,3},{5,4},{6,7},{9,8},{10,11},{13,12},{14,15},{17,16},{18,... | collective-permute-start | bytes 983048 | tf_op jit(solution)/shard_map/ppermute | solution.py:286
  24.6 7.1 %collective-permute-start = (f32[264,128]{1,0:T(8,128)}, f32[264,128]{1,0:T(8,128)S(1)}, u32[]{:S(2)}, u32[]{:S(2)}) collective-permute-start(f32[264,128]{1,0:T(8,128)} %get-tuple-element.33.refs_0_), channel_id=1, source_target_pairs={{0,8},{4,12},{8,0},{12,4},{16,24},{20,28},{24,16},{28,20},{1,9},{5... | collective-permute-start | bytes 405512 | tf_op jit(solution)/shard_map/ppermute | solution.py:275
  29.9 6.2 %collective-permute-start.4 = (f32[264,128]{1,0:T(8,128)}, f32[264,128]{1,0:T(8,128)S(1)}, u32[]{:S(2)}, u32[]{:S(2)}) collective-permute-start(f32[264,128]{1,0:T(8,128)} %get-tuple-element.33.refs_0_), channel_id=1, source_target_pairs={{0,16},{4,20},{8,24},{12,28},{16,0},{20,4},{24,8},{28,12},{1,17},{... | collective-permute-start | bytes 405512 | tf_op jit(solution)/shard_map/ppermute | solution.py:275
  31.7 6.1 %collective-permute-start.5 = (f32[264,128]{1,0:T(8,128)}, f32[264,128]{1,0:T(8,128)S(1)}, u32[]{:S(2)}, u32[]{:S(2)}) collective-permute-start(f32[264,128]{1,0:T(8,128)} %get-tuple-element.33.refs_0_), channel_id=1, source_target_pairs={{0,24},{4,28},{8,16},{12,20},{16,8},{20,12},{24,0},{28,4},{1,25},{... | collective-permute-start | bytes 405512 | tf_op jit(solution)/shard_map/ppermute | solution.py:275
  33.1 17.4 %collective-permute-start.15 = (f32[648,128]{1,0:T(8,128)S(1)}, f32[648,128]{1,0:T(8,128)S(1)}, u32[]{:S(2)}, u32[]{:S(2)}) collective-permute-start(f32[648,128]{1,0:T(8,128)S(1)} %collective-permute-done.13.refs_5_), channel_id=1, source_target_pairs={{1,0},{2,3},{5,4},{6,7},{9,8},{10,11},{13,12},{14,15},{17,16},{18,... | collective-permute-start | bytes 995336 | tf_op jit(solution)/shard_map/ppermute | solution.py:286
  34.4 16.1 %collective-permute-start.16 = (f32[640,128]{1,0:T(8,128)S(1)}, f32[640,128]{1,0:T(8,128)S(1)}, u32[]{:S(2)}, u32[]{:S(2)}) collective-permute-start(f32[640,128]{1,0:T(8,128)S(1)} %collective-permute-done.14.refs_6_), channel_id=1, source_target_pairs={{1,0},{2,3},{5,4},{6,7},{9,8},{10,11},{13,12},{14,15},{17,16},{18,... | collective-permute-start | bytes 983048 | tf_op jit(solution)/shard_map/ppermute | solution.py:286
  37.8 1.4 %collective-permute-start.10 = (f32[264,128]{1,0:T(8,128)S(1)}, f32[264,128]{1,0:T(8,128)S(1)}, u32[]{:S(2)}, u32[]{:S(2)}) collective-permute-start(f32[264,128]{1,0:T(8,128)S(1)} %collective-permute-done.4.refs_4_), channel_id=1, source_target_pairs={{0,4},{4,0},{8,12},{12,8},{16,20},{20,16},{24,28},{28,24},{1,5},{5... | collective-permute-start | bytes 405512 | tf_op jit(solution)/shard_map/ppermute | solution.py:275
  37.8 1.6 %collective-permute-start.11 = (f32[264,128]{1,0:T(8,128)S(1)}, f32[264,128]{1,0:T(8,128)S(1)}, u32[]{:S(2)}, u32[]{:S(2)}) collective-permute-start(f32[264,128]{1,0:T(8,128)S(1)} %collective-permute-done.5.refs_6_), channel_id=1, source_target_pairs={{0,4},{4,0},{8,12},{12,8},{16,20},{20,16},{24,28},{28,24},{1,5},{5... | collective-permute-start | bytes 405512 | tf_op jit(solution)/shard_map/ppermute | solution.py:275
  38.3 1.6 %collective-permute-start.8 = (f32[264,128]{1,0:T(8,128)}, f32[264,128]{1,0:T(8,128)S(1)}, u32[]{:S(2)}, u32[]{:S(2)}) collective-permute-start(f32[264,128]{1,0:T(8,128)} %get-tuple-element.33.refs_0_), channel_id=1, source_target_pairs={{0,4},{4,0},{8,12},{12,8},{16,20},{20,16},{24,28},{28,24},{1,5},{5... | collective-permute-start | bytes 405512 | tf_op jit(solution)/shard_map/ppermute | solution.py:275
  39.2 1.4 %collective-permute-start.9 = (f32[264,128]{1,0:T(8,128)S(1)}, f32[264,128]{1,0:T(8,128)S(1)}, u32[]{:S(2)}, u32[]{:S(2)}) collective-permute-start(f32[264,128]{1,0:T(8,128)S(1)} %collective-permute-done.refs_2_), channel_id=1, source_target_pairs={{0,4},{4,0},{8,12},{12,8},{16,20},{20,16},{24,28},{28,24},{1,5},{5... | collective-permute-start | bytes 405512 | tf_op jit(solution)/shard_map/ppermute | solution.py:275
  40.5 1.0 %copy-start = (f32[648,128]{1,0:T(8,128)S(1)}, f32[648,128]{1,0:T(8,128)}, u32[]{:S(2)}) copy-start(f32[648,128]{1,0:T(8,128)} %get-tuple-element.29.refs_8_) | copy-start | bytes 995332
  41.5 1.0 %copy-start.1 = (f32[640,128]{1,0:T(8,128)S(1)}, f32[640,128]{1,0:T(8,128)}, u32[]{:S(2)}) copy-start(f32[640,128]{1,0:T(8,128)} %get-tuple-element.32.refs_9_) | copy-start | bytes 983044
  42.5 0.9 %copy-start.2 = (f32[264,128]{1,0:T(8,128)S(1)}, f32[264,128]{1,0:T(8,128)}, u32[]{:S(2)}) copy-start(f32[264,128]{1,0:T(8,128)} %get-tuple-element.33.refs_0_) | copy-start | bytes 405508
  52.7 2.0 %collective-permute-start.17 = (f32[8,64,256]{2,1,0:T(8,128)S(1)}, f32[8,64,256]{2,1,0:T(8,128)S(1)}, u32[]{:S(2)}, u32[]{:S(2)}) collective-permute-start(f32[8,64,256]{2,1,0:T(8,128)S(1)} %get-tuple-element.49), channel_id=1, source_target_pairs={{0,4},{4,0},{8,12},{12,8},{16,20},{20,16},{24,28},{28,24},{1,5},{5... | collective-permute-start | bytes 1572872 | tf_op jit(solution)/shard_map/ppermute | solution.py:275
  54.7 7.2 %collective-permute-start.18 = (f32[2,64,256]{2,1,0:T(8,128)S(1)}, f32[2,64,256]{2,1,0:T(8,128)S(1)}, u32[]{:S(2)}, u32[]{:S(2)}) collective-permute-start(f32[2,64,256]{2,1,0:T(8,128)S(1)} %get-tuple-element.51), channel_id=1, source_target_pairs={{0,24},{4,28},{8,16},{12,20},{16,8},{20,12},{24,0},{28,4},{1,25},{... | collective-permute-start | bytes 393224 | tf_op jit(solution)/shard_map/ppermute | solution.py:275
  56.8 7.2 %collective-permute-start.19 = (f32[2,64,256]{2,1,0:T(8,128)S(1)}, f32[2,64,256]{2,1,0:T(8,128)S(1)}, u32[]{:S(2)}, u32[]{:S(2)}) collective-permute-start(f32[2,64,256]{2,1,0:T(8,128)S(1)} %get-tuple-element.52), channel_id=1, source_target_pairs={{0,16},{4,20},{8,24},{12,28},{16,0},{20,4},{24,8},{28,12},{1,17},{... | collective-permute-start | bytes 393224 | tf_op jit(solution)/shard_map/ppermute | solution.py:275
  57.4 6.7 %collective-permute-start.20 = (f32[2,64,256]{2,1,0:T(8,128)S(1)}, f32[2,64,256]{2,1,0:T(8,128)S(1)}, u32[]{:S(2)}, u32[]{:S(2)}) collective-permute-start(f32[2,64,256]{2,1,0:T(8,128)S(1)} %get-tuple-element.53), channel_id=1, source_target_pairs={{0,8},{4,12},{8,0},{12,4},{16,24},{20,28},{24,16},{28,20},{1,9},{5... | collective-permute-start | bytes 393224 | tf_op jit(solution)/shard_map/ppermute | solution.py:275

commit v7 on v5

--- a/solution.py
+++ b/solution.py
@@ -367,8 +367,7 @@
     early = [(low, high)] + split_chain[:1] + other_chain[:1]
     middle = split_chain[1:-1] + other_chain[1:]
     late = split_chain[-1:]
-    acc, weights, goals, panel, ids = stage(True, False, 0, panel_pays, early)
-    acc, weights, goals = stage(False, False, len(early), (acc, panel, weights, ids, goals), middle)
+    acc, weights, goals, panel, ids = stage(True, False, 0, panel_pays, early + middle)
     strips, keep, send = stage(False, True, len(early + middle), (acc, panel, weights, ids, goals), late)
 
     received = swap(send, "row", 1)

time: 65.2 us -> 66.5 us (1.020)
  local copies, waits for them, and re-layouts: 2.85 us -> 4.08 us
  Pallas kernels: 10.3 us -> 11 us
  waiting for transfers between devices: 25.3 us -> 24.6 us
    unnamed x6 -> x8, local copies, waits for them, and re-layouts: 2.85 us -> 4.08 us
    pallas_call x3 -> x2, Pallas kernels: 5.89 us -> 6.62 us  [stage(): call(kernel, tuple(out), len(operands), scratch, flops=2 ** 28, nbytes=4...]
    ppermute x10, waiting for transfers between devices: 15.1 us -> 14.3 us  [hop(): return lax.ppermute(x, 'col', pairs) if pairs else None]
where the time goes in v7:
time: 66.5 us; the launch traced here: 66.1 us
  starting transfers between devices  25 us (38%)
  waiting for transfers between devices  24.6 us (37%)
  Pallas kernels  11 us (17%)
  local copies, waits for them, and re-layouts  4.08 us (6%)
  between operations  1.41 us (2%)
    ppermute x10, starting transfers between devices, hop(): return lax.ppermute(x, 'col', pairs) if pairs else None  15.4 us
    ppermute x10, waiting for transfers between devices, hop(): return lax.ppermute(x, 'col', pairs) if pairs else None  14.3 us
    ppermute x11, waiting for transfers between devices, swap(): return lax.ppermute(x, axis, [(i, i ^ mask) for i in range(n)])  10.3 us
    ppermute x11, starting transfers between devices, swap(): return lax.ppermute(x, axis, [(i, i ^ mask) for i in range(n)])  9.61 us
    pallas_call x2, Pallas kernels, stage(): call(kernel, tuple(out), len(operands), scratch, flops=2 ** 28, nbytes=4...  6.62 us
    unnamed x8, local copies, waits for them, and re-layouts  4.08 us
    pallas_call x1, Pallas kernels, shards(): call(functools.partial(pack, fine_cols, coarse_cols), (shape(low_rows, 2...  2.35 us
  transfers between devices with their start and end apart: 21, of which 13 were waited for; matrix products, arithmetic and copies ran while one was open for 0% of the time, Pallas kernels for 8%

profile of v7, /device:TPU:0, one launch (start us, length us, event | category | flops | bytes accessed | tf_op | source)
XLA Modules:
  0.0 66.1 jit_solution(15841203036916543808)
XLA Ops:
  1.3 2.3 %shard_map.86 = (f32[648,128]{1,0:T(8,128)}, f32[640,128]{1,0:T(8,128)}, f32[264,128]{1,0:T(8,128)}) custom-call(f32[32,1,64,64]{3,2,1,0:T(8,128)} %op.1, f32[8,1,64,64]{3,2,1,0:T(8,128)} %pro.1, s32[1,32]{1,0:T(1,128)} %bitcast.4, s32[1,32]{1,0:T(1,128)} %bitcast.5, s32[1,1]{1,0:T(1,128)S(6)} %copy.9.count, s32[1,8]{1,0:T(1,128)} %bitcast.6, s32[1,8]{1,0:T(1,128)} %bitcast.7), custom_call_target="tpu_custom_call" | custom-call | bytes 4194304 | tf_op jit(solution)/shard_map/pallas_call | solution.py:293
  3.6 3.1 %collective-permute-start.2 = (f32[648,128]{1,0:T(8,128)}, f32[648,128]{1,0:T(8,128)S(1)}, u32[]{:S(2)}, u32[]{:S(2)}) collective-permute-start(f32[648,128]{1,0:T(8,128)} %get-tuple-element.26.refs_8_), channel_id=1, source_target_pairs={{0,1},{1,0},{2,3},{3,2},{4,5},{5,4},{6,7},{7,6},{8,9},{9,8},{10,11... | collective-permute-start | bytes 995336 | tf_op jit(solution)/shard_map/ppermute | solution.py:275
  7.4 4.4 %collective-permute-start.12 = (f32[640,128]{1,0:T(8,128)}, f32[640,128]{1,0:T(8,128)S(1)}, u32[]{:S(2)}, u32[]{:S(2)}) collective-permute-start(f32[640,128]{1,0:T(8,128)} %get-tuple-element.29.refs_9_), channel_id=1, source_target_pairs={{0,1},{1,0},{2,3},{3,2},{4,5},{5,4},{6,7},{7,6},{8,9},{9,8},{10,11... | collective-permute-start | bytes 983048 | tf_op jit(solution)/shard_map/ppermute | solution.py:275
  12.5 3.0 %collective-permute-done.2.refs_10_ = f32[648,128]{1,0:T(8,128)S(1)} collective-permute-done((f32[648,128]{1,0:T(8,128)}, f32[648,128]{1,0:T(8,128)S(1)}, u32[]{:S(2)}, u32[]{:S(2)}) %collective-permute-start.2) | collective-permute-done | bytes 331808 | tf_op jit(solution)/shard_map/ppermute | solution.py:275
  15.6 1.3 %collective-permute-start.3 = (f32[648,128]{1,0:T(8,128)S(1)}, f32[648,128]{1,0:T(8,128)S(1)}, u32[]{:S(2)}, u32[]{:S(2)}) collective-permute-start(f32[648,128]{1,0:T(8,128)S(1)} %collective-permute-done.1.refs_12_), channel_id=1, source_target_pairs={{1,0},{2,3},{5,4},{6,7},{9,8},{10,11},{13,12},{14,15},{17,16},{18,... | collective-permute-start | bytes 995336 | tf_op jit(solution)/shard_map/ppermute | solution.py:275
  17.5 5.0 %collective-permute-done.12.refs_11_ = f32[640,128]{1,0:T(8,128)S(1)} collective-permute-done((f32[640,128]{1,0:T(8,128)}, f32[640,128]{1,0:T(8,128)S(1)}, u32[]{:S(2)}, u32[]{:S(2)}) %collective-permute-start.12) | collective-permute-done | bytes 327712 | tf_op jit(solution)/shard_map/ppermute | solution.py:275
  23.3 1.3 %collective-permute-start.7 = (f32[640,128]{1,0:T(8,128)S(1)}, f32[640,128]{1,0:T(8,128)S(1)}, u32[]{:S(2)}, u32[]{:S(2)}) collective-permute-start(f32[640,128]{1,0:T(8,128)S(1)} %collective-permute-done.6.refs_13_), channel_id=1, source_target_pairs={{1,0},{2,3},{5,4},{6,7},{9,8},{10,11},{13,12},{14,15},{17,16},{18,... | collective-permute-start | bytes 983048 | tf_op jit(solution)/shard_map/ppermute | solution.py:275
  24.6 2.0 %collective-permute-start = (f32[264,128]{1,0:T(8,128)}, f32[264,128]{1,0:T(8,128)S(1)}, u32[]{:S(2)}, u32[]{:S(2)}) collective-permute-start(f32[264,128]{1,0:T(8,128)} %get-tuple-element.30.refs_0_), channel_id=1, source_target_pairs={{0,8},{4,12},{8,0},{12,4},{16,24},{20,28},{24,16},{28,20},{1,9},{5... | collective-permute-start | bytes 405512 | tf_op jit(solution)/shard_map/ppermute | solution.py:264
  26.6 3.3 %collective-permute-done.3.refs_16_ = f32[648,128]{1,0:T(8,128)S(1)} collective-permute-done((f32[648,128]{1,0:T(8,128)S(1)}, f32[648,128]{1,0:T(8,128)S(1)}, u32[]{:S(2)}, u32[]{:S(2)}) %collective-permute-start.3) | collective-permute-done | bytes 331808 | tf_op jit(solution)/shard_map/ppermute | solution.py:275
  29.9 1.8 %collective-permute-start.4 = (f32[264,128]{1,0:T(8,128)}, f32[264,128]{1,0:T(8,128)S(1)}, u32[]{:S(2)}, u32[]{:S(2)}) collective-permute-start(f32[264,128]{1,0:T(8,128)} %get-tuple-element.30.refs_0_), channel_id=1, source_target_pairs={{0,16},{4,20},{8,24},{12,28},{16,0},{20,4},{24,8},{28,12},{1,17},{... | collective-permute-start | bytes 405512 | tf_op jit(solution)/shard_map/ppermute | solution.py:264
  31.7 1.4 %collective-permute-start.5 = (f32[264,128]{1,0:T(8,128)}, f32[264,128]{1,0:T(8,128)S(1)}, u32[]{:S(2)}, u32[]{:S(2)}) collective-permute-start(f32[264,128]{1,0:T(8,128)} %get-tuple-element.30.refs_0_), channel_id=1, source_target_pairs={{0,24},{4,28},{8,16},{12,20},{16,8},{20,12},{24,0},{28,4},{1,25},{... | collective-permute-start | bytes 405512 | tf_op jit(solution)/shard_map/ppermute | solution.py:264
  33.1 1.3 %collective-permute-start.15 = (f32[648,128]{1,0:T(8,128)S(1)}, f32[648,128]{1,0:T(8,128)S(1)}, u32[]{:S(2)}, u32[]{:S(2)}) collective-permute-start(f32[648,128]{1,0:T(8,128)S(1)} %collective-permute-done.13.refs_14_), channel_id=1, source_target_pairs={{1,0},{2,3},{5,4},{6,7},{9,8},{10,11},{13,12},{14,15},{17,16},{18,... | collective-permute-start | bytes 995336 | tf_op jit(solution)/shard_map/ppermute | solution.py:275
  34.4 1.3 %collective-permute-start.16 = (f32[640,128]{1,0:T(8,128)S(1)}, f32[640,128]{1,0:T(8,128)S(1)}, u32[]{:S(2)}, u32[]{:S(2)}) collective-permute-start(f32[640,128]{1,0:T(8,128)S(1)} %collective-permute-done.14.refs_15_), channel_id=1, source_target_pairs={{1,0},{2,3},{5,4},{6,7},{9,8},{10,11},{13,12},{14,15},{17,16},{18,... | collective-permute-start | bytes 983048 | tf_op jit(solution)/shard_map/ppermute | solution.py:275
  36.0 1.8 %collective-permute-done.5.refs_6_ = f32[264,128]{1,0:T(8,128)S(1)} collective-permute-done((f32[264,128]{1,0:T(8,128)}, f32[264,128]{1,0:T(8,128)S(1)}, u32[]{:S(2)}, u32[]{:S(2)}) %collective-permute-start.5) | collective-permute-done | bytes 135200 | tf_op jit(solution)/shard_map/ppermute | solution.py:264
  43.4 4.4 %shard_map.87 = (f32[32,64,128]{2,1,0:T(8,128)S(1)}, bf16[8,256,128]{2,1,0:T(8,128)(2,1)S(1)}, f32[8,128]{1,0:T(8,128)S(1)}, bf16[65,64,128]{2,1,0:T(8,128)(2,1)}, f32[8,128]{1,0:T(8,128)S(1)}) custom-call(f32[264,128]{1,0:T(8,128)S(1)} %copy-done.3, f32[264,128]{1,0:T(8,128)S(1)} %collective-permute-done.8.refs_1_, ...), custom_call_target="tpu_custom_call" | custom-call | flops 268435456 | bytes 4194304 | tf_op jit(solution)/shard_map/pallas_call | solution.py:365
  47.8 2.8 %collective-permute-done.16.refs_6_ = f32[640,128]{1,0:T(8,128)S(1)} collective-permute-done((f32[640,128]{1,0:T(8,128)S(1)}, f32[640,128]{1,0:T(8,128)S(1)}, u32[]{:S(2)}, u32[]{:S(2)}) %collective-permute-start.16) | collective-permute-done | bytes 327712 | tf_op jit(solution)/shard_map/ppermute | solution.py:275
  50.6 1.2 %copy-done = bf16[65,64,128]{2,1,0:T(8,128)(2,1)S(1)} copy-done((bf16[65,64,128]{2,1,0:T(8,128)(2,1)S(1)}, bf16[65,64,128]{2,1,0:T(8,128)(2,1)}, u32[]{:S(2)}) %copy-start) | copy-done | bytes 1064984
  51.8 2.2 %shard_map.88 = (f32[8,64,256]{2,1,0:T(8,128)S(1)}, f32[8,64,256]{2,1,0:T(8,128)S(1)}, f32[8,64,256]{2,1,0:T(8,128)S(1)}) custom-call(f32[32,64,128]{2,1,0:T(8,128)S(1)} %get-tuple-element.36.refs_0_, bf16[65,64,128]{2,1,0:T(8,128)(2,1)S(1)} %copy-done, bf16[8,256,128]{2,1,0:T(8,128)(2,1)S(1)} %get-tuple-element.38.refs_2_, ...), custom_call_target="tpu_custom_call" | custom-call | flops 268435456 | bytes 4194304 | tf_op jit(solution)/shard_map/pallas_call | solution.py:365
  54.1 1.9 %collective-permute-done.17.received = f32[8,64,256]{2,1,0:T(8,128)S(1)} collective-permute-done((f32[8,64,256]{2,1,0:T(8,128)S(1)}, f32[8,64,256]{2,1,0:T(8,128)S(1)}, u32[]{:S(2)}, u32[]{:S(2)}) %collective-permute-start.17) | collective-permute-done | bytes 524320 | tf_op jit(solution)/shard_map/ppermute | solution.py:264
  56.1 1.2 %collective-permute-start.18 = (f32[2,64,256]{2,1,0:T(8,128)S(1)}, f32[2,64,256]{2,1,0:T(8,128)S(1)}, u32[]{:S(2)}, u32[]{:S(2)}) collective-permute-start(f32[2,64,256]{2,1,0:T(8,128)S(1)} %get-tuple-element.45), channel_id=1, source_target_pairs={{0,8},{4,12},{8,0},{12,4},{16,24},{20,28},{24,16},{28,20},{1,9},{5... | collective-permute-start | bytes 393224 | tf_op jit(solution)/shard_map/ppermute | solution.py:264
  57.2 1.5 %collective-permute-start.19 = (f32[2,64,256]{2,1,0:T(8,128)S(1)}, f32[2,64,256]{2,1,0:T(8,128)S(1)}, u32[]{:S(2)}, u32[]{:S(2)}) collective-permute-start(f32[2,64,256]{2,1,0:T(8,128)S(1)} %get-tuple-element.46), channel_id=1, source_target_pairs={{0,16},{4,20},{8,24},{12,28},{16,0},{20,4},{24,8},{28,12},{1,17},{... | collective-permute-start | bytes 393224 | tf_op jit(solution)/shard_map/ppermute | solution.py:264
  59.6 1.2 %shard_map.89 = f32[8,4,64,64]{3,2,1,0:T(8,128)} custom-call(f32[8,64,256]{2,1,0:T(8,128)S(1)} %get-tuple-element.41.strips), custom_call_target="tpu_custom_call" | custom-call | flops 16777216 | bytes 1048576 | tf_op jit(solution)/shard_map/pallas_call | solution.py:374
  60.8 1.7 %collective-permute-done.18.refs_1_ = f32[2,64,256]{2,1,0:T(8,128)S(1)} collective-permute-done((f32[2,64,256]{2,1,0:T(8,128)S(1)}, f32[2,64,256]{2,1,0:T(8,128)S(1)}, u32[]{:S(2)}, u32[]{:S(2)}) %collective-permute-start.18) | collective-permute-done | bytes 131104 | tf_op jit(solution)/shard_map/ppermute | solution.py:264
  62.5 2.8 %collective-permute-done.19.refs_2_ = f32[2,64,256]{2,1,0:T(8,128)S(1)} collective-permute-done((f32[2,64,256]{2,1,0:T(8,128)S(1)}, f32[2,64,256]{2,1,0:T(8,128)S(1)}, u32[]{:S(2)}, u32[]{:S(2)}) %collective-permute-start.19) | collective-permute-done | bytes 131104 | tf_op jit(solution)/shard_map/ppermute | solution.py:264
  (32 shorter events, 10.4 us)
Async XLA Ops:
  3.6 11.9 %collective-permute-start.2 = (f32[648,128]{1,0:T(8,128)}, f32[648,128]{1,0:T(8,128)S(1)}, u32[]{:S(2)}, u32[]{:S(2)}) collective-permute-start(f32[648,128]{1,0:T(8,128)} %get-tuple-element.26.refs_8_), channel_id=1, source_target_pairs={{0,1},{1,0},{2,3},{3,2},{4,5},{5,4},{6,7},{7,6},{8,9},{9,8},{10,11... | collective-permute-start | bytes 995336 | tf_op jit(solution)/shard_map/ppermute | solution.py:275
  6.7 8.8 %collective-permute-start.1 = (f32[648,128]{1,0:T(8,128)}, f32[648,128]{1,0:T(8,128)S(1)}, u32[]{:S(2)}, u32[]{:S(2)}) collective-permute-start(f32[648,128]{1,0:T(8,128)} %get-tuple-element.26.refs_8_), channel_id=1, source_target_pairs={{1,2},{2,1},{5,6},{6,5},{9,10},{10,9},{13,14},{14,13},{17,18},{18,... | collective-permute-start | bytes 995336 | tf_op jit(solution)/shard_map/ppermute | solution.py:275
  7.4 15.2 %collective-permute-start.12 = (f32[640,128]{1,0:T(8,128)}, f32[640,128]{1,0:T(8,128)S(1)}, u32[]{:S(2)}, u32[]{:S(2)}) collective-permute-start(f32[640,128]{1,0:T(8,128)} %get-tuple-element.29.refs_9_), channel_id=1, source_target_pairs={{0,1},{1,0},{2,3},{3,2},{4,5},{5,4},{6,7},{7,6},{8,9},{9,8},{10,11... | collective-permute-start | bytes 983048 | tf_op jit(solution)/shard_map/ppermute | solution.py:275
  11.8 11.4 %collective-permute-start.6 = (f32[640,128]{1,0:T(8,128)}, f32[640,128]{1,0:T(8,128)S(1)}, u32[]{:S(2)}, u32[]{:S(2)}) collective-permute-start(f32[640,128]{1,0:T(8,128)} %get-tuple-element.29.refs_9_), channel_id=1, source_target_pairs={{1,2},{2,1},{5,6},{6,5},{9,10},{10,9},{13,14},{14,13},{17,18},{18,... | collective-permute-start | bytes 983048 | tf_op jit(solution)/shard_map/ppermute | solution.py:275
  15.6 14.3 %collective-permute-start.3 = (f32[648,128]{1,0:T(8,128)S(1)}, f32[648,128]{1,0:T(8,128)S(1)}, u32[]{:S(2)}, u32[]{:S(2)}) collective-permute-start(f32[648,128]{1,0:T(8,128)S(1)} %collective-permute-done.1.refs_12_), channel_id=1, source_target_pairs={{1,0},{2,3},{5,4},{6,7},{9,8},{10,11},{13,12},{14,15},{17,16},{18,... | collective-permute-start | bytes 995336 | tf_op jit(solution)/shard_map/ppermute | solution.py:275
  16.8 16.3 %collective-permute-start.13 = (f32[648,128]{1,0:T(8,128)S(1)}, f32[648,128]{1,0:T(8,128)S(1)}, u32[]{:S(2)}, u32[]{:S(2)}) collective-permute-start(f32[648,128]{1,0:T(8,128)S(1)} %collective-permute-done.2.refs_10_), channel_id=1, source_target_pairs={{1,2},{2,1},{5,6},{6,5},{9,10},{10,9},{13,14},{14,13},{17,18},{18,... | collective-permute-start | bytes 995336 | tf_op jit(solution)/shard_map/ppermute | solution.py:275
  22.6 11.9 %collective-permute-start.14 = (f32[640,128]{1,0:T(8,128)S(1)}, f32[640,128]{1,0:T(8,128)S(1)}, u32[]{:S(2)}, u32[]{:S(2)}) collective-permute-start(f32[640,128]{1,0:T(8,128)S(1)} %collective-permute-done.12.refs_11_), channel_id=1, source_target_pairs={{1,2},{2,1},{5,6},{6,5},{9,10},{10,9},{13,14},{14,13},{17,18},{18,... | collective-permute-start | bytes 983048 | tf_op jit(solution)/shard_map/ppermute | solution.py:275
  23.3 12.7 %collective-permute-start.7 = (f32[640,128]{1,0:T(8,128)S(1)}, f32[640,128]{1,0:T(8,128)S(1)}, u32[]{:S(2)}, u32[]{:S(2)}) collective-permute-start(f32[640,128]{1,0:T(8,128)S(1)} %collective-permute-done.6.refs_13_), channel_id=1, source_target_pairs={{1,0},{2,3},{5,4},{6,7},{9,8},{10,11},{13,12},{14,15},{17,16},{18,... | collective-permute-start | bytes 983048 | tf_op jit(solution)/shard_map/ppermute | solution.py:275
  24.6 7.1 %collective-permute-start = (f32[264,128]{1,0:T(8,128)}, f32[264,128]{1,0:T(8,128)S(1)}, u32[]{:S(2)}, u32[]{:S(2)}) collective-permute-start(f32[264,128]{1,0:T(8,128)} %get-tuple-element.30.refs_0_), channel_id=1, source_target_pairs={{0,8},{4,12},{8,0},{12,4},{16,24},{20,28},{24,16},{28,20},{1,9},{5... | collective-permute-start | bytes 405512 | tf_op jit(solution)/shard_map/ppermute | solution.py:264
  29.9 6.2 %collective-permute-start.4 = (f32[264,128]{1,0:T(8,128)}, f32[264,128]{1,0:T(8,128)S(1)}, u32[]{:S(2)}, u32[]{:S(2)}) collective-permute-start(f32[264,128]{1,0:T(8,128)} %get-tuple-element.30.refs_0_), channel_id=1, source_target_pairs={{0,16},{4,20},{8,24},{12,28},{16,0},{20,4},{24,8},{28,12},{1,17},{... | collective-permute-start | bytes 405512 | tf_op jit(solution)/shard_map/ppermute | solution.py:264
  31.7 6.1 %collective-permute-start.5 = (f32[264,128]{1,0:T(8,128)}, f32[264,128]{1,0:T(8,128)S(1)}, u32[]{:S(2)}, u32[]{:S(2)}) collective-permute-start(f32[264,128]{1,0:T(8,128)} %get-tuple-element.30.refs_0_), channel_id=1, source_target_pairs={{0,24},{4,28},{8,16},{12,20},{16,8},{20,12},{24,0},{28,4},{1,25},{... | collective-permute-start | bytes 405512 | tf_op jit(solution)/shard_map/ppermute | solution.py:264
  33.1 17.4 %collective-permute-start.15 = (f32[648,128]{1,0:T(8,128)S(1)}, f32[648,128]{1,0:T(8,128)S(1)}, u32[]{:S(2)}, u32[]{:S(2)}) collective-permute-start(f32[648,128]{1,0:T(8,128)S(1)} %collective-permute-done.13.refs_14_), channel_id=1, source_target_pairs={{1,0},{2,3},{5,4},{6,7},{9,8},{10,11},{13,12},{14,15},{17,16},{18,... | collective-permute-start | bytes 995336 | tf_op jit(solution)/shard_map/ppermute | solution.py:275
  34.4 16.1 %collective-permute-start.16 = (f32[640,128]{1,0:T(8,128)S(1)}, f32[640,128]{1,0:T(8,128)S(1)}, u32[]{:S(2)}, u32[]{:S(2)}) collective-permute-start(f32[640,128]{1,0:T(8,128)S(1)} %collective-permute-done.14.refs_15_), channel_id=1, source_target_pairs={{1,0},{2,3},{5,4},{6,7},{9,8},{10,11},{13,12},{14,15},{17,16},{18,... | collective-permute-start | bytes 983048 | tf_op jit(solution)/shard_map/ppermute | solution.py:275
  37.8 1.4 %collective-permute-start.10 = (f32[264,128]{1,0:T(8,128)S(1)}, f32[264,128]{1,0:T(8,128)S(1)}, u32[]{:S(2)}, u32[]{:S(2)}) collective-permute-start(f32[264,128]{1,0:T(8,128)S(1)} %collective-permute-done.4.refs_4_), channel_id=1, source_target_pairs={{0,4},{4,0},{8,12},{12,8},{16,20},{20,16},{24,28},{28,24},{1,5},{5... | collective-permute-start | bytes 405512 | tf_op jit(solution)/shard_map/ppermute | solution.py:264
  37.8 1.6 %collective-permute-start.11 = (f32[264,128]{1,0:T(8,128)S(1)}, f32[264,128]{1,0:T(8,128)S(1)}, u32[]{:S(2)}, u32[]{:S(2)}) collective-permute-start(f32[264,128]{1,0:T(8,128)S(1)} %collective-permute-done.5.refs_6_), channel_id=1, source_target_pairs={{0,4},{4,0},{8,12},{12,8},{16,20},{20,16},{24,28},{28,24},{1,5},{5... | collective-permute-start | bytes 405512 | tf_op jit(solution)/shard_map/ppermute | solution.py:264
  38.3 1.6 %collective-permute-start.8 = (f32[264,128]{1,0:T(8,128)}, f32[264,128]{1,0:T(8,128)S(1)}, u32[]{:S(2)}, u32[]{:S(2)}) collective-permute-start(f32[264,128]{1,0:T(8,128)} %get-tuple-element.30.refs_0_), channel_id=1, source_target_pairs={{0,4},{4,0},{8,12},{12,8},{16,20},{20,16},{24,28},{28,24},{1,5},{5... | collective-permute-start | bytes 405512 | tf_op jit(solution)/shard_map/ppermute | solution.py:264
  39.2 1.4 %collective-permute-start.9 = (f32[264,128]{1,0:T(8,128)S(1)}, f32[264,128]{1,0:T(8,128)S(1)}, u32[]{:S(2)}, u32[]{:S(2)}) collective-permute-start(f32[264,128]{1,0:T(8,128)S(1)} %collective-permute-done.refs_2_), channel_id=1, source_target_pairs={{0,4},{4,0},{8,12},{12,8},{16,20},{20,16},{24,28},{28,24},{1,5},{5... | collective-permute-start | bytes 405512 | tf_op jit(solution)/shard_map/ppermute | solution.py:264
  40.5 1.0 %copy-start.1 = (f32[648,128]{1,0:T(8,128)S(1)}, f32[648,128]{1,0:T(8,128)}, u32[]{:S(2)}) copy-start(f32[648,128]{1,0:T(8,128)} %get-tuple-element.26.refs_8_) | copy-start | bytes 995332
  41.5 1.0 %copy-start.2 = (f32[640,128]{1,0:T(8,128)S(1)}, f32[640,128]{1,0:T(8,128)}, u32[]{:S(2)}) copy-start(f32[640,128]{1,0:T(8,128)} %get-tuple-element.29.refs_9_) | copy-start | bytes 983044
  50.6 1.2 %copy-start = (bf16[65,64,128]{2,1,0:T(8,128)(2,1)S(1)}, bf16[65,64,128]{2,1,0:T(8,128)(2,1)}, u32[]{:S(2)}) copy-start(bf16[65,64,128]{2,1,0:T(8,128)(2,1)} %get-tuple-element.37.refs_1_) | copy-start | bytes 3194884
  54.0 2.0 %collective-permute-start.17 = (f32[8,64,256]{2,1,0:T(8,128)S(1)}, f32[8,64,256]{2,1,0:T(8,128)S(1)}, u32[]{:S(2)}, u32[]{:S(2)}) collective-permute-start(f32[8,64,256]{2,1,0:T(8,128)S(1)} %get-tuple-element.43), channel_id=1, source_target_pairs={{0,4},{4,0},{8,12},{12,8},{16,20},{20,16},{24,28},{28,24},{1,5},{5... | collective-permute-start | bytes 1572872 | tf_op jit(solution)/shard_map/ppermute | solution.py:264
  56.1 6.4 %collective-permute-start.18 = (f32[2,64,256]{2,1,0:T(8,128)S(1)}, f32[2,64,256]{2,1,0:T(8,128)S(1)}, u32[]{:S(2)}, u32[]{:S(2)}) collective-permute-start(f32[2,64,256]{2,1,0:T(8,128)S(1)} %get-tuple-element.45), channel_id=1, source_target_pairs={{0,8},{4,12},{8,0},{12,4},{16,24},{20,28},{24,16},{28,20},{1,9},{5... | collective-permute-start | bytes 393224 | tf_op jit(solution)/shard_map/ppermute | solution.py:264
  57.2 8.1 %collective-permute-start.19 = (f32[2,64,256]{2,1,0:T(8,128)S(1)}, f32[2,64,256]{2,1,0:T(8,128)S(1)}, u32[]{:S(2)}, u32[]{:S(2)}) collective-permute-start(f32[2,64,256]{2,1,0:T(8,128)S(1)} %get-tuple-element.46), channel_id=1, source_target_pairs={{0,16},{4,20},{8,24},{12,28},{16,0},{20,4},{24,8},{28,12},{1,17},{... | collective-permute-start | bytes 393224 | tf_op jit(solution)/shard_map/ppermute | solution.py:264
  58.7 6.6 %collective-permute-start.20 = (f32[2,64,256]{2,1,0:T(8,128)S(1)}, f32[2,64,256]{2,1,0:T(8,128)S(1)}, u32[]{:S(2)}, u32[]{:S(2)}) collective-permute-start(f32[2,64,256]{2,1,0:T(8,128)S(1)} %get-tuple-element.47), channel_id=1, source_target_pairs={{0,24},{4,28},{8,16},{12,20},{16,8},{20,12},{24,0},{28,4},{1,25},{... | collective-permute-start | bytes 393224 | tf_op jit(solution)/shard_map/ppermute | solution.py:264
  (1 other events, 0.9 us)
